TPU v7x, 32 devices: a whole 2x2x4 slice. The times are simulated.
32 devices in a mesh: dp: 8 (over z, x), fsdp: 4 (over y, core).
Axes of the slice: x: 2, y: 2, z: 4, core: 2. Of those that a mesh axis runs over, the one named last changes fastest.
Arguments:
- inputs: bfloat16 [2, 3072, 1024], P(None, ('dp', 'fsdp')), may hold values from -6 to 6
- cotangent: bfloat16 [2, 3072, 1024], P(None, ('dp', 'fsdp')), may hold values from -6 to 6
- segments: int32 [2, 3072], P(None, ('dp', 'fsdp')), may hold values from 0 to 63, never falling along the last dimension, each value on 1 to 96 neighbouring positions
- pack_length: int32 [2, 32], P(None, ('dp', 'fsdp')), may hold values from 48 to 96, as said below
- norm_gain: bfloat16 [2, 1024], P(None, ('dp', 'fsdp')), may hold values from 0.5 to 1.5
- norm_shift: bfloat16 [2, 1024], P(None, ('dp', 'fsdp')), may hold values from -4 to 4
- qkv_weight: bfloat16 [2, 1024, 3072], P(None, ('dp', 'fsdp')), may hold values from -0.1875 to 0.1875
- qv_bias: bfloat16 [2, 2048], P(None, ('dp', 'fsdp')), may hold values from -6 to 6
- proj_weight: bfloat16 [2, 1024, 1024], P(None, ('dp', 'fsdp')), may hold values from -0.75 to 0.75
- proj_bias: bfloat16 [2, 1024], P(None, ('dp', 'fsdp')), may hold values from -4 to 4
- up_weight: bfloat16 [2, 1024, 4096], P(None, ('dp', 'fsdp')), may hold values from -0.1875 to 0.1875
- up_bias: bfloat16 [2, 4096], P(None, ('dp', 'fsdp')), may hold values from -6 to 6
- down_weight: bfloat16 [2, 4096, 1024], P(None, ('dp', 'fsdp')), may hold values from -0.09375 to 0.09375
- down_bias: bfloat16 [2, 1024], P(None, ('dp', 'fsdp')), may hold values from -4 to 4
Outputs:
- outputs: bfloat16 [2, 3072, 1024], P(None, ('dp', 'fsdp'))
- input_grad: float32 [2, 3072, 1024], P(None, ('dp', 'fsdp'))
- gain_grad: float32 [2, 1024], P(None, ('dp', 'fsdp'))
- shift_grad: float32 [2, 1024], P(None, ('dp', 'fsdp'))
- qkv_grad: float32 [2, 1024, 3072], P(None, ('dp', 'fsdp'))
- qvbias_grad: float32 [2, 2048], P(None, ('dp', 'fsdp'))
- proj_grad: float32 [2, 1024, 1024], P(None, ('dp', 'fsdp'))
- projbias_grad: float32 [2, 1024], P(None, ('dp', 'fsdp'))
- up_grad: float32 [2, 1024, 4096], P(None, ('dp', 'fsdp'))
- upbias_grad: float32 [2, 4096], P(None, ('dp', 'fsdp'))
- down_grad: float32 [2, 4096, 1024], P(None, ('dp', 'fsdp'))
- downbias_grad: float32 [2, 1024], P(None, ('dp', 'fsdp'))
Inputs may be any that keep to these rules, and one draw needn't show every extreme that they name: `segments`: along each micro-batch the numbers never fall; every number is used; a document spans 1 to 96 rows and one spans exactly 96. `pack_length`: some pack is full and some holds exactly 48 live rows.
All inputs are finite; a program needn't handle non-finite values.
Results may differ from a plain program's by a relative error of at most 0.013.
Values may be sent and summed in bfloat16 or wider, within the bound.
A program may use at most 320 MiB of HBM per device.

v0:
```python
import math

import jax
import jax.numpy as jnp
from jax import lax
from jax.sharding import PartitionSpec as P

D = 1024
HEAD_DIM = 64
ROT = 16


EPS = 1e-05


def rotate(vectors, cosine, sine_table):
    half_dims = cosine.shape[-1]
    first_half = vectors[..., :half_dims]
    second = vectors[..., half_dims : 2 * half_dims]
    remainder = vectors[..., 2 * half_dims :]
    cos_rows = cosine[:, None, :]
    sin_rows = sine_table[:, None, :]
    return jnp.concatenate(
        [
            first_half * cos_rows - second * sin_rows,
            second * cos_rows + first_half * sin_rows,
            remainder,
        ],
        axis=-1,
    )


def gelu_parts(up_proj):
    normal_cdf = 0.5 * (1.0 + lax.erf(up_proj * 0.7071067811865476))
    density = jnp.exp(-0.5 * up_proj * up_proj) * 0.3989422804014327
    return (up_proj * normal_cdf, normal_cdf + up_proj * density)


def masked_scores(queries, key_vectors, allowed):
    scores = jnp.einsum(
        "qhd,khd->hqk", queries, key_vectors, preferred_element_type=jnp.float32
    ) * (1.0 / math.sqrt(HEAD_DIM))
    return jnp.where(allowed[None], scores, -1e30)


def forward_layer(params, stream, allowed, cosine, sine_table):
    (
        norm_gain,
        norm_shift,
        qkv_weight,
        qv_bias,
        proj_weight,
        proj_bias,
        up_weight,
        up_bias,
        down_weight,
        down_bias,
    ) = params
    row_count, model_width = stream.shape
    head_shape = (row_count, model_width // HEAD_DIM, HEAD_DIM)
    average = jnp.mean(stream, axis=-1, keepdims=True)
    centred = stream - average
    variance = jnp.mean(centred * centred, axis=-1, keepdims=True)
    inverse = lax.rsqrt(variance + EPS)
    normed = centred * inverse
    hidden = (normed * norm_gain.astype(jnp.float32) + norm_shift.astype(jnp.float32)).astype(
        jnp.bfloat16
    )
    bias_values = qv_bias.astype(jnp.float32)
    entry_bias = jnp.concatenate(
        [
            bias_values[:model_width],
            jnp.zeros((model_width,), jnp.float32),
            bias_values[model_width:],
        ]
    )
    merged = jnp.dot(hidden, qkv_weight, preferred_element_type=jnp.float32) + entry_bias
    queries = rotate(merged[:, :model_width].reshape(head_shape), cosine, sine_table).astype(
        jnp.bfloat16
    )
    key_vectors = rotate(
        merged[:, model_width : 2 * model_width].reshape(head_shape), cosine, sine_table
    ).astype(jnp.bfloat16)
    value_vectors = merged[:, 2 * model_width :].reshape(head_shape).astype(jnp.bfloat16)
    scores = masked_scores(queries, key_vectors, allowed)
    row_max = jnp.max(scores, axis=-1, keepdims=True)
    shifted = jnp.exp(scores - row_max)
    row_total = jnp.sum(shifted, axis=-1, keepdims=True)
    log_total = row_max + jnp.log(row_total)
    soft_weights = (shifted / row_total).astype(jnp.bfloat16)
    context = jnp.einsum(
        "hqk,khd->qhd", soft_weights, value_vectors, preferred_element_type=jnp.float32
    )
    context = context.reshape(row_count, model_width).astype(jnp.bfloat16)
    attention_out = jnp.dot(
        context, proj_weight, preferred_element_type=jnp.float32
    ) + proj_bias.astype(jnp.float32)
    up_proj = jnp.dot(hidden, up_weight, preferred_element_type=jnp.float32) + up_bias.astype(
        jnp.float32
    )
    activation, gelu_slope = gelu_parts(up_proj)
    activation = activation.astype(jnp.bfloat16)
    mlp_out = jnp.dot(
        activation, down_weight, preferred_element_type=jnp.float32
    ) + down_bias.astype(jnp.float32)
    stored = (
        normed,
        inverse,
        hidden,
        queries,
        key_vectors,
        value_vectors,
        log_total,
        context,
        activation,
        gelu_slope,
    )
    return (stream + attention_out + mlp_out, stored)


def backward_layer(params, stored, upstream, allowed, cosine, sine_table):
    (
        norm_gain,
        norm_shift,
        qkv_weight,
        qv_bias,
        proj_weight,
        proj_bias,
        up_weight,
        up_bias,
        down_weight,
        down_bias,
    ) = params
    (
        normed,
        inverse,
        hidden,
        queries,
        key_vectors,
        value_vectors,
        log_total,
        context,
        activation,
        gelu_slope,
    ) = stored
    row_count, model_width = upstream.shape
    head_shape = (row_count, model_width // HEAD_DIM, HEAD_DIM)
    rounded = upstream.astype(jnp.bfloat16)
    bias_sum = jnp.sum(rounded, axis=0, dtype=jnp.float32)
    up_delta = (
        jnp.einsum("re,fe->rf", rounded, down_weight, preferred_element_type=jnp.float32)
        * gelu_slope
    ).astype(jnp.bfloat16)
    upbias_grad = jnp.sum(up_delta, axis=0, dtype=jnp.float32)
    context_delta = jnp.einsum(
        "re,de->rd", rounded, proj_weight, preferred_element_type=jnp.float32
    )
    context_delta = context_delta.astype(jnp.bfloat16).reshape(head_shape)
    scores = masked_scores(queries, key_vectors, allowed)
    soft_weights = jnp.exp(scores - log_total)
    value_delta = jnp.einsum(
        "hqk,qhd->khd",
        soft_weights.astype(jnp.bfloat16),
        context_delta,
        preferred_element_type=jnp.float32,
    )
    prob_delta = jnp.einsum(
        "qhd,khd->hqk", context_delta, value_vectors, preferred_element_type=jnp.float32
    )
    row_delta = jnp.sum(soft_weights * prob_delta, axis=-1, keepdims=True)
    score_delta = (soft_weights * (prob_delta - row_delta)).astype(jnp.bfloat16)
    score_scale = 1.0 / math.sqrt(HEAD_DIM)
    query_delta = rotate(
        jnp.einsum("hqk,khd->qhd", score_delta, key_vectors, preferred_element_type=jnp.float32)
        * score_scale,
        cosine,
        -sine_table,
    )
    key_delta = rotate(
        jnp.einsum("hqk,qhd->khd", score_delta, queries, preferred_element_type=jnp.float32)
        * score_scale,
        cosine,
        -sine_table,
    )
    merged_delta = jnp.concatenate(
        [
            query_delta.reshape(row_count, model_width),
            key_delta.reshape(row_count, model_width),
            value_delta.reshape(row_count, model_width),
        ],
        axis=1,
    ).astype(jnp.bfloat16)
    column_sums = jnp.sum(merged_delta, axis=0, dtype=jnp.float32)
    qvbias_grad = jnp.concatenate([column_sums[:model_width], column_sums[2 * model_width :]])
    hidden_delta = jnp.einsum(
        "rf,df->rd", merged_delta, qkv_weight, preferred_element_type=jnp.float32
    )
    hidden_delta = hidden_delta + jnp.einsum(
        "rf,df->rd", up_delta, up_weight, preferred_element_type=jnp.float32
    )
    gain_grad = jnp.sum(hidden_delta * normed, axis=0)
    shift_grad = jnp.sum(hidden_delta, axis=0)
    scaled = hidden_delta * norm_gain.astype(jnp.float32)
    input_delta = upstream + inverse * (
        scaled
        - jnp.mean(scaled, axis=-1, keepdims=True)
        - normed * jnp.mean(scaled * normed, axis=-1, keepdims=True)
    )
    operands = (hidden, merged_delta, context, rounded, activation, up_delta)
    vectors = (gain_grad, shift_grad, qvbias_grad, bias_sum, upbias_grad, bias_sum)
    return (input_delta, operands, vectors)


def joint_term(hidden_all, merged_all, context_all, rounded_all, updelta_all):
    merged_part = jnp.einsum(
        "rd,rf->df", hidden_all, merged_all, preferred_element_type=jnp.float32
    )
    proj_part = jnp.einsum(
        "rd,rf->df", context_all, rounded_all, preferred_element_type=jnp.float32
    )
    up_part = jnp.einsum("rd,rf->df", hidden_all, updelta_all, preferred_element_type=jnp.float32)
    return jnp.concatenate([merged_part, proj_part, up_part], axis=1)


def row_term(left_rows, right_rows):
    return jnp.einsum("rd,rf->df", left_rows, right_rows, preferred_element_type=jnp.float32)


def shards(
    inputs,
    cotangent,
    segments,
    pack_length,
    norm_gain,
    norm_shift,
    qkv_weight,
    qv_bias,
    proj_weight,
    proj_bias,
    up_weight,
    up_bias,
    down_weight,
    down_bias,
):
    micro_count = inputs.shape[0]
    row_count = inputs.shape[1]
    layers = qkv_weight.shape[0]
    model_width = D
    position = jnp.arange(row_count)
    is_live = position[None, :] < pack_length
    causal = position[:, None] >= position[None, :]
    diagonal = position[:, None] == position[None, :]
    allowed = [
        (segments[batch_index][:, None] == segments[batch_index][None, :])
        & causal
        & (is_live[batch_index][None, :] | diagonal)
        for batch_index in range(micro_count)
    ]
    angle = (
        position.astype(jnp.float32)[:, None]
        * (10000.0 ** (-jnp.arange(0, ROT, 2, dtype=jnp.float32) / ROT))[None, :]
    )
    cosine = jnp.cos(angle)
    sine_table = jnp.sin(angle)
    states = [inputs[batch_index].astype(jnp.float32) for batch_index in range(micro_count)]
    stored = {}
    fetched = {}
    for layer_index in range(layers):
        params = (
            lax.all_gather(norm_gain[layer_index], ("dp", "fsdp"), axis=0, tiled=True),
            lax.all_gather(norm_shift[layer_index], ("dp", "fsdp"), axis=0, tiled=True),
            lax.all_gather(qkv_weight[layer_index], ("dp", "fsdp"), axis=0, tiled=True),
            lax.all_gather(qv_bias[layer_index], ("dp", "fsdp"), axis=0, tiled=True),
            lax.all_gather(proj_weight[layer_index], ("dp", "fsdp"), axis=0, tiled=True),
            lax.all_gather(proj_bias[layer_index], ("dp", "fsdp"), axis=0, tiled=True),
            lax.all_gather(up_weight[layer_index], ("dp", "fsdp"), axis=0, tiled=True),
            lax.all_gather(up_bias[layer_index], ("dp", "fsdp"), axis=0, tiled=True),
            lax.all_gather(down_weight[layer_index], ("dp", "fsdp"), axis=0, tiled=True),
            lax.all_gather(down_bias[layer_index], ("dp", "fsdp"), axis=0, tiled=True),
        )
        fetched[layer_index] = params
        for batch_index in range(micro_count):
            states[batch_index], stored[layer_index, batch_index] = forward_layer(
                params, states[batch_index], allowed[batch_index], cosine, sine_table
            )
    outputs = [states[batch_index].astype(jnp.bfloat16) for batch_index in range(micro_count)]
    upstreams = [
        cotangent[batch_index].astype(jnp.float32)
        * is_live[batch_index][:, None].astype(jnp.float32)
        for batch_index in range(micro_count)
    ]
    layer_shards = [None] * layers
    for layer_index in reversed(range(layers)):
        params = (
            lax.all_gather(norm_gain[layer_index], ("dp", "fsdp"), axis=0, tiled=True),
            lax.all_gather(norm_shift[layer_index], ("dp", "fsdp"), axis=0, tiled=True),
            lax.all_gather(qkv_weight[layer_index], ("dp", "fsdp"), axis=0, tiled=True),
            lax.all_gather(qv_bias[layer_index], ("dp", "fsdp"), axis=0, tiled=True),
            lax.all_gather(proj_weight[layer_index], ("dp", "fsdp"), axis=0, tiled=True),
            lax.all_gather(proj_bias[layer_index], ("dp", "fsdp"), axis=0, tiled=True),
            lax.all_gather(up_weight[layer_index], ("dp", "fsdp"), axis=0, tiled=True),
            lax.all_gather(up_bias[layer_index], ("dp", "fsdp"), axis=0, tiled=True),
            lax.all_gather(down_weight[layer_index], ("dp", "fsdp"), axis=0, tiled=True),
            lax.all_gather(down_bias[layer_index], ("dp", "fsdp"), axis=0, tiled=True),
        )
        kept_operands = []
        vector_total = None
        for batch_index in range(micro_count):
            upstreams[batch_index], operands, vectors = backward_layer(
                params,
                stored[layer_index, batch_index],
                upstreams[batch_index],
                allowed[batch_index],
                cosine,
                sine_table,
            )
            kept_operands.append(operands)
            if vector_total is None:
                vector_total = vectors
            else:
                vector_total = jax.tree.map(jnp.add, vector_total, vectors)
        joined = [
            jnp.concatenate([operands[member] for operands in kept_operands], axis=0)
            for member in range(6)
        ]
        hidden_all, merged_all, context_all, rounded_all, activation_all, updelta_all = joined
        joint_shard = lax.psum_scatter(
            joint_term(hidden_all, merged_all, context_all, rounded_all, updelta_all),
            ("dp", "fsdp"),
            scatter_dimension=0,
            tiled=True,
        )
        qkv_shard = joint_shard[:, : 3 * model_width]
        proj_shard = joint_shard[:, 3 * model_width : 4 * model_width]
        up_shard = joint_shard[:, 4 * model_width :]
        down_shard = lax.psum_scatter(
            row_term(activation_all, rounded_all), ("dp", "fsdp"), scatter_dimension=0, tiled=True
        )
        gain_shard, shift_shard, qvbias_shard, projbias_shard, upbias_shard, downbias_shard = (
            lax.psum_scatter(vector_total[0], ("dp", "fsdp"), scatter_dimension=0, tiled=True),
            lax.psum_scatter(vector_total[1], ("dp", "fsdp"), scatter_dimension=0, tiled=True),
            lax.psum_scatter(vector_total[2], ("dp", "fsdp"), scatter_dimension=0, tiled=True),
            lax.psum_scatter(vector_total[3], ("dp", "fsdp"), scatter_dimension=0, tiled=True),
            lax.psum_scatter(vector_total[4], ("dp", "fsdp"), scatter_dimension=0, tiled=True),
            lax.psum_scatter(vector_total[5], ("dp", "fsdp"), scatter_dimension=0, tiled=True),
        )
        layer_shards[layer_index] = (
            gain_shard,
            shift_shard,
            qkv_shard,
            qvbias_shard,
            proj_shard,
            projbias_shard,
            up_shard,
            upbias_shard,
            down_shard,
            downbias_shard,
        )
    gradients = [
        jnp.stack([shard_set[member] for shard_set in layer_shards]) for member in range(10)
    ]
    return (
        jnp.stack(outputs),
        jnp.stack(upstreams),
        gradients[0],
        gradients[1],
        gradients[2],
        gradients[3],
        gradients[4],
        gradients[5],
        gradients[6],
        gradients[7],
        gradients[8],
        gradients[9],
    )


def solution(mesh):
    placed = (
        P(None, ("dp", "fsdp"), None),
        P(None, ("dp", "fsdp"), None),
        P(None, ("dp", "fsdp")),
        P(None, ("dp", "fsdp")),
        P(None, ("dp", "fsdp")),
        P(None, ("dp", "fsdp")),
        P(None, ("dp", "fsdp"), None),
        P(None, ("dp", "fsdp")),
        P(None, ("dp", "fsdp"), None),
        P(None, ("dp", "fsdp")),
        P(None, ("dp", "fsdp"), None),
        P(None, ("dp", "fsdp")),
        P(None, ("dp", "fsdp"), None),
        P(None, ("dp", "fsdp")),
    )
    return jax.shard_map(
        shards,
        mesh=mesh,
        in_specs=placed,
        out_specs=(
            P(None, ("dp", "fsdp"), None),
            P(None, ("dp", "fsdp"), None),
            P(None, ("dp", "fsdp")),
            P(None, ("dp", "fsdp")),
            P(None, ("dp", "fsdp"), None),
            P(None, ("dp", "fsdp")),
            P(None, ("dp", "fsdp"), None),
            P(None, ("dp", "fsdp")),
            P(None, ("dp", "fsdp"), None),
            P(None, ("dp", "fsdp")),
            P(None, ("dp", "fsdp"), None),
            P(None, ("dp", "fsdp")),
        ),
        check_vma=False,
    )
```

profile of v0, /device:TPU:0, one launch (start us, length us, event | category | flops | bytes accessed | tf_op | source)
XLA Modules:
  0.0 1886.6 jit_solution(505594859275998040)
XLA Ops:
  7.2 1.6 fusion.370
  8.9 1.8 fusion.369
  15.4 43.0 %all-gather.17 = bf16[1,4096]{1,0:T(2,128)(2,1)S(1)} all-gather(bf16[1,128]{1,0:T(2,128)(2,1)S(1)} %get-tuple-element.170), channel_id=19, replica_groups=mesh['dp'=8,'fsdp'=4] {'dp','fsdp'}, dimensions={1}, use_global_device_ids=true | all-gather | bytes 8448 | tf_op jit(solution)/shard_map/all_gather | solution.py:277
  59.1 36.4 %all-gather.7 = bf16[1,4096]{1,0:T(2,128)(2,1)S(1)} all-gather(bf16[1,128]{1,0:T(2,128)(2,1)S(1)} %get-tuple-element.171), channel_id=9, replica_groups=mesh['dp'=8,'fsdp'=4] {'dp','fsdp'}, dimensions={1}, use_global_device_ids=true | all-gather | bytes 8448 | tf_op jit(solution)/shard_map/all_gather | solution.py:277
  98.3 38.5 %all-reduce.21 = (bf16[1024]{0:T(1024)(128)(2,1)S(1)}, bf16[1024]{0:T(1024)(128)(2,1)S(1)}, bf16[1024]{0:T(1024)(128)(2,1)S(1)}, bf16[2048]{0:T(1024)(128)(2,1)S...) all-reduce(bf16[1024]{0:T(1024)(128)(2,1)S(1)} %dynamic-update-slic, ...), channel_id=3, replica_groups=mesh['dp'=8,'fsdp'=4] {'dp','fsdp'}, use_global_device_ids=true, to_apply=%add.1 | all-reduce | flops 12288 | bytes 49152
  142.4 2.5 fusion.255
  147.5 3.9 fusion.87
  153.3 4.0 fusion.84
  162.2 60.5 %all-gather.33.cloned.1.call-done = bf16[1,1024,4096]{2,1,0:T(8,128)(2,1)} async-done(((bf16[1,32,4096]{2,1,0:T(8,128)(2,1)}), bf16[1,1024,4096]{2,1,0:T(8,128)(2,1)}) %all-gather.33.cloned.1.call-update) | async-done | bytes 8388624 | tf_op jit(solution)/shard_map/all_gather | solution.py:276
  222.7 6.2 multiply_convert_fusion.3
  228.9 73.2 %all-gather.35.cloned.1.call-done = bf16[1,4096,1024]{2,1,0:T(8,128)(2,1)} async-done(((bf16[1,128,1024]{2,1,0:T(8,128)(2,1)}), bf16[1,4096,1024]{2,1,0:T(8,128)(2,1)}) %all-gather.35.cloned.1.call-update) | async-done | bytes 8388624 | tf_op jit(solution)/shard_map/all_gather | solution.py:278
  302.1 4.8 fusion.222
  307.0 52.9 %all-gather.31.cloned.1.call-done = bf16[1,1024,1024]{2,1,0:T(8,128)(2,1)} async-done(((bf16[1,32,1024]{2,1,0:T(8,128)(2,1)}), bf16[1,1024,1024]{2,1,0:T(8,128)(2,1)}) %all-gather.31.cloned.1.call-update) | async-done | bytes 2097168 | tf_op jit(solution)/shard_map/all_gather | solution.py:274
  359.9 2.2 fusion.379
  362.5 68.6 %all-gather.37.cloned.1.call-done = bf16[1,1024,3072]{2,1,0:T(8,128)(2,1)} async-done(((bf16[1,32,3072]{2,1,0:T(8,128)(2,1)}), bf16[1,1024,3072]{2,1,0:T(8,128)(2,1)}) %all-gather.37.cloned.1.call-update) | async-done | bytes 6291472 | tf_op jit(solution)/shard_map/all_gather | solution.py:272
  431.1 3.9 fusion.90
  437.7 1.6 subtract_convert_fusion.13
  441.0 7.0 multiply_convert_fusion.1
  448.0 1.5 fusion.225
  452.1 1.2 fusion.93
  455.1 1.9 fusion.365
  457.1 2.0 copy.124
  459.1 1.8 slice.684
  462.9 1.8 copy.114
  465.7 1.3 fusion.382
  477.5 33.1 %all-gather.41.cloned.1.call-done = bf16[1,1024,4096]{2,1,0:T(8,128)(2,1)} async-done(((bf16[1,32,4096]{2,1,0:T(8,128)(2,1)}), bf16[1,1024,4096]{2,1,0:T(8,128)(2,1)}) %all-gather.41.cloned.1.call-update) | async-done | bytes 8388624 | tf_op jit(solution)/shard_map/all_gather | solution.py:276
  510.6 6.5 multiply_convert_fusion
  517.2 3.1 multiply_convert_fusion.2
  520.3 69.4 %all-gather.43.cloned.1.call-done = bf16[1,4096,1024]{2,1,0:T(8,128)(2,1)} async-done(((bf16[1,128,1024]{2,1,0:T(8,128)(2,1)}), bf16[1,4096,1024]{2,1,0:T(8,128)(2,1)}) %all-gather.43.cloned.1.call-update) | async-done | bytes 8388624 | tf_op jit(solution)/shard_map/all_gather | solution.py:278
  589.7 7.5 convert_reduce_fusion
  597.3 5.9 convert_reduce_fusion.1
  603.2 3.0 fusion.32
  606.3 2.7 fusion.231
  609.1 2.1 fusion.34
  611.3 3.5 multiply_reduce_fusion.5
  614.8 1.9 convert_reduce_fusion.13
  617.4 1.5 fusion.249
  618.8 1.8 copy.138
  620.6 2.1 convolution_convert_fusion
  622.7 2.8 multiply_reduce_fusion
  625.5 1.5 fusion.246
  628.1 1.4 multiply_reduce_fusion.2
  636.9 2.1 fusion.40
  639.1 2.1 fusion.42
  641.3 3.0 convert_reduce_fusion.2
  644.3 3.0 convert_reduce_fusion.3
  647.4 2.7 fusion.219
  650.3 4.2 fusion.310
  659.6 9.2 fusion.164
  670.3 8.2 fusion.160
  683.3 7.1 fusion.144
  690.4 8.2 fusion.156
  698.6 21.3 %pad_maximum_fusion.1 = f32[1024,8192]{1,0:T(8,128)} fusion(f32[1024,4096]{1,0:T(8,128)} %fusion.156, f32[1024,1024]{1,0:T(8,128)S(1)} %fusion.276, f32[1024,3072]{1,0:T(8,128)} %fusion.144), kind=kLoop, calls=%fused_computation.1 | loop fusion | flops 16777216 | bytes 67108864 | tf_op jit(solution)/shard_map/concatenate | solution.py:222
  722.5 7.1 fusion.128
  729.6 8.2 fusion.140
  737.8 21.3 %pad_maximum_fusion = f32[1024,8192]{1,0:T(8,128)} fusion(f32[1024,4096]{1,0:T(8,128)} %fusion.140, f32[1024,1024]{1,0:T(8,128)S(1)} %fusion.272, f32[1024,3072]{1,0:T(8,128)} %fusion.128), kind=kLoop, calls=%fused_computation | loop fusion | flops 16777216 | bytes 67108864 | tf_op jit(solution)/shard_map/concatenate | solution.py:222
  760.3 5.0 fusion.237
  766.5 4.9 fusion.234
  774.2 8.0 all-reduce.24.cloned.1.call-done
  792.0 178.5 %reduce-scatter.11.cloned.1.call-done = f32[128,1024]{1,0:T(8,128)} async-done(((f32[4096,1024]{1,0:T(8,128)}), f32[128,1024]{1,0:T(8,128)}) %reduce-scatter.11.cloned.1.call-update) | async-done | bytes 524304 | tf_op jit(solution)/shard_map/reduce_scatter | solution.py:336
  970.4 187.0 %reduce-scatter.9.cloned.1.call-done = f32[128,1024]{1,0:T(8,128)} async-done(((f32[4096,1024]{1,0:T(8,128)}), f32[128,1024]{1,0:T(8,128)}) %reduce-scatter.9.cloned.1.call-update) | async-done | bytes 524304 | tf_op jit(solution)/shard_map/reduce_scatter | solution.py:336
  1157.4 2.3 pad_maximum_fusion.3
  1159.7 355.8 %reduce-scatter.7.cloned.1.call-done = f32[32,8192]{1,0:T(8,128)} async-done(((f32[1024,8192]{1,0:T(8,128)}), f32[32,8192]{1,0:T(8,128)}) %reduce-scatter.7.cloned.1.call-update) | async-done | bytes 1048592 | tf_op jit(solution)/shard_map/reduce_scatter | solution.py:327
  1516.6 358.7 %reduce-scatter.5.cloned.1.call-done = f32[32,8192]{1,0:T(8,128)} async-done(((f32[1024,8192]{1,0:T(8,128)}), f32[32,8192]{1,0:T(8,128)}) %reduce-scatter.5.cloned.1.call-update) | async-done | bytes 1048592 | tf_op jit(solution)/shard_map/reduce_scatter | solution.py:327
  (728 shorter events, 87.4 us)
Async XLA Ops:
  7.2 135.2 %all-gather.39.cloned.1.call-start = ((), (), s32[]{:S(2)}) async-start(), calls=%async_computation.13 | async-start | bytes 2162688 | tf_op jit(solution)/shard_map/all_gather | solution.py:274
  8.9 138.6 %all-gather.29.cloned.1.call-start = ((), (), s32[]{:S(2)}) async-start(), calls=%async_computation.8 | async-start | bytes 6488064 | tf_op jit(solution)/shard_map/all_gather | solution.py:272
  10.7 85.4 %copy-start.219 = (bf16[2,32]{1,0:T(2,128)(2,1)S(1)}, bf16[2,32]{1,0:T(2,128)(2,1)}, u32[]{:S(2)}) copy-start(bf16[2,32]{1,0:T(2,128)(2,1)} %param.19) | copy-start | bytes 388
  10.8 85.4 %copy-start.220 = (bf16[2,32]{1,0:T(2,128)(2,1)S(1)}, bf16[2,32]{1,0:T(2,128)(2,1)}, u32[]{:S(2)}) copy-start(bf16[2,32]{1,0:T(2,128)(2,1)} %param.18) | copy-start | bytes 388
  10.8 85.4 %copy-start.221 = (bf16[2,32]{1,0:T(2,128)(2,1)S(1)}, bf16[2,32]{1,0:T(2,128)(2,1)}, u32[]{:S(2)}) copy-start(bf16[2,32]{1,0:T(2,128)(2,1)} %param.27) | copy-start | bytes 388
  10.8 85.4 %copy-start.222 = (bf16[2,64]{1,0:T(2,128)(2,1)S(1)}, bf16[2,64]{1,0:T(2,128)(2,1)}, u32[]{:S(2)}) copy-start(bf16[2,64]{1,0:T(2,128)(2,1)} %param.21) | copy-start | bytes 772
  10.8 85.4 %copy-start.223 = (bf16[2,32]{1,0:T(2,128)(2,1)S(1)}, bf16[2,32]{1,0:T(2,128)(2,1)}, u32[]{:S(2)}) copy-start(bf16[2,32]{1,0:T(2,128)(2,1)} %param.23) | copy-start | bytes 388
  10.8 211.9 %all-gather.33.cloned.1.call-start = ((), (), s32[]{:S(2)}) async-start(), calls=%async_computation.10 | async-start | bytes 8650752 | tf_op jit(solution)/shard_map/all_gather | solution.py:276
  11.7 125.1 %copy-start.17 = (bf16[2,96,1024]{2,1,0:T(8,128)(2,1)S(1)}, bf16[2,96,1024]{2,1,0:T(8,128)(2,1)}, u32[]{:S(2)}) copy-start(bf16[2,96,1024]{2,1,0:T(8,128)(2,1)} %param.14) | copy-start | bytes 1179652
  11.7 126.8 %copy-start.224 = (s32[2,96]{1,0:T(2,128)S(1)}, s32[2,96]{1,0:T(2,128)}, u32[]{:S(2)}) copy-start(s32[2,96]{1,0:T(2,128)} %param.16) | copy-start | bytes 2308
  11.7 126.8 %copy-start.229 = (s32[2,1]{0,1:T(1,128)S(1)}, s32[2,1]{0,1:T(1,128)}, u32[]{:S(2)}) copy-start(s32[2,1]{0,1:T(1,128)} %param.17) | copy-start | bytes 28
  11.7 128.2 %copy-start.96 = (bf16[2,96,1024]{2,1,0:T(8,128)(2,1)S(1)}, bf16[2,96,1024]{2,1,0:T(8,128)(2,1)}, u32[]{:S(2)}) copy-start(bf16[2,96,1024]{2,1,0:T(8,128)(2,1)} %param.15) | copy-start | bytes 1179652
  11.7 290.4 %all-gather.35.cloned.1.call-start = ((), (), s32[]{:S(2)}) async-start(), calls=%async_computation.11 | async-start | bytes 8650752 | tf_op jit(solution)/shard_map/all_gather | solution.py:278
  12.7 347.2 %all-gather.31.cloned.1.call-start = ((), (), s32[]{:S(2)}) async-start(), calls=%async_computation.9 | async-start | bytes 2162688 | tf_op jit(solution)/shard_map/all_gather | solution.py:274
  13.2 417.8 %all-gather.37.cloned.1.call-start = ((), (), s32[]{:S(2)}) async-start(), calls=%async_computation.12 | async-start | bytes 6488064 | tf_op jit(solution)/shard_map/all_gather | solution.py:272
  13.8 496.8 %all-gather.41.cloned.1.call-start = ((), (), s32[]{:S(2)}) async-start(), calls=%async_computation.14 | async-start | bytes 8650752 | tf_op jit(solution)/shard_map/all_gather | solution.py:276
  14.6 575.1 %all-gather.43.cloned.1.call-start = ((), (), s32[]{:S(2)}) async-start(), calls=%async_computation.15 | async-start | bytes 8650752 | tf_op jit(solution)/shard_map/all_gather | solution.py:278
  15.3 766.8 %all-reduce.24.cloned.1.call-start = ((), (), s32[]{:S(2)}) async-start(), calls=%async_computation.16 | async-start | bytes 147456
  136.8 8.1 copy-start.159
  137.0 8.0 copy-start.192
  137.0 8.0 copy-start.194
  137.3 7.7 copy-start.210
  137.3 7.7 copy-start.212
  139.9 19.8 %copy-start.161 = (f32[96,8]{0,1:T(8,128)}, f32[96,8]{0,1:T(8,128)S(1)}, u32[]{:S(2)}) copy-start(f32[96,8]{0,1:T(8,128)S(1)} %get-tuple-element.162) | copy-start | bytes 9220
  142.4 80.3 %copy-start.28 = (bf16[96,1024]{1,0:T(8,128)(2,1)}, bf16[96,1024]{1,0:T(8,128)(2,1)S(1)}, u32[]{:S(2)}) copy-start(bf16[96,1024]{1,0:T(8,128)(2,1)S(1)} %get-tuple-element.108) | copy-start | bytes 589828
  161.9 60.8 %copy-start.134 = (f32[1,4096]{1,0:T(1,128)S(1)}, f32[1,4096]{1,0:T(1,128)}, u32[]{:S(2)}) copy-start(f32[1,4096]{1,0:T(1,128)} %convert_element_type.518) | copy-start | bytes 49156
  162.2 197.7 %copy-start.108 = (bf16[16,64,96]{2,1,0:T(8,128)(2,1)}, bf16[16,64,96]{2,1,0:T(8,128)(2,1)S(1)}, u32[]{:S(2)}) copy-start(bf16[16,64,96]{2,1,0:T(8,128)(2,1)S(1)} %convolution_convert_fusion.7) | copy-start | bytes 589828
  222.7 79.5 %copy-start.171 = (f32[1024]{0:T(1024)S(1)}, f32[1024]{0:T(1024)}, u32[]{:S(2)}) copy-start(f32[1024]{0:T(1024)} %convert_element_type.530) | copy-start | bytes 12292
  228.9 78.1 %copy-start.20 = (bf16[96,4096]{1,0:T(8,128)(2,1)}, bf16[96,4096]{1,0:T(8,128)(2,1)S(1)}, u32[]{:S(2)}) copy-start(bf16[96,4096]{1,0:T(8,128)(2,1)S(1)} %get-tuple-element.184) | copy-start | bytes 2359300
  302.1 57.7 %copy-start.167 = (f32[1024]{0:T(1024)S(1)}, f32[1024]{0:T(1024)}, u32[]{:S(2)}) copy-start(f32[1024]{0:T(1024)} %convert_element_type.529) | copy-start | bytes 12292
  359.9 71.2 %copy-start.157 = (f32[3072]{0:T(1024)S(1)}, f32[3072]{0:T(1024)}, u32[]{:S(2)}) copy-start(f32[3072]{0:T(1024)} %get-tuple-element.159) | copy-start | bytes 36868
  362.1 72.9 %copy-start.198 = (f32[96]{0:T(128)}, f32[96]{0:T(128)S(1)}, u32[]{:S(2)}) copy-start(f32[96]{0:T(128)S(1)} %broadcast_multiply_fusion.10) | copy-start | bytes 1156
  362.3 72.7 %copy-start.202 = (f32[96]{0:T(128)}, f32[96]{0:T(128)S(1)}, u32[]{:S(2)}) copy-start(f32[96]{0:T(128)S(1)} %add_rsqrt_fusion.2) | copy-start | bytes 1156
  362.5 154.7 %copy-start.30 = (bf16[96,1024]{1,0:T(8,128)(2,1)}, bf16[96,1024]{1,0:T(8,128)(2,1)S(1)}, u32[]{:S(2)}) copy-start(bf16[96,1024]{1,0:T(8,128)(2,1)S(1)} %add_convert_fusion.1) | copy-start | bytes 589828
  440.6 7.3 slice-start
  440.9 8.6 copy-start.110
  440.9 7.0 slice-start.1
  440.9 7.0 copy-start.172
  452.0 58.6 %copy-start.32 = (bf16[96,1024]{1,0:T(8,128)(2,1)}, bf16[96,1024]{1,0:T(8,128)(2,1)S(1)}, u32[]{:S(2)}) copy-start(bf16[96,1024]{1,0:T(8,128)(2,1)S(1)} %add_convert_fusion) | copy-start | bytes 589828
  467.0 8.2 copy-start.8
  469.7 6.7 copy-start.10
  473.9 36.7 %copy-start.133 = (f32[1,4096]{1,0:T(1,128)S(1)}, f32[1,4096]{1,0:T(1,128)}, u32[]{:S(2)}) copy-start(f32[1,4096]{1,0:T(1,128)} %convert_element_type.524) | copy-start | bytes 49156
  517.2 72.5 %copy-start.46 = (bf16[96,1024]{1,0:T(8,128)(2,1)S(1)}, bf16[96,1024]{1,0:T(8,128)(2,1)}, u32[]{:S(2)}) copy-start(bf16[96,1024]{1,0:T(8,128)(2,1)} %copy-done.45) | copy-start | bytes 589828
  589.7 7.6 copy-start
  589.7 7.6 copy-start.43
  589.7 13.5 slice-start.12
  589.7 16.5 slice-start.6
  597.2 9.0 copy-start.34
  597.3 9.0 slice-start.7
  628.1 8.8 slice-start.8
  650.3 6.7 copy-start.163
  650.3 9.3 copy-start.24
  650.3 9.3 copy-start.26
  650.3 9.3 copy-start.44
  659.3 311.1 %reduce-scatter.11.cloned.1.call-start = ((), (), s32[]{:S(2)}) async-start(), calls=%async_computation.7 | async-start | bytes 17301504 | tf_op jit(solution)/shard_map/reduce_scatter | solution.py:336
  668.8 488.6 %reduce-scatter.9.cloned.1.call-start = ((), (), s32[]{:S(2)}) async-start(), calls=%async_computation.6 | async-start | bytes 17301504 | tf_op jit(solution)/shard_map/reduce_scatter | solution.py:336
  678.5 837.0 %reduce-scatter.7.cloned.1.call-start = ((), (), s32[]{:S(2)}) async-start(), calls=%async_computation.5 | async-start | bytes 34603008 | tf_op jit(solution)/shard_map/reduce_scatter | solution.py:327
  683.2 7.1 copy-start.35
  683.3 7.1 copy-start.37
  720.0 1155.3 %reduce-scatter.5.cloned.1.call-start = ((), (), s32[]{:S(2)}) async-start(), calls=%async_computation.4 | async-start | bytes 34603008 | tf_op jit(solution)/shard_map/reduce_scatter | solution.py:327
  722.5 7.1 copy-start.39
  722.5 7.1 copy-start.41
  783.7 1095.6 %copy-start.215 = (f32[2,32]{1,0:T(2,128)}, f32[2,32]{1,0:T(2,128)S(1)}, u32[]{:S(2)}) copy-start(f32[2,32]{1,0:T(2,128)S(1)} %pad_maximum_fusion.65) | copy-start | bytes 772
  1515.5 361.9 %copy-start.106 = (f32[32,8192]{1,0:T(8,128)S(1)}, f32[32,8192]{1,0:T(8,128)}, u32[]{:S(2)}) copy-start(f32[32,8192]{1,0:T(8,128)} %reduce-scatter.7.cloned.1.call-done) | copy-start | bytes 3145732
  (193 other events, 430.9 us)
Sparse Core Ops, SparseCore 0:
  11.5 59.1 all-gather.38
  74.1 69.0 all-gather.28
  146.6 76.0 all-gather.32
  226.0 76.1 all-gather.34
  304.8 54.9 all-gather.30
  362.6 68.4 all-gather.36
  434.5 76.0 all-gather.40
  513.5 76.1 all-gather.42
  659.5 122.6 all-reduce.23
  784.4 185.9 reduce-scatter.10
  972.8 184.5 reduce-scatter.8
  1159.7 355.7 reduce-scatter.6
  1517.9 357.3 reduce-scatter.4
where the time goes:
time: 1900 us; the launch traced here: 1890 us
  waiting for transfers between devices  1450 us (76%)
  matrix products  170 us (9%)
  blocking collectives  118 us (6%)
  other arithmetic  76.3 us (4%)
  local copies, waits for them, and re-layouts  56.4 us (3%)
    reduce_scatter x2, waiting for transfers between devices, shards(): lax.psum_scatter(joint_term(hidden_all, merged_all, context_all, rounded_...  715 us
    reduce_scatter x2, waiting for transfers between devices, shards(): lax.psum_scatter(row_term(activation_all, rounded_all), ('dp', 'fsdp'), s...  365 us
    all_gather x2, waiting for transfers between devices, shards(): lax.all_gather(down_weight[layer_index], ('dp', 'fsdp'), axis=0, tiled=True)  143 us
    all_gather x2, waiting for transfers between devices, shards(): lax.all_gather(up_weight[layer_index], ('dp', 'fsdp'), axis=0, tiled=True)  93.6 us
    all_gather x2, blocking collectives, shards(): lax.all_gather(up_bias[layer_index], ('dp', 'fsdp'), axis=0, tiled=True)  79.4 us
    all_gather x2, waiting for transfers between devices, shards(): lax.all_gather(qkv_weight[layer_index], ('dp', 'fsdp'), axis=0, tiled=True)  68.6 us
    all_gather x2, waiting for transfers between devices, shards(): lax.all_gather(proj_weight[layer_index], ('dp', 'fsdp'), axis=0, tiled=True)  52.9 us
    concatenate x2, other arithmetic, joint_term(): return jnp.concatenate([merged_part, proj_part, up_part], axis=1)  42.7 us
  transfers between devices with their start and end apart: 13, of which 11 were waited for; matrix products, arithmetic and copies ran while one was open for 11% of the time, Pallas kernels for 0%

commit v1 on v0

v1 whole, which is shorter than its diff:
```python
import math

import jax
import jax.numpy as jnp
from jax import lax
from jax.sharding import Mesh
from jax.sharding import PartitionSpec as P

HEAD_DIM = 64
ROT = 16
EPS = 1e-05

AXES = ("e", "zh", "zl", "x", "y", "c")
HEAD_BITS = ("zh", "zl", "x", "y")
T1, T2, D1, D2 = "y", "zl", "zh", "x"
TP = (T1, T2, "c")
DP = ("e", D1, D2)

F32, BF16 = jnp.float32, jnp.bfloat16


def swap(value, *axes):
    pairs = []
    sizes = 2 ** len(axes)
    for i in range(sizes):
        pairs.append((i, sizes - 1 - i))
    return lax.ppermute(value, tuple(sorted(axes, key=AXES.index)), pairs)


def pick(value, dim, index):
    return lax.dynamic_index_in_dim(value, index, dim, keepdims=False)


def pair(value, axis):
    other = swap(value, axis)
    first = lax.axis_index(axis) == 0
    return jnp.where(first, jnp.stack([value, other]), jnp.stack([other, value]))


def gather_dp(value):
    out = pair(pair(value, D1), D2)
    out = jnp.swapaxes(out, 0, 1)
    return lax.all_gather(out, "e", axis=0)


def fold(value, dim, axis):
    index = lax.axis_index(axis)
    kept = pick(value, dim, index)
    sent = pick(value, dim, 1 - index).astype(BF16)
    return kept + swap(sent, axis).astype(F32)


def scatter_dp(value):
    if value.shape[0] > 1:
        value = lax.psum_scatter(value, "e", scatter_dimension=0, tiled=True)
    value = value[0]
    return fold(fold(value, 1, D2), 0, D1)


def trade(value, dim, axis):
    index = lax.axis_index(axis)
    kept = pick(value, dim, index)
    got = swap(pick(value, dim, 1 - index), axis)
    return jnp.where(
        index == 0, jnp.stack([kept, got], dim), jnp.stack([got, kept], dim)
    )


def trade_tp(value):
    return trade(trade(trade(value, 2, "c"), 1, T2), 0, T1)


def gather_rows(value):
    pieces = [value, swap(value, T2), swap(value, T1), swap(value, T1, T2)]
    near = jnp.stack(pieces)
    return jnp.stack([near, swap(near, "c")], 1)


def scatter_rows(value):
    near = value[:, 0] + swap(value[:, 1].astype(BF16), "c").astype(F32)
    sent = near[1:].astype(BF16)
    got = [swap(sent[0], T2), swap(sent[1], T1), swap(sent[2], T1, T2)]
    return near[0] + got[0].astype(F32) + got[1].astype(F32) + got[2].astype(F32)


def gather_small(value):
    for axis in reversed(AXES[1:]):
        value = pair(value, axis)
        value = value.reshape((-1,) + value.shape[2:]) if value.ndim > 2 else value
    return lax.all_gather(value, "e", axis=0, tiled=True)


def scatter_small(value):
    devices = value.shape[0]
    extra = devices // 32
    if extra > 1:
        value = lax.psum_scatter(value, "e", scatter_dimension=0, tiled=True)
    for axis in AXES[1:]:
        value = value.reshape((2, value.shape[0] // 2) + value.shape[1:])
        index = lax.axis_index(axis)
        value = pick(value, 0, index) + swap(pick(value, 0, 1 - index), axis)
    return value[0]


def split_heads(value, parts):
    lead = value.ndim - 1
    value = value.reshape(value.shape[:-1] + (parts, 2, 2, 2, 2, HEAD_DIM))
    place = {axis: lead + 1 + i for i, axis in enumerate(HEAD_BITS)}
    order = [place[T1], place[T2], place[D2]] + list(range(lead + 1)) + [place[D1], lead + 5]
    return value.transpose(order)


def join_heads(value):
    lead = value.ndim - 6
    names = {T1: 0, T2: 1, D2: 2, D1: lead + 4}
    order = [3 + i for i in range(lead)] + [3 + lead] + [names[a] for a in HEAD_BITS] + [lead + 5]
    value = value.transpose(order)
    return value.reshape(value.shape[:lead] + (-1,))


def split_hidden(value, extra):
    lead = value.ndim - 1
    value = value.reshape(value.shape[:-1] + (extra, 2, 2, 2, 2, 2, -1))
    place = {axis: lead + i for i, axis in enumerate(AXES)}
    order = [place[a] for a in TP] + list(range(lead)) + [place[a] for a in DP] + [lead + 6]
    return value.transpose(order)


def join_hidden(value):
    lead = value.ndim - 7
    names = {a: i for i, a in enumerate(TP)} | {a: 3 + lead + i for i, a in enumerate(DP)}
    order = [3 + i for i in range(lead)] + [names[a] for a in AXES] + [lead + 6]
    value = value.transpose(order)
    return value.reshape(value.shape[:lead] + (-1,))


def whole_rows(value):
    names = {a: i for i, a in enumerate(DP + TP)}
    order = [names[a] for a in AXES] + list(range(6, value.ndim))
    value = value.transpose(order)
    return value.reshape((-1,) + value.shape[7:])


def part_rows(value, extra):
    rows = value.shape[0]
    value = value.reshape((extra, 2, 2, 2, 2, 2, rows // (32 * extra)) + value.shape[1:])
    place = {axis: i for i, axis in enumerate(AXES)}
    return value.transpose([place[a] for a in DP + TP] + list(range(6, value.ndim)))


def own_part(value):
    for axis in TP:
        value = pick(value, 0, lax.axis_index(axis))
    return value


def gather_proj(block, extra):
    width = block.shape[1]
    if extra > 1:
        whole = lax.all_gather(block, AXES, axis=0, tiled=True)
        parted = split_heads(whole.T, 1)
        return own_part(parted).reshape(width, -1).T
    near = pair(pair(block, D1), D2)
    near = trade(near, 0, "c")
    return near.transpose(1, 0, 2, 3).reshape(-1, width)


def scatter_proj(value, extra):
    width = value.shape[1]
    if extra > 1:
        whole = jnp.zeros((2, 2, 2, 1, 2, HEAD_DIM, width), F32)
        place = [lax.axis_index(a) for a in TP] + [0, 0, 0, 0]
        whole = lax.dynamic_update_slice(whole, value.reshape(1, 1, 1, 1, 2, HEAD_DIM, width), place)
        names = {T1: 0, T2: 1, D2: 2, D1: 4}
        whole = whole.transpose([names[a] for a in HEAD_BITS] + [3, 5, 6]).reshape(-1, width)
        return lax.psum_scatter(whole, AXES, scatter_dimension=0, tiled=True)
    value = value.reshape(2, 2, HEAD_DIM // 2, width).transpose(1, 0, 2, 3)
    index = lax.axis_index("c")
    kept = pick(value, 0, index)
    got = swap(pick(value, 0, 1 - index).astype(BF16), "c").astype(F32)
    value = jnp.where(index == 0, jnp.stack([kept, got]), jnp.stack([got, kept]))
    return fold(fold(value, 0, D2), 0, D1)


def rotate(vectors, cosine, sine):
    half = cosine.shape[-1]
    a, b = vectors[..., :half], vectors[..., half : 2 * half]
    return jnp.concatenate(
        [a * cosine - b * sine, b * cosine + a * sine, vectors[..., 2 * half :]], axis=-1
    )


def normalise(stream):
    average = jnp.mean(stream, axis=-1, keepdims=True)
    centred = stream - average
    variance = jnp.mean(centred * centred, axis=-1, keepdims=True)
    inverse = lax.rsqrt(variance + EPS)
    return centred * inverse, inverse


def dot(a, b, contract):
    return lax.dot_general(a, b, (contract, ((), ())), preferred_element_type=F32)


def forward(hidden, weights, allowed, cosine, sine):
    qkv, qkv_bias, proj, up, up_bias, down = weights
    rows, packs, pack = hidden.shape[0], allowed.shape[0], allowed.shape[1]
    merged = dot(hidden, qkv, ((1,), (0,))) + qkv_bias
    merged = merged.reshape(packs, pack, 3, 2, HEAD_DIM)
    queries = rotate(merged[:, :, 0], cosine, sine).astype(BF16)
    keys = rotate(merged[:, :, 1], cosine, sine).astype(BF16)
    values = merged[:, :, 2].astype(BF16)
    scores = jnp.einsum("pqhd,pkhd->phqk", queries, keys, preferred_element_type=F32)
    scores = jnp.where(allowed[:, None], scores * (1.0 / math.sqrt(HEAD_DIM)), -1e30)
    shifted = jnp.exp(scores - jnp.max(scores, axis=-1, keepdims=True))
    soft = shifted / jnp.sum(shifted, axis=-1, keepdims=True)
    context = jnp.einsum("phqk,pkhd->pqhd", soft.astype(BF16), values, preferred_element_type=F32)
    context = context.reshape(rows, 2 * HEAD_DIM).astype(BF16)
    raised = dot(hidden, up, ((1,), (0,))) + up_bias
    cdf = 0.5 * (1.0 + lax.erf(raised * 0.7071067811865476))
    density = jnp.exp(-0.5 * raised * raised) * 0.3989422804014327
    activation = (raised * cdf).astype(BF16)
    slope = cdf + raised * density
    partial = dot(context, proj, ((1,), (0,))) + dot(activation, down, ((1,), (0,)))
    return partial, (queries, keys, values, soft, context, activation, slope)


def backward(hidden, rounded, weights, stored, cosine, sine):
    qkv, _, proj, up, _, down = weights
    queries, keys, values, soft, context, activation, slope = stored
    rows, packs, pack = hidden.shape[0], queries.shape[0], queries.shape[1]
    up_delta = (dot(rounded, down, ((1,), (1,))) * slope).astype(BF16)
    context_delta = dot(rounded, proj, ((1,), (1,))).astype(BF16)
    context_delta = context_delta.reshape(packs, pack, 2, HEAD_DIM)
    down_grad = dot(activation, rounded, ((0,), (0,)))
    proj_grad = dot(context, rounded, ((0,), (0,)))
    value_delta = jnp.einsum(
        "phqk,pqhd->pkhd", soft.astype(BF16), context_delta, preferred_element_type=F32
    )
    prob_delta = jnp.einsum("pqhd,pkhd->phqk", context_delta, values, preferred_element_type=F32)
    row_delta = jnp.sum(soft * prob_delta, axis=-1, keepdims=True)
    score_delta = (soft * (prob_delta - row_delta)).astype(BF16)
    scale = 1.0 / math.sqrt(HEAD_DIM)
    query_delta = jnp.einsum("phqk,pkhd->pqhd", score_delta, keys, preferred_element_type=F32)
    key_delta = jnp.einsum("phqk,pqhd->pkhd", score_delta, queries, preferred_element_type=F32)
    merged_delta = jnp.stack(
        [
            rotate(query_delta * scale, cosine, -sine),
            rotate(key_delta * scale, cosine, -sine),
            value_delta,
        ],
        axis=2,
    )
    merged_delta = merged_delta.astype(BF16).reshape(rows, -1)
    partial = dot(merged_delta, qkv, ((1,), (1,))) + dot(up_delta, up, ((1,), (1,)))
    up_grad = dot(hidden, up_delta, ((0,), (0,)))
    qkv_grad = dot(hidden, merged_delta, ((0,), (0,)))
    upbias_grad = jnp.sum(up_delta, axis=0, dtype=F32)
    qkvbias_grad = jnp.sum(merged_delta, axis=0, dtype=F32)
    return partial, (qkv_grad, qkvbias_grad, proj_grad, up_grad, upbias_grad, down_grad)


def shards(
    inputs,
    cotangent,
    segments,
    pack_length,
    norm_gain,
    norm_shift,
    qkv_weight,
    qv_bias,
    proj_weight,
    proj_bias,
    up_weight,
    up_bias,
    down_weight,
    down_bias,
):
    micros, pack, width = inputs.shape
    layers = qkv_weight.shape[0]
    extra = lax.axis_size("e")
    devices = 32 * extra
    position = jnp.arange(pack)
    is_live = position[None, :] < pack_length
    marks = gather_rows(jnp.concatenate([segments, pack_length], axis=1)).reshape(-1, pack + 1)
    group_segments, group_length = marks[:, :pack], marks[:, pack:]
    group_live = position[None, :] < group_length
    causal = position[:, None] >= position[None, :]
    diagonal = position[:, None] == position[None, :]
    allowed = (
        (group_segments[:, :, None] == group_segments[:, None, :])
        & causal
        & (group_live[:, None, :] | diagonal)
    )
    angle = position.astype(F32)[:, None] * (
        10000.0 ** (-jnp.arange(0, ROT, 2, dtype=F32) / ROT)
    )[None, :]
    cosine, sine = jnp.cos(angle)[:, None, :], jnp.sin(angle)[:, None, :]

    small = jnp.concatenate(
        [norm_gain, norm_shift, qv_bias, proj_bias, up_bias, down_bias], axis=1
    )
    cuts = [norm_gain.shape[1], norm_shift.shape[1], qv_bias.shape[1], proj_bias.shape[1]]
    cuts = cuts + [up_bias.shape[1], down_bias.shape[1]]
    offsets = [sum(cuts[:i]) for i in range(7)]
    small = gather_small(small.reshape(-1)).reshape(devices, layers, -1).astype(F32)
    vectors = []
    for layer in range(layers):
        vectors.append(
            [small[:, layer, offsets[i] : offsets[i + 1]].reshape(-1) for i in range(6)]
        )

    weights = []
    for layer in range(layers):
        gain, shift, qv, projb, upb, downb = vectors[layer]
        qkv_parts = split_heads(qkv_weight[layer], 3)
        qkv_parts = qkv_parts.reshape(qkv_parts.shape[:4] + (-1,))
        up_parts = split_hidden(up_weight[layer], extra)
        up_parts = up_parts.reshape(up_parts.shape[:4] + (-1,))
        qkv_block = trade_tp(qkv_parts)
        up_block = trade_tp(up_parts)
        qkv = whole_rows(gather_dp(qkv_block))
        up = whole_rows(gather_dp(up_block))
        proj = gather_proj(proj_weight[layer], extra)
        down = gather_dp(down_weight[layer]).reshape(-1, width)
        q_bias = own_part(split_heads(qv[:width], 1)).reshape(-1)
        v_bias = own_part(split_heads(qv[width:], 1)).reshape(-1)
        bias = jnp.concatenate([q_bias, jnp.zeros_like(q_bias), v_bias])
        upb = own_part(split_hidden(upb, extra)).reshape(-1)
        weights.append((qkv, bias, proj, up, upb, down))

    stream = inputs.astype(F32)
    kept = []
    for layer in range(layers):
        gain, shift, _, projb, _, downb = vectors[layer]
        normed, inverse = normalise(stream)
        hidden = (normed * gain + shift).astype(BF16)
        group_hidden = gather_rows(hidden).reshape(-1, width)
        partial, stored = forward(group_hidden, weights[layer], allowed, cosine, sine)
        kept.append((normed, inverse, group_hidden, stored))
        total = scatter_rows(partial.reshape(4, 2, micros, pack, width))
        stream = stream + total + (projb + downb)
    outputs = stream.astype(BF16)

    upstream = cotangent.astype(F32) * is_live[:, :, None].astype(F32)
    grads = [None] * layers
    for layer in reversed(range(layers)):
        gain = vectors[layer][0]
        normed, inverse, group_hidden, stored = kept[layer]
        rounded = upstream.astype(BF16)
        bias_sum = jnp.sum(rounded, axis=(0, 1), dtype=F32)
        group_rounded = gather_rows(rounded).reshape(-1, width)
        partial, slices = backward(
            group_hidden, group_rounded, weights[layer], stored, cosine, sine
        )
        qkv_grad, qkvbias_grad, proj_grad, up_grad, upbias_grad, down_grad = slices
        hidden_delta = scatter_rows(partial.reshape(4, 2, micros, pack, width))
        gain_grad = jnp.sum(hidden_delta * normed, axis=(0, 1))
        shift_grad = jnp.sum(hidden_delta, axis=(0, 1))
        scaled = hidden_delta * gain
        upstream = upstream + inverse * (
            scaled
            - jnp.mean(scaled, axis=-1, keepdims=True)
            - normed * jnp.mean(scaled * normed, axis=-1, keepdims=True)
        )
        down_own = scatter_dp(down_grad.reshape(extra, 2, 2, -1, width))
        proj_own = scatter_proj(proj_grad, extra)
        up_own = trade_tp(scatter_dp(part_rows(up_grad, extra)).astype(BF16))
        qkv_own = trade_tp(scatter_dp(part_rows(qkv_grad, extra)).astype(BF16))
        rows = up_own.shape[3]
        up_own = join_hidden(up_own.reshape(2, 2, 2, rows, extra, 2, 2, -1)).astype(F32)
        qkv_own = join_heads(qkv_own.reshape(2, 2, 2, rows, 3, 2, HEAD_DIM)).astype(F32)

        place = [lax.axis_index(a) for a in TP]
        per = qkvbias_grad.shape[0] // 3
        wide = jnp.zeros((2, 2, 2, 2, 2, HEAD_DIM), F32)
        both = jnp.stack([qkvbias_grad[:per], qkvbias_grad[2 * per :]]).reshape(1, 1, 1, 2, 2, HEAD_DIM)
        qv_full = join_heads(lax.dynamic_update_slice(wide, both, place + [0, 0, 0])[:, :, :, :, :, :])
        chunk = up_bias.shape[1]
        wide = jnp.zeros((2, 2, 2, extra, 2, 2, chunk), F32)
        upb_full = join_hidden(
            lax.dynamic_update_slice(
                wide, upbias_grad.reshape(1, 1, 1, extra, 2, 2, chunk), place + [0] * 4
            )
        )
        small_grad = jnp.concatenate(
            [
                v.reshape(devices, -1)
                for v in (gain_grad, shift_grad, qv_full, bias_sum, upb_full)
            ],
            axis=1,
        )
        grads[layer] = (small_grad, qkv_own, proj_own, up_own, down_own)
    input_grad = upstream

    small_out = scatter_small(jnp.stack([g[0] for g in grads], axis=1))
    bounds = [0]
    for size in (cuts[0], cuts[1], cuts[2], cuts[3], cuts[4]):
        bounds.append(bounds[-1] + size)
    gain_out, shift_out, qvbias_out, projbias_out, upbias_out = [
        small_out[:, bounds[i] : bounds[i + 1]] for i in range(5)
    ]
    return (
        outputs,
        input_grad,
        gain_out,
        shift_out,
        jnp.stack([g[1] for g in grads]),
        qvbias_out,
        jnp.stack([g[2] for g in grads]),
        projbias_out,
        jnp.stack([g[3] for g in grads]),
        upbias_out,
        jnp.stack([g[4] for g in grads]),
        projbias_out,
    )


def solution(mesh):
    devices = mesh.devices.size
    fine = Mesh(mesh.devices.reshape(devices // 32, 2, 2, 2, 2, 2), AXES)
    cube, flat = P(None, AXES, None), P(None, AXES)
    placed = (cube, cube, flat, flat, flat, flat, cube, flat, cube, flat, cube, flat, cube, flat)
    given = (cube, cube, flat, flat, cube, flat, cube, flat, cube, flat, cube, flat)
    return jax.shard_map(shards, mesh=fine, in_specs=placed, out_specs=given, check_vma=False)
```

time: 1900 us -> 706 us (0.37)
  waiting for transfers between devices: 1450 us -> 277 us
  blocking collectives: 118 us -> 0 us
  starting transfers between devices: 0.91 us -> 107 us
  local copies, waits for them, and re-layouts: 56.4 us -> 158 us
  matrix products: 170 us -> 74.1 us
    reduce_scatter x4 -> x0, waiting for transfers between devices: 1080 us -> none  [the longest x2 715 us: shards(): lax.psum_scatter(joint_term(hidden_all, merged_all, context_all, rounded_...]
    all_gather x8 -> x0, waiting for transfers between devices: 358 us -> none  [the longest x2 143 us: shards(): lax.all_gather(down_weight[layer_index], ('dp', 'fsdp'), axis=0, tiled=True)]
    ppermute x0 -> x106, waiting for transfers between devices: none -> 277 us  [swap(): return lax.ppermute(value, tuple(sorted(axes, key=AXES.index)), pairs)]
    ppermute x0 -> x106, starting transfers between devices: none -> 107 us  [swap(): return lax.ppermute(value, tuple(sorted(axes, key=AXES.index)), pairs)]
    dot_general x64 -> x34, matrix products: 170 us -> 69.6 us  [the longest x24 58.7 us: dot(): lax.dot_general(a, b, (contract, ((), ())), preferred_element_type=F32)]
    all_gather x2 -> x0, blocking collectives: 79.4 us -> none  [shards(): lax.all_gather(up_bias[layer_index], ('dp', 'fsdp'), axis=0, tiled=True)]
    concatenate x11 -> x2, other arithmetic: 46.6 us -> 1.34 us  [the longest x1 0.75 us: shards(): jnp.concatenate([segments, pack_length], axis=1)]
    unnamed x1 -> x0, blocking collectives: 38.5 us -> none
  transfers between devices with their start and end apart: 13 -> 106, of which waited for: 11 -> 51; matrix products, arithmetic and copies ran while one was open for 11% -> 29% of each run, Pallas kernels for 0% -> 0%
where the time goes in v1:
time: 706 us; the launch traced here: 700 us
  waiting for transfers between devices  277 us (39%)
  local copies, waits for them, and re-layouts  158 us (22%)
  starting transfers between devices  107 us (15%)
  other arithmetic  80.2 us (11%)
  matrix products  74.1 us (10%)
    ppermute x106, waiting for transfers between devices, swap(): return lax.ppermute(value, tuple(sorted(axes, key=AXES.index)), pairs)  277 us
    ppermute x106, starting transfers between devices, swap(): return lax.ppermute(value, tuple(sorted(axes, key=AXES.index)), pairs)  107 us
    dot_general x24, matrix products, dot(): lax.dot_general(a, b, (contract, ((), ())), preferred_element_type=F32)  58.7 us
    unnamed x258, local copies, waits for them, and re-layouts  39.2 us
  transfers between devices with their start and end apart: 106, of which 51 were waited for; matrix products, arithmetic and copies ran while one was open for 29% of the time, Pallas kernels for 0%

profile of v1, /device:TPU:0, one launch (start us, length us, event | category | flops | bytes accessed | tf_op | source)
XLA Modules:
  0.0 699.8 jit_solution(7733298412498961000)
XLA Ops:
  2.1 3.0 collective-permute-start.15
  9.2 3.0 collective-permute-start.18
  38.4 2.9 collective-permute-start.4
  43.2 2.9 collective-permute-start.26
  60.7 5.1 collective-permute-done.10
  68.6 10.3 %collective-permute-done.22 = bf16[2,2,32,512]{3,2,1,0:T(8,128)(2,1)S(1)} collective-permute-done((bf16[2,2,32,512]{3,2,1,0:T(8,128)(2,1)S(1)}, bf16[2,2,32,512]{3,2,1,0:T(8,128)(2,1)S(1)}, u32[]{:S(2)}, u32[]{:S(2)}) %collective-permute-start.22) | collective-permute-done | bytes 131104 | tf_op jit(solution)/shard_map/ppermute | solution.py:27
  79.3 4.1 collective-permute-done.11
  86.6 2.9 collective-permute-done.23
  91.6 10.9 %collective-permute-done.12 = bf16[2,2,2,32,384]{4,3,2,0,1:T(8,128)(2,1)S(1)} collective-permute-done((bf16[2,2,2,32,384]{4,3,2,0,1:T(8,128)(2,1)S(1)}, bf16[2,2,2,32,384]{4,3,2,0,1:T(8,128)(2,1)S(1)}, u32[]{:S(2)}, u32[]{:S(2)}) %collective-permute-start.12) | collective-permute-done | bytes 196640 | tf_op jit(solution)/shard_map/ppermute | solution.py:27
  104.1 3.4 collective-permute-done.24
  110.5 6.9 collective-permute-done.27
  118.5 7.3 %collective-permute-done.13 = bf16[2,2,2,2,32,384]{5,4,3,1,2,0:T(8,128)(2,1)S(1)} collective-permute-done((bf16[2,2,2,2,32,384]{5,4,3,1,2,0:T(8,128)(2,1)S(1)}, bf16[2,2,2,2,32,384]{5,4,3,1,2,0:T(8,128)(2,1)S(1)}, u32[]{:S(2)}, u32[]{:S(2)}) %collective-permute-start.13) | collective-permute-done | bytes 393248 | tf_op jit(solution)/shard_map/ppermute | solution.py:27
  126.4 8.4 %collective-permute-done.25 = bf16[2,2,2,2,32,512]{5,4,3,1,2,0:T(8,128)(2,1)S(1)} collective-permute-done((bf16[2,2,2,2,32,512]{5,4,3,1,2,0:T(8,128)(2,1)S(1)}, bf16[2,2,2,2,32,512]{5,4,3,1,2,0:T(8,128)(2,1)S(1)}, u32[]{:S(2)}, u32[]{:S(2)}) %collective-permute-start.25) | collective-permute-done | bytes 524320 | tf_op jit(solution)/shard_map/ppermute | solution.py:27
  137.9 3.3 convolution_add_fusion.7
  141.2 5.9 reshape.1916
  149.1 3.4 fusion.196
  154.3 3.4 copy.275
  170.8 5.7 fusion.20
  184.8 4.3 collective-permute-start.37
  192.4 3.0 collective-permute-done.45
  204.5 7.6 %collective-permute-done.29 = bf16[2,96,1024]{2,1,0:T(8,128)(2,1)S(1)} collective-permute-done((bf16[2,96,1024]{2,1,0:T(8,128)(2,1)S(1)}, bf16[2,96,1024]{2,1,0:T(8,128)(2,1)S(1)}, u32[]{:S(2)}, u32[]{:S(2)}) %collective-permute-start.29) | collective-permute-done | bytes 393248 | tf_op jit(solution)/shard_map/ppermute | solution.py:27
  213.9 6.8 collective-permute-done.31
  226.3 4.9 collective-permute-done.56
  232.9 4.7 collective-permute-start.34
  239.3 7.2 %collective-permute-done.33 = bf16[2,96,1024]{2,1,0:T(8,128)(2,1)S(1)} collective-permute-done((bf16[2,96,1024]{2,1,0:T(8,128)(2,1)S(1)}, bf16[2,96,1024]{2,1,0:T(8,128)(2,1)S(1)}, u32[]{:S(2)}, u32[]{:S(2)}) %collective-permute-start.33) | collective-permute-done | bytes 393248 | tf_op jit(solution)/shard_map/ppermute | solution.py:27
  251.3 8.8 %collective-permute-done.39 = bf16[2,2,2,32,384]{4,3,2,0,1:T(8,128)(2,1)S(1)} collective-permute-done((bf16[2,2,2,32,384]{4,3,2,0,1:T(8,128)(2,1)S(1)}, bf16[2,2,2,32,384]{4,3,2,0,1:T(8,128)(2,1)S(1)}, u32[]{:S(2)}, u32[]{:S(2)}) %collective-permute-start.39) | collective-permute-done | bytes 196640 | tf_op jit(solution)/shard_map/ppermute | solution.py:27
  266.6 5.2 collective-permute-done.40
  273.0 6.3 collective-permute-done.48
  285.2 2.9 copy.204
  288.1 4.7 copy.228
  296.6 3.2 convolution_add_fusion.6
  299.8 5.9 reshape.1917
  305.7 2.9 slice.424
  308.6 3.4 fusion.195
  312.0 3.4 copy.280
  325.3 3.0 fusion.44
  332.2 3.4 fusion.21
  335.7 4.3 convert_reduce_fusion
  340.0 3.8 fusion.27
  351.3 2.7 convert_element_type.580
  354.0 5.2 copy.231
  359.3 3.4 fusion.204
  375.2 2.7 copy-done.8
  387.5 16.2 %collective-permute-done.90 = bf16[2,32,1024]{2,1,0:T(8,128)(2,1)S(1)} collective-permute-done((bf16[2,32,1024]{2,1,0:T(8,128)(2,1)S(1)}, bf16[2,32,1024]{2,1,0:T(8,128)(2,1)S(1)}, u32[]{:S(2)}, u32[]{:S(2)}) %collective-permute-start.90) | collective-permute-done | bytes 131104 | tf_op jit(solution)/shard_map/ppermute | solution.py:27
  417.8 11.6 %collective-permute-done.82 = bf16[2,2,2,32,384]{4,3,2,0,1:T(8,128)(2,1)S(1)} collective-permute-done((bf16[2,2,2,32,384]{4,3,2,0,1:T(8,128)(2,1)S(1)}, bf16[2,2,2,32,384]{4,3,2,0,1:T(8,128)(2,1)S(1)}, u32[]{:S(2)}, u32[]{:S(2)}) %collective-permute-start.82) | collective-permute-done | bytes 196640 | tf_op jit(solution)/shard_map/ppermute | solution.py:27
  435.3 8.1 %collective-permute-done.60 = bf16[2,96,1024]{2,1,0:T(8,128)(2,1)S(1)} collective-permute-done((bf16[2,96,1024]{2,1,0:T(8,128)(2,1)S(1)}, bf16[2,96,1024]{2,1,0:T(8,128)(2,1)S(1)}, u32[]{:S(2)}, u32[]{:S(2)}) %collective-permute-start.60) | collective-permute-done | bytes 393248 | tf_op jit(solution)/shard_map/ppermute | solution.py:27
  443.4 8.2 %collective-permute-done.62 = bf16[2,96,1024]{2,1,0:T(8,128)(2,1)S(1)} collective-permute-done((bf16[2,96,1024]{2,1,0:T(8,128)(2,1)S(1)}, bf16[2,96,1024]{2,1,0:T(8,128)(2,1)S(1)}, u32[]{:S(2)}, u32[]{:S(2)}) %collective-permute-start.62) | collective-permute-done | bytes 393248 | tf_op jit(solution)/shard_map/ppermute | solution.py:27
  454.5 5.8 collective-permute-done.52
  460.3 8.2 %collective-permute-done.54 = bf16[2,96,1024]{2,1,0:T(8,128)(2,1)S(1)} collective-permute-done((bf16[2,96,1024]{2,1,0:T(8,128)(2,1)S(1)}, bf16[2,96,1024]{2,1,0:T(8,128)(2,1)S(1)}, u32[]{:S(2)}, u32[]{:S(2)}) %collective-permute-start.54) | collective-permute-done | bytes 393248 | tf_op jit(solution)/shard_map/ppermute | solution.py:27
  478.2 13.3 %collective-permute-done.65 = bf16[2,96,1024]{2,1,0:T(8,128)(2,1)S(1)} collective-permute-done((bf16[2,96,1024]{2,1,0:T(8,128)(2,1)S(1)}, bf16[2,96,1024]{2,1,0:T(8,128)(2,1)S(1)}, u32[]{:S(2)}, u32[]{:S(2)}) %collective-permute-start.65) | collective-permute-done | bytes 393248 | tf_op jit(solution)/shard_map/ppermute | solution.py:27
  491.5 7.7 %collective-permute-done.63 = bf16[2,96,1024]{2,1,0:T(8,128)(2,1)S(1)} collective-permute-done((bf16[2,96,1024]{2,1,0:T(8,128)(2,1)S(1)}, bf16[2,96,1024]{2,1,0:T(8,128)(2,1)S(1)}, u32[]{:S(2)}, u32[]{:S(2)}) %collective-permute-start.63) | collective-permute-done | bytes 393248 | tf_op jit(solution)/shard_map/ppermute | solution.py:27
  528.8 4.3 convert_reduce_fusion.2
  550.3 2.9 convert_element_type.590
  553.2 3.7 fusion.205
  566.2 2.7 copy-done.5
  571.0 15.9 %collective-permute-done.87 = bf16[2,32,1024]{2,1,0:T(8,128)(2,1)S(1)} collective-permute-done((bf16[2,32,1024]{2,1,0:T(8,128)(2,1)S(1)}, bf16[2,32,1024]{2,1,0:T(8,128)(2,1)S(1)}, u32[]{:S(2)}, u32[]{:S(2)}) %collective-permute-start.87) | collective-permute-done | bytes 131104 | tf_op jit(solution)/shard_map/ppermute | solution.py:27
  601.3 11.2 %collective-permute-done.77 = bf16[2,2,2,32,384]{4,3,2,0,1:T(8,128)(2,1)S(1)} collective-permute-done((bf16[2,2,2,32,384]{4,3,2,0,1:T(8,128)(2,1)S(1)}, bf16[2,2,2,32,384]{4,3,2,0,1:T(8,128)(2,1)S(1)}, u32[]{:S(2)}, u32[]{:S(2)}) %collective-permute-start.77) | collective-permute-done | bytes 196640 | tf_op jit(solution)/shard_map/ppermute | solution.py:27
  614.9 2.9 collective-permute-start.103
  617.8 3.2 collective-permute-done.79
  624.0 6.5 collective-permute-done.103
  636.3 3.5 collective-permute-done.95
  639.9 4.9 fusion.184
  651.2 17.7 %collective-permute-done.96 = bf16[2,2,32,512]{3,2,1,0:T(8,128)(2,1)} collective-permute-done((bf16[2,2,32,512]{3,2,1,0:T(8,128)(2,1)S(1)}, bf16[2,2,32,512]{3,2,1,0:T(8,128)(2,1)}, u32[]{:S(2)}, u32[]{:S(2)}) %collective-permute-start.96) | collective-permute-done | bytes 131104 | tf_op jit(solution)/shard_map/ppermute | solution.py:27
  670.7 2.8 fusion.65
  (778 shorter events, 328.4 us)
Async XLA Ops:
  2.1 23.4 %collective-permute-start.15 = (s32[2,97]{1,0:T(2,128)S(1)}, s32[2,97]{1,0:T(2,128)S(1)}, u32[]{:S(2)}, u32[]{:S(2)}) collective-permute-start(s32[2,97]{1,0:T(2,128)S(1)} %pad_add_fusion.2), channel_id=1, source_target_pairs={{0,2},{2,0},{1,3},{3,1},{4,6},{6,4},{5,7},{7,5},{8,10},{10,8},{9,1... | collective-permute-start | bytes 2336 | tf_op jit(solution)/shard_map/ppermute | solution.py:27
  5.1 20.4 %collective-permute-start.14 = (s32[2,97]{1,0:T(2,128)S(1)}, s32[2,97]{1,0:T(2,128)S(1)}, u32[]{:S(2)}, u32[]{:S(2)}) collective-permute-start(s32[2,97]{1,0:T(2,128)S(1)} %pad_add_fusion.2), channel_id=1, source_target_pairs={{0,8},{8,0},{1,9},{9,1},{2,10},{10,2},{3,11},{11,3},{4,12},{12,4},... | collective-permute-start | bytes 2336 | tf_op jit(solution)/shard_map/ppermute | solution.py:27
  6.7 19.1 %collective-permute-start.16 = (s32[2,97]{1,0:T(2,128)S(1)}, s32[2,97]{1,0:T(2,128)S(1)}, u32[]{:S(2)}, u32[]{:S(2)}) collective-permute-start(s32[2,97]{1,0:T(2,128)S(1)} %pad_add_fusion.2), channel_id=1, source_target_pairs={{0,10},{2,8},{8,2},{10,0},{1,11},{3,9},{9,3},{11,1},{4,14},{6,12},... | collective-permute-start | bytes 2336 | tf_op jit(solution)/shard_map/ppermute | solution.py:27
  7.6 18.5 %collective-permute-start = (bf16[640]{0:T(1024)(128)(2,1)S(1)}, bf16[640]{0:T(1024)(128)(2,1)S(1)}, u32[]{:S(2)}, u32[]{:S(2)}) collective-permute-start(bf16[640]{0:T(1024)(128)(2,1)S(1)} %reshape.1862), channel_id=1, source_target_pairs={{0,1},{1,0},{2,3},{3,2},{4,5},{5,4},{6,7},{7,6},{8,9},{9,8},{10,11... | collective-permute-start | bytes 3848 | tf_op jit(solution)/shard_map/ppermute | solution.py:27
  9.2 42.7 %collective-permute-start.18 = (bf16[32,1024]{1,0:T(8,128)(2,1)S(1)}, bf16[32,1024]{1,0:T(8,128)(2,1)S(1)}, u32[]{:S(2)}, u32[]{:S(2)}) collective-permute-start(bf16[32,1024]{1,0:T(8,128)(2,1)S(1)} %get-tuple-element.155), channel_id=1, source_target_pairs={{0,16},{16,0},{1,17},{17,1},{2,18},{18,2},{3,19},{19,3},{4,20},{20... | collective-permute-start | bytes 196616 | tf_op jit(solution)/shard_map/ppermute | solution.py:27
  25.5 154.2 %collective-permute-start.41 = (bf16[32,1024]{1,0:T(8,128)(2,1)}, bf16[32,1024]{1,0:T(8,128)(2,1)}, u32[]{:S(2)}, u32[]{:S(2)}) collective-permute-start(bf16[32,1024]{1,0:T(8,128)(2,1)} %get-tuple-element.156), channel_id=1, source_target_pairs={{0,16},{16,0},{1,17},{17,1},{2,18},{18,2},{3,19},{19,3},{4,20},{20... | collective-permute-start | bytes 196616 | tf_op jit(solution)/shard_map/ppermute | solution.py:27
  25.5 27.9 %collective-permute-start.9 = (bf16[2,2,32,384]{3,2,0,1:T(8,128)(2,1)}, bf16[2,2,32,384]{3,2,0,1:T(8,128)(2,1)S(1)}, u32[]{:S(2)}, u32[]{:S(2)}) collective-permute-start(bf16[2,2,32,384]{3,2,0,1:T(8,128)(2,1)} %get-tuple-element.152), channel_id=1, source_target_pairs={{0,1},{1,0},{2,3},{3,2},{4,5},{5,4},{6,7},{7,6},{8,9},{9,8},{10,11... | collective-permute-start | bytes 294920 | tf_op jit(solution)/shard_map/ppermute | solution.py:27
  25.8 29.4 %collective-permute-start.21 = (bf16[2,2,32,512]{3,2,0,1:T(8,128)(2,1)}, bf16[2,2,32,512]{3,2,0,1:T(8,128)(2,1)}, u32[]{:S(2)}, u32[]{:S(2)}) collective-permute-start(bf16[2,2,32,512]{3,2,0,1:T(8,128)(2,1)} %get-tuple-element.126), channel_id=1, source_target_pairs={{0,1},{1,0},{2,3},{3,2},{4,5},{5,4},{6,7},{7,6},{8,9},{9,8},{10,11... | collective-permute-start | bytes 393224 | tf_op jit(solution)/shard_map/ppermute | solution.py:27
  43.2 22.7 %collective-permute-start.26 = (bf16[128,1024]{1,0:T(8,128)(2,1)S(1)}, bf16[128,1024]{1,0:T(8,128)(2,1)S(1)}, u32[]{:S(2)}, u32[]{:S(2)}) collective-permute-start(bf16[128,1024]{1,0:T(8,128)(2,1)S(1)} %get-tuple-element.91), channel_id=1, source_target_pairs={{0,16},{16,0},{1,17},{17,1},{2,18},{18,2},{3,19},{19,3},{4,20},{20... | collective-permute-start | bytes 786440 | tf_op jit(solution)/shard_map/ppermute | solution.py:27
  51.8 31.7 %collective-permute-start.6 = (bf16[2,96,1024]{2,1,0:T(8,128)(2,1)}, bf16[2,96,1024]{2,1,0:T(8,128)(2,1)S(1)}, u32[]{:S(2)}, u32[]{:S(2)}) collective-permute-start(bf16[2,96,1024]{2,1,0:T(8,128)(2,1)} %fusion.60), channel_id=1, source_target_pairs={{0,2},{2,0},{1,3},{3,1},{4,6},{6,4},{5,7},{7,5},{8,10},{10,8},{9,1... | collective-permute-start | bytes 1179656 | tf_op jit(solution)/shard_map/ppermute | solution.py:27
  53.4 30.6 %collective-permute-start.5 = (bf16[2,96,1024]{2,1,0:T(8,128)(2,1)}, bf16[2,96,1024]{2,1,0:T(8,128)(2,1)S(1)}, u32[]{:S(2)}, u32[]{:S(2)}) collective-permute-start(bf16[2,96,1024]{2,1,0:T(8,128)(2,1)} %fusion.60), channel_id=1, source_target_pairs={{0,8},{8,0},{1,9},{9,1},{2,10},{10,2},{3,11},{11,3},{4,12},{12,4},... | collective-permute-start | bytes 1179656 | tf_op jit(solution)/shard_map/ppermute | solution.py:27
  65.8 20.5 %collective-permute-start.7 = (bf16[2,96,1024]{2,1,0:T(8,128)(2,1)}, bf16[2,96,1024]{2,1,0:T(8,128)(2,1)S(1)}, u32[]{:S(2)}, u32[]{:S(2)}) collective-permute-start(bf16[2,96,1024]{2,1,0:T(8,128)(2,1)} %fusion.60), channel_id=1, source_target_pairs={{0,10},{2,8},{8,2},{10,0},{1,11},{3,9},{9,3},{11,1},{4,14},{6,12},... | collective-permute-start | bytes 1179656 | tf_op jit(solution)/shard_map/ppermute | solution.py:27
  83.5 25.6 %collective-permute-start.20 = (bf16[2,32,1024]{2,1,0:T(8,128)(2,1)S(1)}, bf16[2,32,1024]{2,1,0:T(8,128)(2,1)S(1)}, u32[]{:S(2)}, u32[]{:S(2)}) collective-permute-start(bf16[2,32,1024]{2,1,0:T(8,128)(2,1)S(1)} %get-tuple-element.118), channel_id=1, source_target_pairs={{0,1},{1,0},{2,3},{3,2},{4,5},{5,4},{6,7},{7,6},{8,9},{9,8},{10,11... | collective-permute-start | bytes 393224 | tf_op jit(solution)/shard_map/ppermute | solution.py:27
  84.1 18.5 %collective-permute-start.12 = (bf16[2,2,2,32,384]{4,3,2,0,1:T(8,128)(2,1)S(1)}, bf16[2,2,2,32,384]{4,3,2,0,1:T(8,128)(2,1)S(1)}, u32[]{:S(2)}, u32[]{:S(2)}) collective-permute-start(bf16[2,2,2,32,384]{4,3,2,0,1:T(8,128)(2,1)S(1)} %maximum_select_fusion.36), channel_id=1, source_target_pairs={{0,16},{16,0},{1,17},{17,1},{2,18},{18,2},{3,19},{19,3},{4,20},{20... | collective-permute-start | bytes 589832 | tf_op jit(solution)/shard_map/ppermute | solution.py:27
  86.5 49.4 %collective-permute-start.8 = (bf16[4,2,96,1024]{3,2,1,0:T(8,128)(2,1)S(1)}, bf16[4,2,96,1024]{3,2,1,0:T(8,128)(2,1)S(1)}, u32[]{:S(2)}, u32[]{:S(2)}) collective-permute-start(bf16[4,2,96,1024]{3,2,1,0:T(8,128)(2,1)S(1)} %get-tuple-element.69), channel_id=1, source_target_pairs={{0,1},{1,0},{2,3},{3,2},{4,5},{5,4},{6,7},{7,6},{8,9},{9,8},{10,11... | collective-permute-start | bytes 4718600 | tf_op jit(solution)/shard_map/ppermute | solution.py:27
  89.6 17.9 %collective-permute-start.24 = (bf16[2,2,2,32,512]{4,3,2,0,1:T(8,128)(2,1)S(1)}, bf16[2,2,2,32,512]{4,3,2,0,1:T(8,128)(2,1)S(1)}, u32[]{:S(2)}, u32[]{:S(2)}) collective-permute-start(bf16[2,2,2,32,512]{4,3,2,0,1:T(8,128)(2,1)S(1)} %maximum_select_fusion.23), channel_id=1, source_target_pairs={{0,16},{16,0},{1,17},{17,1},{2,18},{18,2},{3,19},{19,3},{4,20},{20... | collective-permute-start | bytes 786440 | tf_op jit(solution)/shard_map/ppermute | solution.py:27
  107.4 18.4 %collective-permute-start.13 = (bf16[2,2,2,2,32,384]{5,4,3,1,2,0:T(8,128)(2,1)S(1)}, bf16[2,2,2,2,32,384]{5,4,3,1,2,0:T(8,128)(2,1)S(1)}, u32[]{:S(2)}, u32[]{:S(2)}) collective-permute-start(bf16[2,2,2,2,32,384]{5,4,3,1,2,0:T(8,128)(2,1)S(1)} %maximum_select_fusion.16), channel_id=1, source_target_pairs={{0,4},{4,0},{1,5},{5,1},{2,6},{6,2},{3,7},{7,3},{8,12},{12,8},{9,1... | collective-permute-start | bytes 1179656 | tf_op jit(solution)/shard_map/ppermute | solution.py:27
  109.0 25.7 %collective-permute-start.25 = (bf16[2,2,2,2,32,512]{5,4,3,1,2,0:T(8,128)(2,1)S(1)}, bf16[2,2,2,2,32,512]{5,4,3,1,2,0:T(8,128)(2,1)S(1)}, u32[]{:S(2)}, u32[]{:S(2)}) collective-permute-start(bf16[2,2,2,2,32,512]{5,4,3,1,2,0:T(8,128)(2,1)S(1)} %maximum_select_fusion.7), channel_id=1, source_target_pairs={{0,4},{4,0},{1,5},{5,1},{2,6},{6,2},{3,7},{7,3},{8,12},{12,8},{9,1... | collective-permute-start | bytes 1572872 | tf_op jit(solution)/shard_map/ppermute | solution.py:27
  117.4 64.8 %collective-permute-start.36 = (bf16[2,2,32,384]{3,2,0,1:T(8,128)(2,1)}, bf16[2,2,32,384]{3,2,0,1:T(8,128)(2,1)}, u32[]{:S(2)}, u32[]{:S(2)}) collective-permute-start(bf16[2,2,32,384]{3,2,0,1:T(8,128)(2,1)} %get-tuple-element.144), channel_id=1, source_target_pairs={{0,1},{1,0},{2,3},{3,2},{4,5},{5,4},{6,7},{7,6},{8,9},{9,8},{10,11... | collective-permute-start | bytes 294920 | tf_op jit(solution)/shard_map/ppermute | solution.py:27
  125.8 99.1 %collective-permute-start.57 = (bf16[2,96,1024]{2,1,0:T(8,128)(2,1)S(1)}, bf16[2,96,1024]{2,1,0:T(8,128)(2,1)}, u32[]{:S(2)}, u32[]{:S(2)}) collective-permute-start(bf16[2,96,1024]{2,1,0:T(8,128)(2,1)S(1)} %get-tuple-element.27), channel_id=1, source_target_pairs={{0,10},{2,8},{8,2},{10,0},{1,11},{3,9},{9,3},{11,1},{4,14},{6,12},... | collective-permute-start | bytes 1179656 | tf_op jit(solution)/shard_map/ppermute | solution.py:27
  134.7 50.1 %collective-permute-start.44 = (bf16[2,2,32,512]{3,2,0,1:T(8,128)(2,1)}, bf16[2,2,32,512]{3,2,0,1:T(8,128)(2,1)}, u32[]{:S(2)}, u32[]{:S(2)}) collective-permute-start(bf16[2,2,32,512]{3,2,0,1:T(8,128)(2,1)} %get-tuple-element.116), channel_id=1, source_target_pairs={{0,1},{1,0},{2,3},{3,2},{4,5},{5,4},{6,7},{7,6},{8,9},{9,8},{10,11... | collective-permute-start | bytes 393224 | tf_op jit(solution)/shard_map/ppermute | solution.py:27
  135.9 60.8 %collective-permute-start.49 = (bf16[128,1024]{1,0:T(8,128)(2,1)}, bf16[128,1024]{1,0:T(8,128)(2,1)}, u32[]{:S(2)}, u32[]{:S(2)}) collective-permute-start(bf16[128,1024]{1,0:T(8,128)(2,1)} %get-tuple-element.92), channel_id=1, source_target_pairs={{0,16},{16,0},{1,17},{17,1},{2,18},{18,2},{3,19},{19,3},{4,20},{20... | collective-permute-start | bytes 786440 | tf_op jit(solution)/shard_map/ppermute | solution.py:27
  179.7 19.3 %collective-permute-start.28 = (bf16[4,2,96,1024]{3,2,1,0:T(8,128)(2,1)S(1)}, bf16[4,2,96,1024]{3,2,1,0:T(8,128)(2,1)S(1)}, u32[]{:S(2)}, u32[]{:S(2)}) collective-permute-start(bf16[4,2,96,1024]{3,2,1,0:T(8,128)(2,1)S(1)} %fusion.28), channel_id=1, source_target_pairs={{0,1},{1,0},{2,3},{3,2},{4,5},{5,4},{6,7},{7,6},{8,9},{9,8},{10,11... | collective-permute-start | bytes 4718600 | tf_op jit(solution)/shard_map/ppermute | solution.py:27
  201.8 18.9 %collective-permute-start.31 = (bf16[2,96,1024]{2,1,0:T(8,128)(2,1)S(1)}, bf16[2,96,1024]{2,1,0:T(8,128)(2,1)S(1)}, u32[]{:S(2)}, u32[]{:S(2)}) collective-permute-start(bf16[2,96,1024]{2,1,0:T(8,128)(2,1)S(1)} %get-tuple-element.66), channel_id=1, source_target_pairs={{0,10},{2,8},{8,2},{10,0},{1,11},{3,9},{9,3},{11,1},{4,14},{6,12},... | collective-permute-start | bytes 1179656 | tf_op jit(solution)/shard_map/ppermute | solution.py:27
  202.2 20.5 %collective-permute-start.30 = (bf16[2,96,1024]{2,1,0:T(8,128)(2,1)S(1)}, bf16[2,96,1024]{2,1,0:T(8,128)(2,1)S(1)}, u32[]{:S(2)}, u32[]{:S(2)}) collective-permute-start(bf16[2,96,1024]{2,1,0:T(8,128)(2,1)S(1)} %get-tuple-element.67), channel_id=1, source_target_pairs={{0,2},{2,0},{1,3},{3,1},{4,6},{6,4},{5,7},{7,5},{8,10},{10,8},{9,1... | collective-permute-start | bytes 1179656 | tf_op jit(solution)/shard_map/ppermute | solution.py:27
  203.7 27.4 %collective-permute-start.56 = (bf16[2,96,1024]{2,1,0:T(8,128)(2,1)S(1)}, bf16[2,96,1024]{2,1,0:T(8,128)(2,1)S(1)}, u32[]{:S(2)}, u32[]{:S(2)}) collective-permute-start(bf16[2,96,1024]{2,1,0:T(8,128)(2,1)S(1)} %get-tuple-element.27), channel_id=1, source_target_pairs={{0,2},{2,0},{1,3},{3,1},{4,6},{6,4},{5,7},{7,5},{8,10},{10,8},{9,1... | collective-permute-start | bytes 1179656 | tf_op jit(solution)/shard_map/ppermute | solution.py:27
  212.1 20.8 %collective-permute-start.55 = (bf16[2,96,1024]{2,1,0:T(8,128)(2,1)S(1)}, bf16[2,96,1024]{2,1,0:T(8,128)(2,1)S(1)}, u32[]{:S(2)}, u32[]{:S(2)}) collective-permute-start(bf16[2,96,1024]{2,1,0:T(8,128)(2,1)S(1)} %get-tuple-element.27), channel_id=1, source_target_pairs={{0,8},{8,0},{1,9},{9,1},{2,10},{10,2},{3,11},{11,3},{4,12},{12,4},... | collective-permute-start | bytes 1179656 | tf_op jit(solution)/shard_map/ppermute | solution.py:27
  220.7 18.2 %collective-permute-start.46 = (bf16[2,2,32,512]{3,2,1,0:T(8,128)(2,1)S(1)}, bf16[2,2,32,512]{3,2,1,0:T(8,128)(2,1)S(1)}, u32[]{:S(2)}, u32[]{:S(2)}) collective-permute-start(bf16[2,2,32,512]{3,2,1,0:T(8,128)(2,1)S(1)} %get-tuple-element.111), channel_id=1, source_target_pairs={{0,2},{2,0},{1,3},{3,1},{4,6},{6,4},{5,7},{7,5},{8,10},{10,8},{9,1... | collective-permute-start | bytes 393224 | tf_op jit(solution)/shard_map/ppermute | solution.py:27
  222.7 42.7 %collective-permute-start.50 = (bf16[2,128,1024]{2,1,0:T(8,128)(2,1)S(1)}, bf16[2,128,1024]{2,1,0:T(8,128)(2,1)S(1)}, u32[]{:S(2)}, u32[]{:S(2)}) collective-permute-start(bf16[2,128,1024]{2,1,0:T(8,128)(2,1)S(1)} %maximum_select_fusion.12), channel_id=1, source_target_pairs={{0,4},{4,0},{1,5},{5,1},{2,6},{6,2},{3,7},{7,3},{8,12},{12,8},{9,1... | collective-permute-start | bytes 1572872 | tf_op jit(solution)/shard_map/ppermute | solution.py:27
  224.9 21.6 %collective-permute-start.33 = (bf16[2,96,1024]{2,1,0:T(8,128)(2,1)S(1)}, bf16[2,96,1024]{2,1,0:T(8,128)(2,1)S(1)}, u32[]{:S(2)}, u32[]{:S(2)}) collective-permute-start(bf16[2,96,1024]{2,1,0:T(8,128)(2,1)S(1)} %add_convert_fusion), channel_id=1, source_target_pairs={{0,2},{2,0},{1,3},{3,1},{4,6},{6,4},{5,7},{7,5},{8,10},{10,8},{9,1... | collective-permute-start | bytes 1179656 | tf_op jit(solution)/shard_map/ppermute | solution.py:27
  231.1 17.1 %collective-permute-start.32 = (bf16[2,96,1024]{2,1,0:T(8,128)(2,1)S(1)}, bf16[2,96,1024]{2,1,0:T(8,128)(2,1)S(1)}, u32[]{:S(2)}, u32[]{:S(2)}) collective-permute-start(bf16[2,96,1024]{2,1,0:T(8,128)(2,1)S(1)} %add_convert_fusion), channel_id=1, source_target_pairs={{0,8},{8,0},{1,9},{9,1},{2,10},{10,2},{3,11},{11,3},{4,12},{12,4},... | collective-permute-start | bytes 1179656 | tf_op jit(solution)/shard_map/ppermute | solution.py:27
  232.9 16.5 %collective-permute-start.34 = (bf16[2,96,1024]{2,1,0:T(8,128)(2,1)S(1)}, bf16[2,96,1024]{2,1,0:T(8,128)(2,1)S(1)}, u32[]{:S(2)}, u32[]{:S(2)}) collective-permute-start(bf16[2,96,1024]{2,1,0:T(8,128)(2,1)S(1)} %add_convert_fusion), channel_id=1, source_target_pairs={{0,10},{2,8},{8,2},{10,0},{1,11},{3,9},{9,3},{11,1},{4,14},{6,12},... | collective-permute-start | bytes 1179656 | tf_op jit(solution)/shard_map/ppermute | solution.py:27
  238.9 41.7 %collective-permute-start.58 = (bf16[4,2,96,1024]{3,2,1,0:T(8,128)(2,1)S(1)}, bf16[4,2,96,1024]{3,2,1,0:T(8,128)(2,1)S(1)}, u32[]{:S(2)}, u32[]{:S(2)}) collective-permute-start(bf16[4,2,96,1024]{3,2,1,0:T(8,128)(2,1)S(1)} %get-tuple-element.59), channel_id=1, source_target_pairs={{0,1},{1,0},{2,3},{3,2},{4,5},{5,4},{6,7},{7,6},{8,9},{9,8},{10,11... | collective-permute-start | bytes 4718600 | tf_op jit(solution)/shard_map/ppermute | solution.py:27
  250.9 41.9 %collective-permute-start.35 = (bf16[4,2,96,1024]{3,2,1,0:T(8,128)(2,1)}, bf16[4,2,96,1024]{3,2,1,0:T(8,128)(2,1)}, u32[]{:S(2)}, u32[]{:S(2)}) collective-permute-start(bf16[4,2,96,1024]{3,2,1,0:T(8,128)(2,1)} %get-tuple-element.64), channel_id=1, source_target_pairs={{0,1},{1,0},{2,3},{3,2},{4,5},{5,4},{6,7},{7,6},{8,9},{9,8},{10,11... | collective-permute-start | bytes 4718600 | tf_op jit(solution)/shard_map/ppermute | solution.py:27
  348.0 37.2 %collective-permute-start.89 = (bf16[2,32,1024]{2,1,0:T(8,128)(2,1)}, bf16[2,32,1024]{2,1,0:T(8,128)(2,1)}, u32[]{:S(2)}, u32[]{:S(2)}) collective-permute-start(bf16[2,32,1024]{2,1,0:T(8,128)(2,1)} %fusion.127), channel_id=1, source_target_pairs={{0,1},{1,0},{2,3},{3,2},{4,5},{5,4},{6,7},{7,6},{8,9},{9,8},{10,11... | collective-permute-start | bytes 393224 | tf_op jit(solution)/shard_map/ppermute | solution.py:27
  367.2 42.6 %collective-permute-start.81 = (bf16[2,2,2,2,32,384]{5,4,3,1,2,0:T(8,128)(2,1)}, bf16[2,2,2,2,32,384]{5,4,3,1,2,0:T(8,128)(2,1)S(1)}, u32[]{:S(2)}, u32[]{:S(2)}) collective-permute-start(bf16[2,2,2,2,32,384]{5,4,3,1,2,0:T(8,128)(2,1)} %fusion.103), channel_id=1, source_target_pairs={{0,4},{4,0},{1,5},{5,1},{2,6},{6,2},{3,7},{7,3},{8,12},{12,8},{9,1... | collective-permute-start | bytes 1179656 | tf_op jit(solution)/shard_map/ppermute | solution.py:27
  371.2 42.1 %collective-permute-start.104 = (bf16[2,128,1024]{2,1,0:T(8,128)(2,1)}, bf16[2,128,1024]{2,1,0:T(8,128)(2,1)}, u32[]{:S(2)}, u32[]{:S(2)}) collective-permute-start(bf16[2,128,1024]{2,1,0:T(8,128)(2,1)} %fusion.89), channel_id=1, source_target_pairs={{0,4},{4,0},{1,5},{5,1},{2,6},{6,2},{3,7},{7,3},{8,12},{12,8},{9,1... | collective-permute-start | bytes 1572872 | tf_op jit(solution)/shard_map/ppermute | solution.py:27
  373.2 43.4 %collective-permute-start.97 = (bf16[2,2,2,2,32,512]{5,4,3,1,2,0:T(8,128)(2,1)}, bf16[2,2,2,2,32,512]{5,4,3,1,2,0:T(8,128)(2,1)}, u32[]{:S(2)}, u32[]{:S(2)}) collective-permute-start(bf16[2,2,2,2,32,512]{5,4,3,1,2,0:T(8,128)(2,1)} %fusion.88), channel_id=1, source_target_pairs={{0,4},{4,0},{1,5},{5,1},{2,6},{6,2},{3,7},{7,3},{8,12},{12,8},{9,1... | collective-permute-start | bytes 1572872 | tf_op jit(solution)/shard_map/ppermute | solution.py:27
  385.2 44.3 %collective-permute-start.59 = (bf16[4,2,96,1024]{3,2,1,0:T(8,128)(2,1)}, bf16[4,2,96,1024]{3,2,1,0:T(8,128)(2,1)S(1)}, u32[]{:S(2)}, u32[]{:S(2)}) collective-permute-start(bf16[4,2,96,1024]{3,2,1,0:T(8,128)(2,1)} %fusion.30), channel_id=1, source_target_pairs={{0,1},{1,0},{2,3},{3,2},{4,5},{5,4},{6,7},{7,6},{8,9},{9,8},{10,11... | collective-permute-start | bytes 4718600 | tf_op jit(solution)/shard_map/ppermute | solution.py:27
  386.3 17.4 %collective-permute-start.90 = (bf16[2,32,1024]{2,1,0:T(8,128)(2,1)S(1)}, bf16[2,32,1024]{2,1,0:T(8,128)(2,1)S(1)}, u32[]{:S(2)}, u32[]{:S(2)}) collective-permute-start(bf16[2,32,1024]{2,1,0:T(8,128)(2,1)S(1)} %fusion.126), channel_id=1, source_target_pairs={{0,4},{4,0},{1,5},{5,1},{2,6},{6,2},{3,7},{7,3},{8,12},{12,8},{9,1... | collective-permute-start | bytes 393224 | tf_op jit(solution)/shard_map/ppermute | solution.py:27
  409.1 25.0 %collective-permute-start.51 = (bf16[4,2,96,1024]{3,2,1,0:T(8,128)(2,1)}, bf16[4,2,96,1024]{3,2,1,0:T(8,128)(2,1)S(1)}, u32[]{:S(2)}, u32[]{:S(2)}) collective-permute-start(bf16[4,2,96,1024]{3,2,1,0:T(8,128)(2,1)} %fusion.29), channel_id=1, source_target_pairs={{0,1},{1,0},{2,3},{3,2},{4,5},{5,4},{6,7},{7,6},{8,9},{9,8},{10,11... | collective-permute-start | bytes 4718600 | tf_op jit(solution)/shard_map/ppermute | solution.py:27
  411.2 18.3 %collective-permute-start.82 = (bf16[2,2,2,32,384]{4,3,2,0,1:T(8,128)(2,1)S(1)}, bf16[2,2,2,32,384]{4,3,2,0,1:T(8,128)(2,1)S(1)}, u32[]{:S(2)}, u32[]{:S(2)}) collective-permute-start(bf16[2,2,2,32,384]{4,3,2,0,1:T(8,128)(2,1)S(1)} %fusion.123), channel_id=1, source_target_pairs={{0,16},{16,0},{1,17},{17,1},{2,18},{18,2},{3,19},{19,3},{4,20},{20... | collective-permute-start | bytes 589832 | tf_op jit(solution)/shard_map/ppermute | solution.py:27
  415.7 90.6 %collective-permute-start.105 = (bf16[128,1024]{1,0:T(8,128)(2,1)}, bf16[128,1024]{1,0:T(8,128)(2,1)}, u32[]{:S(2)}, u32[]{:S(2)}) collective-permute-start(bf16[128,1024]{1,0:T(8,128)(2,1)} %fusion.115), channel_id=1, source_target_pairs={{0,16},{16,0},{1,17},{17,1},{2,18},{18,2},{3,19},{19,3},{4,20},{20... | collective-permute-start | bytes 786440 | tf_op jit(solution)/shard_map/ppermute | solution.py:27
  430.6 21.0 %collective-permute-start.62 = (bf16[2,96,1024]{2,1,0:T(8,128)(2,1)S(1)}, bf16[2,96,1024]{2,1,0:T(8,128)(2,1)S(1)}, u32[]{:S(2)}, u32[]{:S(2)}) collective-permute-start(bf16[2,96,1024]{2,1,0:T(8,128)(2,1)S(1)} %get-tuple-element.56), channel_id=1, source_target_pairs={{0,10},{2,8},{8,2},{10,0},{1,11},{3,9},{9,3},{11,1},{4,14},{6,12},... | collective-permute-start | bytes 1179656 | tf_op jit(solution)/shard_map/ppermute | solution.py:27
  432.3 21.0 %collective-permute-start.61 = (bf16[2,96,1024]{2,1,0:T(8,128)(2,1)S(1)}, bf16[2,96,1024]{2,1,0:T(8,128)(2,1)S(1)}, u32[]{:S(2)}, u32[]{:S(2)}) collective-permute-start(bf16[2,96,1024]{2,1,0:T(8,128)(2,1)S(1)} %get-tuple-element.57), channel_id=1, source_target_pairs={{0,2},{2,0},{1,3},{3,1},{4,6},{6,4},{5,7},{7,5},{8,10},{10,8},{9,1... | collective-permute-start | bytes 1179656 | tf_op jit(solution)/shard_map/ppermute | solution.py:27
  435.2 25.1 %collective-permute-start.52 = (bf16[2,96,1024]{2,1,0:T(8,128)(2,1)S(1)}, bf16[2,96,1024]{2,1,0:T(8,128)(2,1)S(1)}, u32[]{:S(2)}, u32[]{:S(2)}) collective-permute-start(bf16[2,96,1024]{2,1,0:T(8,128)(2,1)S(1)} %get-tuple-element.60), channel_id=1, source_target_pairs={{0,8},{8,0},{1,9},{9,1},{2,10},{10,2},{3,11},{11,3},{4,12},{12,4},... | collective-permute-start | bytes 1179656 | tf_op jit(solution)/shard_map/ppermute | solution.py:27
  443.4 25.1 %collective-permute-start.54 = (bf16[2,96,1024]{2,1,0:T(8,128)(2,1)S(1)}, bf16[2,96,1024]{2,1,0:T(8,128)(2,1)S(1)}, u32[]{:S(2)}, u32[]{:S(2)}) collective-permute-start(bf16[2,96,1024]{2,1,0:T(8,128)(2,1)S(1)} %get-tuple-element.61), channel_id=1, source_target_pairs={{0,10},{2,8},{8,2},{10,0},{1,11},{3,9},{9,3},{11,1},{4,14},{6,12},... | collective-permute-start | bytes 1179656 | tf_op jit(solution)/shard_map/ppermute | solution.py:27
  451.7 19.4 %collective-permute-start.53 = (bf16[2,96,1024]{2,1,0:T(8,128)(2,1)S(1)}, bf16[2,96,1024]{2,1,0:T(8,128)(2,1)S(1)}, u32[]{:S(2)}, u32[]{:S(2)}) collective-permute-start(bf16[2,96,1024]{2,1,0:T(8,128)(2,1)S(1)} %get-tuple-element.62), channel_id=1, source_target_pairs={{0,2},{2,0},{1,3},{3,1},{4,6},{6,4},{5,7},{7,5},{8,10},{10,8},{9,1... | collective-permute-start | bytes 1179656 | tf_op jit(solution)/shard_map/ppermute | solution.py:27
  472.9 18.6 %collective-permute-start.65 = (bf16[2,96,1024]{2,1,0:T(8,128)(2,1)S(1)}, bf16[2,96,1024]{2,1,0:T(8,128)(2,1)S(1)}, u32[]{:S(2)}, u32[]{:S(2)}) collective-permute-start(bf16[2,96,1024]{2,1,0:T(8,128)(2,1)S(1)} %get-tuple-element.31), channel_id=1, source_target_pairs={{0,10},{2,8},{8,2},{10,0},{1,11},{3,9},{9,3},{11,1},{4,14},{6,12},... | collective-permute-start | bytes 1179656 | tf_op jit(solution)/shard_map/ppermute | solution.py:27
  472.9 18.6 %collective-permute-start.64 = (bf16[2,96,1024]{2,1,0:T(8,128)(2,1)S(1)}, bf16[2,96,1024]{2,1,0:T(8,128)(2,1)S(1)}, u32[]{:S(2)}, u32[]{:S(2)}) collective-permute-start(bf16[2,96,1024]{2,1,0:T(8,128)(2,1)S(1)} %get-tuple-element.31), channel_id=1, source_target_pairs={{0,2},{2,0},{1,3},{3,1},{4,6},{6,4},{5,7},{7,5},{8,10},{10,8},{9,1... | collective-permute-start | bytes 1179656 | tf_op jit(solution)/shard_map/ppermute | solution.py:27
  474.6 24.6 %collective-permute-start.63 = (bf16[2,96,1024]{2,1,0:T(8,128)(2,1)S(1)}, bf16[2,96,1024]{2,1,0:T(8,128)(2,1)S(1)}, u32[]{:S(2)}, u32[]{:S(2)}) collective-permute-start(bf16[2,96,1024]{2,1,0:T(8,128)(2,1)S(1)} %get-tuple-element.31), channel_id=1, source_target_pairs={{0,8},{8,0},{1,9},{9,1},{2,10},{10,2},{3,11},{11,3},{4,12},{12,4},... | collective-permute-start | bytes 1179656 | tf_op jit(solution)/shard_map/ppermute | solution.py:27
  477.8 22.9 %collective-permute-start.98 = (bf16[2,2,2,32,512]{4,3,2,0,1:T(8,128)(2,1)S(1)}, bf16[2,2,2,32,512]{4,3,2,0,1:T(8,128)(2,1)S(1)}, u32[]{:S(2)}, u32[]{:S(2)}) collective-permute-start(bf16[2,2,2,32,512]{4,3,2,0,1:T(8,128)(2,1)S(1)} %fusion.113), channel_id=1, source_target_pairs={{0,16},{16,0},{1,17},{17,1},{2,18},{18,2},{3,19},{19,3},{4,20},{20... | collective-permute-start | bytes 786440 | tf_op jit(solution)/shard_map/ppermute | solution.py:27
  500.7 23.1 %collective-permute-start.66 = (bf16[4,2,96,1024]{3,2,1,0:T(8,128)(2,1)}, bf16[4,2,96,1024]{3,2,1,0:T(8,128)(2,1)}, u32[]{:S(2)}, u32[]{:S(2)}) collective-permute-start(bf16[4,2,96,1024]{3,2,1,0:T(8,128)(2,1)} %get-tuple-element.54), channel_id=1, source_target_pairs={{0,1},{1,0},{2,3},{3,2},{4,5},{5,4},{6,7},{7,6},{8,9},{9,8},{10,11... | collective-permute-start | bytes 4718600 | tf_op jit(solution)/shard_map/ppermute | solution.py:27
  543.9 26.4 %collective-permute-start.86 = (bf16[2,32,1024]{2,1,0:T(8,128)(2,1)S(1)}, bf16[2,32,1024]{2,1,0:T(8,128)(2,1)S(1)}, u32[]{:S(2)}, u32[]{:S(2)}) collective-permute-start(bf16[2,32,1024]{2,1,0:T(8,128)(2,1)S(1)} %fusion.124), channel_id=1, source_target_pairs={{0,1},{1,0},{2,3},{3,2},{4,5},{5,4},{6,7},{7,6},{8,9},{9,8},{10,11... | collective-permute-start | bytes 393224 | tf_op jit(solution)/shard_map/ppermute | solution.py:27
  546.8 65.9 %collective-permute-start.102 = (bf16[2,128,1024]{2,1,0:T(8,128)(2,1)}, bf16[2,128,1024]{2,1,0:T(8,128)(2,1)}, u32[]{:S(2)}, u32[]{:S(2)}) collective-permute-start(bf16[2,128,1024]{2,1,0:T(8,128)(2,1)} %fusion.87), channel_id=1, source_target_pairs={{0,4},{4,0},{1,5},{5,1},{2,6},{6,2},{3,7},{7,3},{8,12},{12,8},{9,1... | collective-permute-start | bytes 1572872 | tf_op jit(solution)/shard_map/ppermute | solution.py:27
  561.4 33.7 %collective-permute-start.76 = (bf16[2,2,2,2,32,384]{5,4,3,1,2,0:T(8,128)(2,1)}, bf16[2,2,2,2,32,384]{5,4,3,1,2,0:T(8,128)(2,1)}, u32[]{:S(2)}, u32[]{:S(2)}) collective-permute-start(bf16[2,2,2,2,32,384]{5,4,3,1,2,0:T(8,128)(2,1)} %fusion.102), channel_id=1, source_target_pairs={{0,4},{4,0},{1,5},{5,1},{2,6},{6,2},{3,7},{7,3},{8,12},{12,8},{9,1... | collective-permute-start | bytes 1179656 | tf_op jit(solution)/shard_map/ppermute | solution.py:27
  562.8 34.4 %collective-permute-start.92 = (bf16[2,2,2,2,32,512]{5,4,3,1,2,0:T(8,128)(2,1)}, bf16[2,2,2,2,32,512]{5,4,3,1,2,0:T(8,128)(2,1)}, u32[]{:S(2)}, u32[]{:S(2)}) collective-permute-start(bf16[2,2,2,2,32,512]{5,4,3,1,2,0:T(8,128)(2,1)} %fusion.86), channel_id=1, source_target_pairs={{0,4},{4,0},{1,5},{5,1},{2,6},{6,2},{3,7},{7,3},{8,12},{12,8},{9,1... | collective-permute-start | bytes 1572872 | tf_op jit(solution)/shard_map/ppermute | solution.py:27
  570.2 69.6 %collective-permute-start.67 = (bf16[4,2,96,1024]{3,2,1,0:T(8,128)(2,1)}, bf16[4,2,96,1024]{3,2,1,0:T(8,128)(2,1)}, u32[]{:S(2)}, u32[]{:S(2)}) collective-permute-start(bf16[4,2,96,1024]{3,2,1,0:T(8,128)(2,1)} %fusion.31), channel_id=1, source_target_pairs={{0,1},{1,0},{2,3},{3,2},{4,5},{5,4},{6,7},{7,6},{8,9},{9,8},{10,11... | collective-permute-start | bytes 4718600 | tf_op jit(solution)/shard_map/ppermute | solution.py:27
  570.4 16.5 %collective-permute-start.87 = (bf16[2,32,1024]{2,1,0:T(8,128)(2,1)S(1)}, bf16[2,32,1024]{2,1,0:T(8,128)(2,1)S(1)}, u32[]{:S(2)}, u32[]{:S(2)}) collective-permute-start(bf16[2,32,1024]{2,1,0:T(8,128)(2,1)S(1)} %fusion.125), channel_id=1, source_target_pairs={{0,4},{4,0},{1,5},{5,1},{2,6},{6,2},{3,7},{7,3},{8,12},{12,8},{9,1... | collective-permute-start | bytes 393224 | tf_op jit(solution)/shard_map/ppermute | solution.py:27
  599.3 22.7 %collective-permute-start.93 = (bf16[2,2,2,32,512]{4,3,2,0,1:T(8,128)(2,1)}, bf16[2,2,2,32,512]{4,3,2,0,1:T(8,128)(2,1)}, u32[]{:S(2)}, u32[]{:S(2)}) collective-permute-start(bf16[2,2,2,32,512]{4,3,2,0,1:T(8,128)(2,1)} %fusion.112), channel_id=1, source_target_pairs={{0,16},{16,0},{1,17},{17,1},{2,18},{18,2},{3,19},{19,3},{4,20},{20... | collective-permute-start | bytes 786440 | tf_op jit(solution)/shard_map/ppermute | solution.py:27
  645.8 24.0 %collective-permute-start.68 = (bf16[2,96,1024]{2,1,0:T(8,128)(2,1)}, bf16[2,96,1024]{2,1,0:T(8,128)(2,1)S(1)}, u32[]{:S(2)}, u32[]{:S(2)}) collective-permute-start(bf16[2,96,1024]{2,1,0:T(8,128)(2,1)} %get-tuple-element.50), channel_id=1, source_target_pairs={{0,8},{8,0},{1,9},{9,1},{2,10},{10,2},{3,11},{11,3},{4,12},{12,4},... | collective-permute-start | bytes 1179656 | tf_op jit(solution)/shard_map/ppermute | solution.py:27
  646.1 23.7 %collective-permute-start.70 = (bf16[2,96,1024]{2,1,0:T(8,128)(2,1)}, bf16[2,96,1024]{2,1,0:T(8,128)(2,1)S(1)}, u32[]{:S(2)}, u32[]{:S(2)}) collective-permute-start(bf16[2,96,1024]{2,1,0:T(8,128)(2,1)} %get-tuple-element.51), channel_id=1, source_target_pairs={{0,10},{2,8},{8,2},{10,0},{1,11},{3,9},{9,3},{11,1},{4,14},{6,12},... | collective-permute-start | bytes 1179656 | tf_op jit(solution)/shard_map/ppermute | solution.py:27
  648.1 21.8 %collective-permute-start.69 = (bf16[2,96,1024]{2,1,0:T(8,128)(2,1)}, bf16[2,96,1024]{2,1,0:T(8,128)(2,1)}, u32[]{:S(2)}, u32[]{:S(2)}) collective-permute-start(bf16[2,96,1024]{2,1,0:T(8,128)(2,1)} %get-tuple-element.52), channel_id=1, source_target_pairs={{0,2},{2,0},{1,3},{3,1},{4,6},{6,4},{5,7},{7,5},{8,10},{10,8},{9,1... | collective-permute-start | bytes 1179656 | tf_op jit(solution)/shard_map/ppermute | solution.py:27
  649.3 19.5 %collective-permute-start.96 = (bf16[2,2,32,512]{3,2,1,0:T(8,128)(2,1)S(1)}, bf16[2,2,32,512]{3,2,1,0:T(8,128)(2,1)}, u32[]{:S(2)}, u32[]{:S(2)}) collective-permute-start(bf16[2,2,32,512]{3,2,1,0:T(8,128)(2,1)S(1)} %get-tuple-element.98), channel_id=1, source_target_pairs={{0,2},{2,0},{1,3},{3,1},{4,6},{6,4},{5,7},{7,5},{8,10},{10,8},{9,1... | collective-permute-start | bytes 393224 | tf_op jit(solution)/shard_map/ppermute | solution.py:27
  (167 other events, 1473.2 us)

commit v2 on v1

--- a/solution.py
+++ b/solution.py
@@ -3,6 +3,8 @@
 import jax
 import jax.numpy as jnp
 from jax import lax
+from jax.experimental import pallas as pl
+from jax.experimental.pallas import tpu as pltpu
 from jax.sharding import Mesh
 from jax.sharding import PartitionSpec as P
 
@@ -14,7 +16,7 @@
 HEAD_BITS = ("zh", "zl", "x", "y")
 T1, T2, D1, D2 = "y", "zl", "zh", "x"
 TP = (T1, T2, "c")
-DP = ("e", D1, D2)
+DP = (D1, D2)
 
 F32, BF16 = jnp.float32, jnp.bfloat16
 
@@ -37,24 +39,11 @@
     return jnp.where(first, jnp.stack([value, other]), jnp.stack([other, value]))
 
 
-def gather_dp(value):
-    out = pair(pair(value, D1), D2)
-    out = jnp.swapaxes(out, 0, 1)
-    return lax.all_gather(out, "e", axis=0)
-
-
 def fold(value, dim, axis):
     index = lax.axis_index(axis)
     kept = pick(value, dim, index)
     sent = pick(value, dim, 1 - index).astype(BF16)
     return kept + swap(sent, axis).astype(F32)
-
-
-def scatter_dp(value):
-    if value.shape[0] > 1:
-        value = lax.psum_scatter(value, "e", scatter_dimension=0, tiled=True)
-    value = value[0]
-    return fold(fold(value, 1, D2), 0, D1)
 
 
 def trade(value, dim, axis):
@@ -118,34 +107,10 @@
     return value.reshape(value.shape[:lead] + (-1,))
 
 
-def split_hidden(value, extra):
-    lead = value.ndim - 1
-    value = value.reshape(value.shape[:-1] + (extra, 2, 2, 2, 2, 2, -1))
-    place = {axis: lead + i for i, axis in enumerate(AXES)}
-    order = [place[a] for a in TP] + list(range(lead)) + [place[a] for a in DP] + [lead + 6]
-    return value.transpose(order)
-
-
-def join_hidden(value):
-    lead = value.ndim - 7
-    names = {a: i for i, a in enumerate(TP)} | {a: 3 + lead + i for i, a in enumerate(DP)}
-    order = [3 + i for i in range(lead)] + [names[a] for a in AXES] + [lead + 6]
-    value = value.transpose(order)
-    return value.reshape(value.shape[:lead] + (-1,))
-
-
-def whole_rows(value):
-    names = {a: i for i, a in enumerate(DP + TP)}
-    order = [names[a] for a in AXES] + list(range(6, value.ndim))
-    value = value.transpose(order)
-    return value.reshape((-1,) + value.shape[7:])
-
-
-def part_rows(value, extra):
-    rows = value.shape[0]
-    value = value.reshape((extra, 2, 2, 2, 2, 2, rows // (32 * extra)) + value.shape[1:])
-    place = {axis: i for i, axis in enumerate(AXES)}
-    return value.transpose([place[a] for a in DP + TP] + list(range(6, value.ndim)))
+def part_rows(value):
+    value = value.reshape((2, 2, 2, 2, 2, value.shape[0] // 32) + value.shape[1:])
+    place = {axis: i for i, axis in enumerate(AXES[1:])}
+    return value.transpose([place[a] for a in DP + TP] + list(range(5, value.ndim)))
 
 
 def own_part(value):
@@ -154,32 +119,214 @@
     return value
 
 
-def gather_proj(block, extra):
-    width = block.shape[1]
-    if extra > 1:
-        whole = lax.all_gather(block, AXES, axis=0, tiled=True)
-        parted = split_heads(whole.T, 1)
-        return own_part(parted).reshape(width, -1).T
-    near = pair(pair(block, D1), D2)
-    near = trade(near, 0, "c")
-    return near.transpose(1, 0, 2, 3).reshape(-1, width)
-
-
-def scatter_proj(value, extra):
+def scatter_proj(value):
     width = value.shape[1]
-    if extra > 1:
-        whole = jnp.zeros((2, 2, 2, 1, 2, HEAD_DIM, width), F32)
-        place = [lax.axis_index(a) for a in TP] + [0, 0, 0, 0]
-        whole = lax.dynamic_update_slice(whole, value.reshape(1, 1, 1, 1, 2, HEAD_DIM, width), place)
-        names = {T1: 0, T2: 1, D2: 2, D1: 4}
-        whole = whole.transpose([names[a] for a in HEAD_BITS] + [3, 5, 6]).reshape(-1, width)
-        return lax.psum_scatter(whole, AXES, scatter_dimension=0, tiled=True)
     value = value.reshape(2, 2, HEAD_DIM // 2, width).transpose(1, 0, 2, 3)
     index = lax.axis_index("c")
     kept = pick(value, 0, index)
     got = swap(pick(value, 0, 1 - index).astype(BF16), "c").astype(F32)
     value = jnp.where(index == 0, jnp.stack([kept, got]), jnp.stack([got, kept]))
     return fold(fold(value, 0, D2), 0, D1)
+
+
+MESH = pl.DeviceIdType.MESH
+NEAR = (("c",), (T1,), (T2,), (T1, "c"), (T2, "c"), (T1, T2), (T1, T2, "c"))
+FAR = ((D1,), (D2,))
+
+
+class Links:
+    def __init__(self, send_sem, recv_sem):
+        self.place = {axis: lax.axis_index(axis) for axis in AXES}
+        self.send_sem, self.recv_sem, self.used = send_sem, recv_sem, 0
+
+    def peer(self, axes):
+        return {axis: 1 - self.place[axis] for axis in axes}
+
+    def meet(self):
+        barrier = pltpu.get_barrier_semaphore()
+        for axes in NEAR + FAR:
+            pl.semaphore_signal(barrier, inc=1, device_id=self.peer(axes), device_id_type=MESH)
+        pl.semaphore_wait(barrier, len(NEAR) + len(FAR))
+
+    def copy(self, source, target, axes):
+        i = self.used
+        self.used += 1
+        return pltpu.make_async_remote_copy(
+            src_ref=source,
+            dst_ref=target,
+            send_sem=self.send_sem.at[i],
+            recv_sem=self.recv_sem.at[i],
+            device_id=self.peer(axes),
+            device_id_type=MESH,
+        )
+
+
+def rank_of(place):
+    return place[T1] * 4 + place[T2] * 2 + place["c"]
+
+
+def block_of(place):
+    index = place["zh"]
+    for axis in AXES[2:]:
+        index = index * 2 + place[axis]
+    return index
+
+
+def flipped(place, axes):
+    return {a: (1 - i if a in axes else i) for a, i in place.items()}
+
+
+def gather_kernel(parts, down, proj, cat_all, down_all, proj_all, send_sem, recv_sem, own_sem):
+    links = Links(send_sem, recv_sem)
+    me = links.place
+    layers = parts.shape[0]
+    own = []
+    for layer in range(layers):
+        own.append(
+            pltpu.make_async_copy(
+                parts.at[layer, rank_of(me)], cat_all.at[layer, block_of(me)], own_sem.at[layer, 0]
+            )
+        )
+        own.append(
+            pltpu.make_async_copy(
+                down.at[layer], down_all.at[layer, me[D2] * 2 + me[D1]], own_sem.at[layer, 1]
+            )
+        )
+    for copy in own:
+        copy.start()
+    links.meet()
+    for layer in range(layers):
+        trades = []
+        for axes in NEAR:
+            trades.append(
+                links.copy(
+                    parts.at[layer, rank_of(flipped(me, axes))],
+                    cat_all.at[layer, block_of(me)],
+                    axes,
+                )
+            )
+        for copy in trades:
+            copy.start()
+        slot = me[D2] * 2 + me[D1]
+        down_first = links.copy(down.at[layer], down_all.at[layer, slot], (D1,))
+        down_first.start()
+        half = proj_all.at[layer, me["zh"], me["c"]]
+        to_core = links.copy(proj.at[layer], half, ("c",))
+        stays = pltpu.make_async_copy(proj.at[layer], half, own_sem.at[layer, 2])
+        mine = me["c"] == me[D2]
+
+        @pl.when(mine)
+        def _():
+            stays.start()
+            stays.wait()
+
+        @pl.when(jnp.logical_not(mine))
+        def _():
+            to_core.start()
+            to_core.wait_send()
+
+        proj_first = links.copy(
+            proj_all.at[layer, me["zh"]], proj_all.at[layer, me["zh"]], (D1,)
+        )
+        proj_second = links.copy(proj_all.at[layer], proj_all.at[layer], (D2,))
+
+        @pl.when(mine)
+        def _():
+            to_core.wait_recv()
+            proj_first.start()
+
+        for copy in trades:
+            copy.wait()
+        own[2 * layer].wait()
+        own[2 * layer + 1].wait()
+        firsts = []
+        for zl in range(2):
+            rows = cat_all.at[layer, pl.ds(me["zh"] * 16 + zl * 8 + me["x"] * 4, 4)]
+            firsts.append(links.copy(rows, rows, (D1,)))
+        for copy in firsts:
+            copy.start()
+        down_first.wait()
+        both = down_all.at[layer, pl.ds(me[D2] * 2, 2)]
+        down_second = links.copy(both, both, (D2,))
+        down_second.start()
+
+        @pl.when(mine)
+        def _():
+            proj_first.wait()
+            proj_second.start()
+            proj_second.wait_send()
+
+        seconds = []
+        for zl in range(2):
+            firsts[zl].wait()
+            for zh in range(2):
+                rows = cat_all.at[layer, pl.ds(zh * 16 + zl * 8 + me["x"] * 4, 4)]
+                copy = links.copy(rows, rows, (D2,))
+                copy.start()
+                seconds.append(copy)
+        for copy in seconds:
+            copy.wait()
+        down_second.wait()
+
+        @pl.when(jnp.logical_not(mine))
+        def _():
+            proj_second.wait_recv()
+
+
+def gather_weights(parts, down, proj):
+    layers, _, rows, columns = parts.shape
+    copies = 32 * layers
+    vmem = pl.BlockSpec(memory_space=pltpu.VMEM)
+    return pl.pallas_call(
+        gather_kernel,
+        out_shape=(
+            jax.ShapeDtypeStruct((layers, 32, rows, columns), BF16),
+            jax.ShapeDtypeStruct((layers, 4) + down.shape[1:], BF16),
+            jax.ShapeDtypeStruct((layers, 2, 2) + proj.shape[1:], BF16),
+        ),
+        in_specs=[vmem] * 3,
+        out_specs=(vmem, vmem, vmem),
+        scratch_shapes=[
+            pltpu.SemaphoreType.DMA((copies,)),
+            pltpu.SemaphoreType.DMA((copies,)),
+            pltpu.SemaphoreType.DMA((layers, 3)),
+        ],
+        compiler_params=pltpu.CompilerParams(
+            collective_id=0, has_side_effects=True, vmem_limit_bytes=48 << 20
+        ),
+    )(parts, down, proj)
+
+
+def refold(block, extra, width):
+    if extra == 1:
+        return block
+    whole = lax.all_gather(block, AXES, axis=1, tiled=True)
+    index = lax.axis_index(AXES[1:])
+    rows = whole.shape[1] // 32
+    return lax.dynamic_slice_in_dim(whole, index * rows, rows, 1)
+
+
+def unfold(block, extra):
+    if extra == 1:
+        return block
+    rows = block.shape[0]
+    whole = jnp.zeros((32 * rows,) + block.shape[1:], F32)
+    whole = lax.dynamic_update_slice_in_dim(whole, block, lax.axis_index(AXES[1:]) * rows, 0)
+    return lax.psum_scatter(whole, AXES, scatter_dimension=0, tiled=True)
+
+
+def join_columns(value):
+    lead = value.ndim - 6
+    names = {a: i for i, a in enumerate(TP)} | {D2: 3 + lead, D1: 4 + lead}
+    order = [3 + i for i in range(lead)] + [names[a] for a in AXES[1:]] + [lead + 5]
+    value = value.transpose(order)
+    return value.reshape(value.shape[:lead] + (-1,))
+
+
+def split_columns(value):
+    value = value.reshape(value.shape[:2] + (2, 2, 2, 2, 2, -1))
+    place = {axis: 2 + i for i, axis in enumerate(AXES[1:])}
+    return value.transpose([0] + [place[a] for a in TP] + [1, place[D2], place[D1], 7])
 
 
 def rotate(vectors, cosine, sine):
@@ -310,23 +457,29 @@
             [small[:, layer, offsets[i] : offsets[i + 1]].reshape(-1) for i in range(6)]
         )
 
+    qkv_mine, up_mine = refold(qkv_weight, extra, width), refold(up_weight, extra, width)
+    proj_mine, down_mine = refold(proj_weight, extra, width), refold(down_weight, extra, width)
+    rows = qkv_mine.shape[1]
+    qkv_parts = jnp.stack([split_heads(qkv_mine[l], 3) for l in range(layers)])
+    parts = jnp.concatenate(
+        [
+            qkv_parts.reshape(layers, 8, rows, -1),
+            split_columns(up_mine).reshape(layers, 8, rows, -1),
+        ],
+        axis=-1,
+    )
+    cat_all, down_all, proj_all = gather_weights(parts, down_mine, proj_mine)
     weights = []
     for layer in range(layers):
         gain, shift, qv, projb, upb, downb = vectors[layer]
-        qkv_parts = split_heads(qkv_weight[layer], 3)
-        qkv_parts = qkv_parts.reshape(qkv_parts.shape[:4] + (-1,))
-        up_parts = split_hidden(up_weight[layer], extra)
-        up_parts = up_parts.reshape(up_parts.shape[:4] + (-1,))
-        qkv_block = trade_tp(qkv_parts)
-        up_block = trade_tp(up_parts)
-        qkv = whole_rows(gather_dp(qkv_block))
-        up = whole_rows(gather_dp(up_block))
-        proj = gather_proj(proj_weight[layer], extra)
-        down = gather_dp(down_weight[layer]).reshape(-1, width)
+        cat = cat_all[layer].reshape(width, -1)
+        qkv, up = cat[:, : 6 * HEAD_DIM], cat[:, 6 * HEAD_DIM :]
+        proj = proj_all[layer].reshape(-1, width)
+        down = down_all[layer].reshape(-1, width)
         q_bias = own_part(split_heads(qv[:width], 1)).reshape(-1)
         v_bias = own_part(split_heads(qv[width:], 1)).reshape(-1)
         bias = jnp.concatenate([q_bias, jnp.zeros_like(q_bias), v_bias])
-        upb = own_part(split_hidden(upb, extra)).reshape(-1)
+        upb = own_part(split_columns(upb[None, None])[0]).reshape(-1)
         weights.append((qkv, bias, proj, up, upb, down))
 
     stream = inputs.astype(F32)
@@ -363,25 +516,25 @@
             - jnp.mean(scaled, axis=-1, keepdims=True)
             - normed * jnp.mean(scaled * normed, axis=-1, keepdims=True)
         )
-        down_own = scatter_dp(down_grad.reshape(extra, 2, 2, -1, width))
-        proj_own = scatter_proj(proj_grad, extra)
-        up_own = trade_tp(scatter_dp(part_rows(up_grad, extra)).astype(BF16))
-        qkv_own = trade_tp(scatter_dp(part_rows(qkv_grad, extra)).astype(BF16))
-        rows = up_own.shape[3]
-        up_own = join_hidden(up_own.reshape(2, 2, 2, rows, extra, 2, 2, -1)).astype(F32)
+        down_grad = down_grad.reshape(2, 2, -1, width)
+        down_own = unfold(fold(fold(down_grad, 0, D2), 0, D1), extra)
+        proj_own = unfold(scatter_proj(proj_grad), extra)
+        cat_grad = part_rows(jnp.concatenate([qkv_grad, up_grad], axis=1))
+        cat_own = trade_tp(fold(fold(cat_grad, 1, D2), 0, D1).astype(BF16))
+        rows = cat_own.shape[3]
+        qkv_own, up_own = cat_own[..., : 6 * HEAD_DIM], cat_own[..., 6 * HEAD_DIM :]
+        up_own = unfold(join_columns(up_own.reshape(2, 2, 2, rows, 2, 2, -1)).astype(F32), extra)
         qkv_own = join_heads(qkv_own.reshape(2, 2, 2, rows, 3, 2, HEAD_DIM)).astype(F32)
+        qkv_own = unfold(qkv_own, extra)
 
         place = [lax.axis_index(a) for a in TP]
         per = qkvbias_grad.shape[0] // 3
         wide = jnp.zeros((2, 2, 2, 2, 2, HEAD_DIM), F32)
         both = jnp.stack([qkvbias_grad[:per], qkvbias_grad[2 * per :]]).reshape(1, 1, 1, 2, 2, HEAD_DIM)
-        qv_full = join_heads(lax.dynamic_update_slice(wide, both, place + [0, 0, 0])[:, :, :, :, :, :])
-        chunk = up_bias.shape[1]
-        wide = jnp.zeros((2, 2, 2, extra, 2, 2, chunk), F32)
-        upb_full = join_hidden(
-            lax.dynamic_update_slice(
-                wide, upbias_grad.reshape(1, 1, 1, extra, 2, 2, chunk), place + [0] * 4
-            )
+        qv_full = join_heads(lax.dynamic_update_slice(wide, both, place + [0, 0, 0]))
+        wide = jnp.zeros((2, 2, 2, 2, 2, upbias_grad.shape[0] // 4), F32)
+        upb_full = join_columns(
+            lax.dynamic_update_slice(wide, upbias_grad.reshape(1, 1, 1, 2, 2, -1), place + [0] * 3)
         )
         small_grad = jnp.concatenate(
             [

time: 706 us -> 680 us (0.963)
  Pallas kernels: 0 us -> 108 us
  waiting for transfers between devices: 277 us -> 207 us
  starting transfers between devices: 107 us -> 60.2 us
  local copies, waits for them, and re-layouts: 158 us -> 138 us
  matrix products: 74.1 us -> 93.5 us
  other arithmetic: 80.2 us -> 64.7 us
    pallas_call x0 -> x1, Pallas kernels: none -> 108 us  [gather_weights(): pl.pallas_call(gather_kernel, out_shape=(jax.ShapeDtypeStruct((layers, 32...]
    ppermute x106 -> x66, waiting for transfers between devices: 277 us -> 207 us  [swap(): return lax.ppermute(value, tuple(sorted(axes, key=AXES.index)), pairs)]
    ppermute x106 -> x66, starting transfers between devices: 107 us -> 60.2 us  [swap(): return lax.ppermute(value, tuple(sorted(axes, key=AXES.index)), pairs)]
    dot_general x24, matrix products: 58.7 us -> 77 us  [dot(): lax.dot_general(a, b, (contract, ((), ())), preferred_element_type=F32)]
    another operation x23 -> x11, local copies, waits for them, and re-layouts: 12.6 us -> 1.31 us  [the longest x8 6.19 us: trade(): jnp.stack([kept, got], dim)]
    concatenate x0 -> x2, local copies, waits for them, and re-layouts: none -> 10.4 us  [shards(): cat_grad = part_rows(jnp.concatenate([qkv_grad, up_grad], axis=1))]
    dot_general x2 -> x0, local copies, waits for them, and re-layouts: 9.87 us -> none  [dot(): lax.dot_general(a, b, (contract, ((), ())), preferred_element_type=F32)]
    another operation x10, other arithmetic: 8.36 us -> 15.6 us  [gather_rows(): return jnp.stack([near, swap(near, 'c')], 1)]
  transfers between devices with their start and end apart: 106 -> 66, of which waited for: 51 -> 36; matrix products, arithmetic and copies ran while one was open for 29% -> 22% of each run, Pallas kernels for 0% -> 16%
where the time goes in v2:
time: 680 us; the launch traced here: 674 us
  waiting for transfers between devices  207 us (30%)
  local copies, waits for them, and re-layouts  138 us (20%)
  Pallas kernels  108 us (16%)
  matrix products  93.5 us (14%)
  other arithmetic  64.7 us (10%)
  starting transfers between devices  60.2 us (9%)
    ppermute x66, waiting for transfers between devices, swap(): return lax.ppermute(value, tuple(sorted(axes, key=AXES.index)), pairs)  207 us
    pallas_call x1, Pallas kernels, gather_weights(): pl.pallas_call(gather_kernel, out_shape=(jax.ShapeDtypeStruct((layers, 32...  108 us
    dot_general x24, matrix products, dot(): lax.dot_general(a, b, (contract, ((), ())), preferred_element_type=F32)  77 us
    ppermute x66, starting transfers between devices, swap(): return lax.ppermute(value, tuple(sorted(axes, key=AXES.index)), pairs)  60.2 us
    unnamed x258, local copies, waits for them, and re-layouts  35.7 us
    another operation x10, other arithmetic, gather_rows(): return jnp.stack([near, swap(near, 'c')], 1)  15.6 us
  transfers between devices with their start and end apart: 66, of which 36 were waited for; matrix products, arithmetic and copies ran while one was open for 22% of the time, Pallas kernels for 16%

profile of v2, /device:TPU:0, one launch (start us, length us, event | category | flops | bytes accessed | tf_op | source)
XLA Modules:
  0.0 674.1 jit_solution(6510690235715288127)
XLA Ops:
  2.7 3.0 collective-permute-start.10
  12.4 108.0 %shard_map.232 = (bf16[2,32,32,896]{3,2,1,0:T(8,128)(2,1)}, bf16[2,4,128,1024]{3,2,1,0:T(8,128)(2,1)S(1)}, bf16[2,2,2,32,1024]{4,3,2,1,0:T(8,128)(2,1)S(1)}) custom-call(bf16[2,8,32,896]{3,2,1,0:T(8,128)(2,1)S(1)} %pad_maximum_fusion.11.parts, bf16[2,128,1024]{2,1,0:T(8,128)(2,1)S(1)} %copy-done, bf16[2,32,1024]{2,1,0:T(8,128)(2,1)S(1)} %copy-done.1), custom_call_target="tpu_custom_call" | custom-call | tf_op jit(solution)/shard_map/pallas_call | solution.py:280
  120.4 4.1 fusion.178
  127.9 4.7 collective-permute-start.1
  134.3 3.6 collective-permute-done.2
  138.2 3.4 collective-permute-done.3
  143.0 3.7 collective-permute-done.4
  152.0 5.6 collective-permute-done.6
  159.0 2.8 collective-permute-done.7
  175.2 2.9 convolution_add_fusion.7
  178.2 4.4 reshape.767
  184.6 3.3 fusion.177
  189.3 3.6 copy.430
  205.0 5.5 fusion.20
  213.8 3.3 collective-permute-done.13
  220.1 2.9 collective-permute-start.16
  228.2 3.5 collective-permute-done.14
  232.0 9.5 %collective-permute-done.16 = bf16[2,96,1024]{2,1,0:T(8,128)(2,1)} collective-permute-done((bf16[2,96,1024]{2,1,0:T(8,128)(2,1)S(1)}, bf16[2,96,1024]{2,1,0:T(8,128)(2,1)}, u32[]{:S(2)}, u32[]{:S(2)}) %collective-permute-start.16) | collective-permute-done | bytes 393248 | tf_op jit(solution)/shard_map/ppermute | solution.py:29
  241.5 10.4 %collective-permute-done.15 = bf16[2,96,1024]{2,1,0:T(8,128)(2,1)} collective-permute-done((bf16[2,96,1024]{2,1,0:T(8,128)(2,1)S(1)}, bf16[2,96,1024]{2,1,0:T(8,128)(2,1)}, u32[]{:S(2)}, u32[]{:S(2)}) %collective-permute-start.15) | collective-permute-done | bytes 393248 | tf_op jit(solution)/shard_map/ppermute | solution.py:29
  254.8 2.9 collective-permute-start.19
  263.6 12.1 %collective-permute-done.18 = bf16[2,96,1024]{2,1,0:T(8,128)(2,1)S(1)} collective-permute-done((bf16[2,96,1024]{2,1,0:T(8,128)(2,1)S(1)}, bf16[2,96,1024]{2,1,0:T(8,128)(2,1)S(1)}, u32[]{:S(2)}, u32[]{:S(2)}) %collective-permute-start.18) | collective-permute-done | bytes 393248 | tf_op jit(solution)/shard_map/ppermute | solution.py:29
  286.4 2.9 copy.362
  293.2 4.4 convolution_add_fusion.6
  297.6 5.9 reshape.768
  303.4 2.9 slice.455
  306.4 3.4 fusion.176
  309.8 3.4 copy.435
  323.8 3.0 convolution_bitcast_fusion.1
  330.5 3.3 fusion.21
  333.9 3.8 convert_reduce_fusion
  337.7 4.1 fusion.27
  341.8 3.2 fusion.194
  345.0 4.6 fusion.46
  359.8 3.8 fusion.193
  363.6 3.1 fusion.190
  369.1 5.4 copy.393
  377.6 4.0 convolution_add_fusion
  381.6 3.6 convolution_add_fusion.3
  393.5 9.9 %collective-permute-done.60 = bf16[2,32,1024]{2,1,0:T(8,128)(2,1)S(1)} collective-permute-done((bf16[2,32,1024]{2,1,0:T(8,128)(2,1)S(1)}, bf16[2,32,1024]{2,1,0:T(8,128)(2,1)S(1)}, u32[]{:S(2)}, u32[]{:S(2)}) %collective-permute-start.60) | collective-permute-done | bytes 131104 | tf_op jit(solution)/shard_map/ppermute | solution.py:29
  406.0 3.5 fusion.168
  415.5 15.9 %collective-permute-done.30 = bf16[2,96,1024]{2,1,0:T(8,128)(2,1)S(1)} collective-permute-done((bf16[2,96,1024]{2,1,0:T(8,128)(2,1)S(1)}, bf16[2,96,1024]{2,1,0:T(8,128)(2,1)S(1)}, u32[]{:S(2)}, u32[]{:S(2)}) %collective-permute-start.30) | collective-permute-done | bytes 393248 | tf_op jit(solution)/shard_map/ppermute | solution.py:29
  431.4 9.3 %collective-permute-done.32 = bf16[2,96,1024]{2,1,0:T(8,128)(2,1)S(1)} collective-permute-done((bf16[2,96,1024]{2,1,0:T(8,128)(2,1)S(1)}, bf16[2,96,1024]{2,1,0:T(8,128)(2,1)S(1)}, u32[]{:S(2)}, u32[]{:S(2)}) %collective-permute-start.32) | collective-permute-done | bytes 393248 | tf_op jit(solution)/shard_map/ppermute | solution.py:29
  441.9 6.4 collective-permute-done.22
  448.3 7.3 %collective-permute-done.24 = bf16[2,96,1024]{2,1,0:T(8,128)(2,1)S(1)} collective-permute-done((bf16[2,96,1024]{2,1,0:T(8,128)(2,1)S(1)}, bf16[2,96,1024]{2,1,0:T(8,128)(2,1)S(1)}, u32[]{:S(2)}, u32[]{:S(2)}) %collective-permute-start.24) | collective-permute-done | bytes 393248 | tf_op jit(solution)/shard_map/ppermute | solution.py:29
  464.2 8.2 %collective-permute-done.35 = bf16[2,96,1024]{2,1,0:T(8,128)(2,1)S(1)} collective-permute-done((bf16[2,96,1024]{2,1,0:T(8,128)(2,1)S(1)}, bf16[2,96,1024]{2,1,0:T(8,128)(2,1)S(1)}, u32[]{:S(2)}, u32[]{:S(2)}) %collective-permute-start.35) | collective-permute-done | bytes 393248 | tf_op jit(solution)/shard_map/ppermute | solution.py:29
  472.4 3.2 collective-permute-done.34
  484.5 6.7 collective-permute-done.54
  492.1 2.9 collective-permute-start.55
  514.2 4.5 convert_reduce_fusion.2
  528.4 3.1 fusion.192
  531.5 4.5 fusion.49
  542.5 2.9 convert_element_type.542
  545.3 3.8 fusion.191
  551.6 5.0 copy.387
  561.1 4.9 convolution_add_fusion.2
  571.2 13.6 %collective-permute-done.57 = bf16[2,32,1024]{2,1,0:T(8,128)(2,1)S(1)} collective-permute-done((bf16[2,32,1024]{2,1,0:T(8,128)(2,1)S(1)}, bf16[2,32,1024]{2,1,0:T(8,128)(2,1)S(1)}, u32[]{:S(2)}, u32[]{:S(2)}) %collective-permute-start.57) | collective-permute-done | bytes 131104 | tf_op jit(solution)/shard_map/ppermute | solution.py:29
  591.4 21.4 %collective-permute-done.63 = bf16[128,1024]{1,0:T(8,128)(2,1)S(1)} collective-permute-done((bf16[128,1024]{1,0:T(8,128)(2,1)S(1)}, bf16[128,1024]{1,0:T(8,128)(2,1)S(1)}, u32[]{:S(2)}, u32[]{:S(2)}) %collective-permute-start.63) | collective-permute-done | bytes 262176 | tf_op jit(solution)/shard_map/ppermute | solution.py:29
  612.8 8.4 %collective-permute-done.47 = bf16[2,2,2,32,896]{4,3,2,0,1:T(8,128)(2,1)S(1)} collective-permute-done((bf16[2,2,2,32,896]{4,3,2,0,1:T(8,128)(2,1)S(1)}, bf16[2,2,2,32,896]{4,3,2,0,1:T(8,128)(2,1)S(1)}, u32[]{:S(2)}, u32[]{:S(2)}) %collective-permute-start.47) | collective-permute-done | bytes 458784 | tf_op jit(solution)/shard_map/ppermute | solution.py:29
  624.0 3.1 collective-permute-start.40
  629.6 6.3 collective-permute-done.38
  635.9 9.5 %collective-permute-done.40 = bf16[2,96,1024]{2,1,0:T(8,128)(2,1)S(1)} collective-permute-done((bf16[2,96,1024]{2,1,0:T(8,128)(2,1)S(1)}, bf16[2,96,1024]{2,1,0:T(8,128)(2,1)S(1)}, u32[]{:S(2)}, u32[]{:S(2)}) %collective-permute-start.40) | collective-permute-done | bytes 393248 | tf_op jit(solution)/shard_map/ppermute | solution.py:29
  650.6 3.4 collective-permute-done.41
  654.8 3.1 collective-permute-done.42
  662.3 3.1 collective-permute-done.44
  (618 shorter events, 229.4 us)
Async XLA Ops:
  2.7 162.4 %collective-permute-start.10 = (s32[2,97]{1,0:T(2,128)}, s32[2,97]{1,0:T(2,128)S(1)}, u32[]{:S(2)}, u32[]{:S(2)}) collective-permute-start(s32[2,97]{1,0:T(2,128)} %pad_add_fusion.2), channel_id=1, source_target_pairs={{0,2},{2,0},{1,3},{3,1},{4,6},{6,4},{5,7},{7,5},{8,10},{10,8},{9,1... | collective-permute-start | bytes 2336 | tf_op jit(solution)/shard_map/ppermute | solution.py:29
  5.7 159.4 %collective-permute-start.9 = (s32[2,97]{1,0:T(2,128)}, s32[2,97]{1,0:T(2,128)}, u32[]{:S(2)}, u32[]{:S(2)}) collective-permute-start(s32[2,97]{1,0:T(2,128)} %pad_add_fusion.2), channel_id=1, source_target_pairs={{0,8},{8,0},{1,9},{9,1},{2,10},{10,2},{3,11},{11,3},{4,12},{12,4},... | collective-permute-start | bytes 2336 | tf_op jit(solution)/shard_map/ppermute | solution.py:29
  8.2 119.7 %collective-permute-start = (bf16[640]{0:T(1024)(128)(2,1)S(1)}, bf16[640]{0:T(1024)(128)(2,1)S(1)}, u32[]{:S(2)}, u32[]{:S(2)}) collective-permute-start(bf16[640]{0:T(1024)(128)(2,1)S(1)} %reshape.731), channel_id=1, source_target_pairs={{0,1},{1,0},{2,3},{3,2},{4,5},{5,4},{6,7},{7,6},{8,9},{9,8},{10,11... | collective-permute-start | bytes 3848 | tf_op jit(solution)/shard_map/ppermute | solution.py:29
  127.9 6.2 collective-permute-start.1
  134.2 3.7 collective-permute-start.2
  137.9 3.7 collective-permute-start.3
  141.6 5.0 collective-permute-start.4
  148.1 9.5 %collective-permute-start.6 = (bf16[2,96,1024]{2,1,0:T(8,128)(2,1)S(1)}, bf16[2,96,1024]{2,1,0:T(8,128)(2,1)S(1)}, u32[]{:S(2)}, u32[]{:S(2)}) collective-permute-start(bf16[2,96,1024]{2,1,0:T(8,128)(2,1)S(1)} %fusion.57), channel_id=1, source_target_pairs={{0,2},{2,0},{1,3},{3,1},{4,6},{6,4},{5,7},{7,5},{8,10},{10,8},{9,1... | collective-permute-start | bytes 1179656 | tf_op jit(solution)/shard_map/ppermute | solution.py:29
  150.0 8.9 %collective-permute-start.5 = (bf16[2,96,1024]{2,1,0:T(8,128)(2,1)S(1)}, bf16[2,96,1024]{2,1,0:T(8,128)(2,1)S(1)}, u32[]{:S(2)}, u32[]{:S(2)}) collective-permute-start(bf16[2,96,1024]{2,1,0:T(8,128)(2,1)S(1)} %fusion.57), channel_id=1, source_target_pairs={{0,8},{8,0},{1,9},{9,1},{2,10},{10,2},{3,11},{11,3},{4,12},{12,4},... | collective-permute-start | bytes 1179656 | tf_op jit(solution)/shard_map/ppermute | solution.py:29
  150.2 11.6 %collective-permute-start.7 = (bf16[2,96,1024]{2,1,0:T(8,128)(2,1)S(1)}, bf16[2,96,1024]{2,1,0:T(8,128)(2,1)S(1)}, u32[]{:S(2)}, u32[]{:S(2)}) collective-permute-start(bf16[2,96,1024]{2,1,0:T(8,128)(2,1)S(1)} %fusion.57), channel_id=1, source_target_pairs={{0,10},{2,8},{8,2},{10,0},{1,11},{3,9},{9,3},{11,1},{4,14},{6,12},... | collective-permute-start | bytes 1179656 | tf_op jit(solution)/shard_map/ppermute | solution.py:29
  157.6 7.5 %collective-permute-start.11 = (s32[2,97]{1,0:T(2,128)}, s32[2,97]{1,0:T(2,128)S(1)}, u32[]{:S(2)}, u32[]{:S(2)}) collective-permute-start(s32[2,97]{1,0:T(2,128)} %pad_add_fusion.2), channel_id=1, source_target_pairs={{0,10},{2,8},{8,2},{10,0},{1,11},{3,9},{9,3},{11,1},{4,14},{6,12},... | collective-permute-start | bytes 2336 | tf_op jit(solution)/shard_map/ppermute | solution.py:29
  165.0 6.9 %collective-permute-start.8 = (bf16[4,2,96,1024]{3,2,1,0:T(8,128)(2,1)}, bf16[4,2,96,1024]{3,2,1,0:T(8,128)(2,1)}, u32[]{:S(2)}, u32[]{:S(2)}) collective-permute-start(bf16[4,2,96,1024]{3,2,1,0:T(8,128)(2,1)} %get-tuple-element.79), channel_id=1, source_target_pairs={{0,1},{1,0},{2,3},{3,2},{4,5},{5,4},{6,7},{7,6},{8,9},{9,8},{10,11... | collective-permute-start | bytes 4718600 | tf_op jit(solution)/shard_map/ppermute | solution.py:29
  213.6 3.5 collective-permute-start.13
  219.7 12.0 %collective-permute-start.14 = (bf16[2,96,1024]{2,1,0:T(8,128)(2,1)S(1)}, bf16[2,96,1024]{2,1,0:T(8,128)(2,1)S(1)}, u32[]{:S(2)}, u32[]{:S(2)}) collective-permute-start(bf16[2,96,1024]{2,1,0:T(8,128)(2,1)S(1)} %get-tuple-element.75), channel_id=1, source_target_pairs={{0,8},{8,0},{1,9},{9,1},{2,10},{10,2},{3,11},{11,3},{4,12},{12,4},... | collective-permute-start | bytes 1179656 | tf_op jit(solution)/shard_map/ppermute | solution.py:29
  220.1 21.4 %collective-permute-start.16 = (bf16[2,96,1024]{2,1,0:T(8,128)(2,1)S(1)}, bf16[2,96,1024]{2,1,0:T(8,128)(2,1)}, u32[]{:S(2)}, u32[]{:S(2)}) collective-permute-start(bf16[2,96,1024]{2,1,0:T(8,128)(2,1)S(1)} %get-tuple-element.76), channel_id=1, source_target_pairs={{0,10},{2,8},{8,2},{10,0},{1,11},{3,9},{9,3},{11,1},{4,14},{6,12},... | collective-permute-start | bytes 1179656 | tf_op jit(solution)/shard_map/ppermute | solution.py:29
  222.9 29.0 %collective-permute-start.15 = (bf16[2,96,1024]{2,1,0:T(8,128)(2,1)S(1)}, bf16[2,96,1024]{2,1,0:T(8,128)(2,1)}, u32[]{:S(2)}, u32[]{:S(2)}) collective-permute-start(bf16[2,96,1024]{2,1,0:T(8,128)(2,1)S(1)} %get-tuple-element.77), channel_id=1, source_target_pairs={{0,2},{2,0},{1,3},{3,1},{4,6},{6,4},{5,7},{7,5},{8,10},{10,8},{9,1... | collective-permute-start | bytes 1179656 | tf_op jit(solution)/shard_map/ppermute | solution.py:29
  224.1 30.7 %collective-permute-start.27 = (bf16[2,96,1024]{2,1,0:T(8,128)(2,1)S(1)}, bf16[2,96,1024]{2,1,0:T(8,128)(2,1)S(1)}, u32[]{:S(2)}, u32[]{:S(2)}) collective-permute-start(bf16[2,96,1024]{2,1,0:T(8,128)(2,1)S(1)} %get-tuple-element.33), channel_id=1, source_target_pairs={{0,10},{2,8},{8,2},{10,0},{1,11},{3,9},{9,3},{11,1},{4,14},{6,12},... | collective-permute-start | bytes 1179656 | tf_op jit(solution)/shard_map/ppermute | solution.py:29
  225.5 34.8 %collective-permute-start.26 = (bf16[2,96,1024]{2,1,0:T(8,128)(2,1)S(1)}, bf16[2,96,1024]{2,1,0:T(8,128)(2,1)S(1)}, u32[]{:S(2)}, u32[]{:S(2)}) collective-permute-start(bf16[2,96,1024]{2,1,0:T(8,128)(2,1)S(1)} %get-tuple-element.33), channel_id=1, source_target_pairs={{0,2},{2,0},{1,3},{3,1},{4,6},{6,4},{5,7},{7,5},{8,10},{10,8},{9,1... | collective-permute-start | bytes 1179656 | tf_op jit(solution)/shard_map/ppermute | solution.py:29
  231.7 28.5 %collective-permute-start.25 = (bf16[2,96,1024]{2,1,0:T(8,128)(2,1)S(1)}, bf16[2,96,1024]{2,1,0:T(8,128)(2,1)S(1)}, u32[]{:S(2)}, u32[]{:S(2)}) collective-permute-start(bf16[2,96,1024]{2,1,0:T(8,128)(2,1)S(1)} %get-tuple-element.33), channel_id=1, source_target_pairs={{0,8},{8,0},{1,9},{9,1},{2,10},{10,2},{3,11},{11,3},{4,12},{12,4},... | collective-permute-start | bytes 1179656 | tf_op jit(solution)/shard_map/ppermute | solution.py:29
  254.1 21.5 %collective-permute-start.18 = (bf16[2,96,1024]{2,1,0:T(8,128)(2,1)S(1)}, bf16[2,96,1024]{2,1,0:T(8,128)(2,1)S(1)}, u32[]{:S(2)}, u32[]{:S(2)}) collective-permute-start(bf16[2,96,1024]{2,1,0:T(8,128)(2,1)S(1)} %add_convert_fusion), channel_id=1, source_target_pairs={{0,2},{2,0},{1,3},{3,1},{4,6},{6,4},{5,7},{7,5},{8,10},{10,8},{9,1... | collective-permute-start | bytes 1179656 | tf_op jit(solution)/shard_map/ppermute | solution.py:29
  254.5 21.1 %collective-permute-start.17 = (bf16[2,96,1024]{2,1,0:T(8,128)(2,1)S(1)}, bf16[2,96,1024]{2,1,0:T(8,128)(2,1)S(1)}, u32[]{:S(2)}, u32[]{:S(2)}) collective-permute-start(bf16[2,96,1024]{2,1,0:T(8,128)(2,1)S(1)} %add_convert_fusion), channel_id=1, source_target_pairs={{0,8},{8,0},{1,9},{9,1},{2,10},{10,2},{3,11},{11,3},{4,12},{12,4},... | collective-permute-start | bytes 1179656 | tf_op jit(solution)/shard_map/ppermute | solution.py:29
  254.8 20.9 %collective-permute-start.19 = (bf16[2,96,1024]{2,1,0:T(8,128)(2,1)S(1)}, bf16[2,96,1024]{2,1,0:T(8,128)(2,1)S(1)}, u32[]{:S(2)}, u32[]{:S(2)}) collective-permute-start(bf16[2,96,1024]{2,1,0:T(8,128)(2,1)S(1)} %add_convert_fusion), channel_id=1, source_target_pairs={{0,10},{2,8},{8,2},{10,0},{1,11},{3,9},{9,3},{11,1},{4,14},{6,12},... | collective-permute-start | bytes 1179656 | tf_op jit(solution)/shard_map/ppermute | solution.py:29
  263.4 16.8 %collective-permute-start.28 = (bf16[4,2,96,1024]{3,2,1,0:T(8,128)(2,1)}, bf16[4,2,96,1024]{3,2,1,0:T(8,128)(2,1)}, u32[]{:S(2)}, u32[]{:S(2)}) collective-permute-start(bf16[4,2,96,1024]{3,2,1,0:T(8,128)(2,1)} %get-tuple-element.69), channel_id=1, source_target_pairs={{0,1},{1,0},{2,3},{3,2},{4,5},{5,4},{6,7},{7,6},{8,9},{9,8},{10,11... | collective-permute-start | bytes 4718600 | tf_op jit(solution)/shard_map/ppermute | solution.py:29
  277.6 11.7 %collective-permute-start.20 = (bf16[4,2,96,1024]{3,2,1,0:T(8,128)(2,1)}, bf16[4,2,96,1024]{3,2,1,0:T(8,128)(2,1)}, u32[]{:S(2)}, u32[]{:S(2)}) collective-permute-start(bf16[4,2,96,1024]{3,2,1,0:T(8,128)(2,1)} %get-tuple-element.74), channel_id=1, source_target_pairs={{0,1},{1,0},{2,3},{3,2},{4,5},{5,4},{6,7},{7,6},{8,9},{9,8},{10,11... | collective-permute-start | bytes 4718600 | tf_op jit(solution)/shard_map/ppermute | solution.py:29
  353.8 35.2 %collective-permute-start.59 = (bf16[2,32,1024]{2,1,0:T(8,128)(2,1)}, bf16[2,32,1024]{2,1,0:T(8,128)(2,1)S(1)}, u32[]{:S(2)}, u32[]{:S(2)}) collective-permute-start(bf16[2,32,1024]{2,1,0:T(8,128)(2,1)} %fusion.110), channel_id=1, source_target_pairs={{0,1},{1,0},{2,3},{3,2},{4,5},{5,4},{6,7},{7,6},{8,9},{9,8},{10,11... | collective-permute-start | bytes 393224 | tf_op jit(solution)/shard_map/ppermute | solution.py:29
  377.2 26.2 %collective-permute-start.51 = (bf16[2,2,2,2,32,896]{5,4,3,1,2,0:T(8,128)(2,1)}, bf16[2,2,2,2,32,896]{5,4,3,1,2,0:T(8,128)(2,1)}, u32[]{:S(2)}, u32[]{:S(2)}) collective-permute-start(bf16[2,2,2,2,32,896]{5,4,3,1,2,0:T(8,128)(2,1)} %fusion.53), channel_id=1, source_target_pairs={{0,4},{4,0},{1,5},{5,1},{2,6},{6,2},{3,7},{7,3},{8,12},{12,8},{9,1... | collective-permute-start | bytes 2752520 | tf_op jit(solution)/shard_map/ppermute | solution.py:29
  386.9 19.1 %collective-permute-start.29 = (bf16[4,2,96,1024]{3,2,1,0:T(8,128)(2,1)}, bf16[4,2,96,1024]{3,2,1,0:T(8,128)(2,1)}, u32[]{:S(2)}, u32[]{:S(2)}) collective-permute-start(bf16[4,2,96,1024]{3,2,1,0:T(8,128)(2,1)} %fusion.30), channel_id=1, source_target_pairs={{0,1},{1,0},{2,3},{3,2},{4,5},{5,4},{6,7},{7,6},{8,9},{9,8},{10,11... | collective-permute-start | bytes 4718600 | tf_op jit(solution)/shard_map/ppermute | solution.py:29
  388.9 23.7 %collective-permute-start.21 = (bf16[4,2,96,1024]{3,2,1,0:T(8,128)(2,1)}, bf16[4,2,96,1024]{3,2,1,0:T(8,128)(2,1)}, u32[]{:S(2)}, u32[]{:S(2)}) collective-permute-start(bf16[4,2,96,1024]{3,2,1,0:T(8,128)(2,1)} %fusion.29), channel_id=1, source_target_pairs={{0,1},{1,0},{2,3},{3,2},{4,5},{5,4},{6,7},{7,6},{8,9},{9,8},{10,11... | collective-permute-start | bytes 4718600 | tf_op jit(solution)/shard_map/ppermute | solution.py:29
  389.2 14.2 %collective-permute-start.60 = (bf16[2,32,1024]{2,1,0:T(8,128)(2,1)S(1)}, bf16[2,32,1024]{2,1,0:T(8,128)(2,1)S(1)}, u32[]{:S(2)}, u32[]{:S(2)}) collective-permute-start(bf16[2,32,1024]{2,1,0:T(8,128)(2,1)S(1)} %fusion.109), channel_id=1, source_target_pairs={{0,4},{4,0},{1,5},{5,1},{2,6},{6,2},{3,7},{7,3},{8,12},{12,8},{9,1... | collective-permute-start | bytes 393224 | tf_op jit(solution)/shard_map/ppermute | solution.py:29
  392.8 84.4 %collective-permute-start.64 = (bf16[2,128,1024]{2,1,0:T(8,128)(2,1)}, bf16[2,128,1024]{2,1,0:T(8,128)(2,1)}, u32[]{:S(2)}, u32[]{:S(2)}) collective-permute-start(bf16[2,128,1024]{2,1,0:T(8,128)(2,1)} %fusion.86), channel_id=1, source_target_pairs={{0,4},{4,0},{1,5},{5,1},{2,6},{6,2},{3,7},{7,3},{8,12},{12,8},{9,1... | collective-permute-start | bytes 1572872 | tf_op jit(solution)/shard_map/ppermute | solution.py:29
  405.5 56.2 %collective-permute-start.52 = (bf16[2,2,2,32,896]{4,3,2,0,1:T(8,128)(2,1)S(1)}, bf16[2,2,2,32,896]{4,3,2,0,1:T(8,128)(2,1)S(1)}, u32[]{:S(2)}, u32[]{:S(2)}) collective-permute-start(bf16[2,2,2,32,896]{4,3,2,0,1:T(8,128)(2,1)S(1)} %fusion.96), channel_id=1, source_target_pairs={{0,16},{16,0},{1,17},{17,1},{2,18},{18,2},{3,19},{19,3},{4,20},{20... | collective-permute-start | bytes 1376264 | tf_op jit(solution)/shard_map/ppermute | solution.py:29
  409.6 21.8 %collective-permute-start.30 = (bf16[2,96,1024]{2,1,0:T(8,128)(2,1)S(1)}, bf16[2,96,1024]{2,1,0:T(8,128)(2,1)S(1)}, u32[]{:S(2)}, u32[]{:S(2)}) collective-permute-start(bf16[2,96,1024]{2,1,0:T(8,128)(2,1)S(1)} %get-tuple-element.65), channel_id=1, source_target_pairs={{0,8},{8,0},{1,9},{9,1},{2,10},{10,2},{3,11},{11,3},{4,12},{12,4},... | collective-permute-start | bytes 1179656 | tf_op jit(solution)/shard_map/ppermute | solution.py:29
  411.0 29.7 %collective-permute-start.32 = (bf16[2,96,1024]{2,1,0:T(8,128)(2,1)S(1)}, bf16[2,96,1024]{2,1,0:T(8,128)(2,1)S(1)}, u32[]{:S(2)}, u32[]{:S(2)}) collective-permute-start(bf16[2,96,1024]{2,1,0:T(8,128)(2,1)S(1)} %get-tuple-element.66), channel_id=1, source_target_pairs={{0,10},{2,8},{8,2},{10,0},{1,11},{3,9},{9,3},{11,1},{4,14},{6,12},... | collective-permute-start | bytes 1179656 | tf_op jit(solution)/shard_map/ppermute | solution.py:29
  412.5 28.2 %collective-permute-start.31 = (bf16[2,96,1024]{2,1,0:T(8,128)(2,1)S(1)}, bf16[2,96,1024]{2,1,0:T(8,128)(2,1)S(1)}, u32[]{:S(2)}, u32[]{:S(2)}) collective-permute-start(bf16[2,96,1024]{2,1,0:T(8,128)(2,1)S(1)} %get-tuple-element.67), channel_id=1, source_target_pairs={{0,2},{2,0},{1,3},{3,1},{4,6},{6,4},{5,7},{7,5},{8,10},{10,8},{9,1... | collective-permute-start | bytes 1179656 | tf_op jit(solution)/shard_map/ppermute | solution.py:29
  431.4 16.9 %collective-permute-start.22 = (bf16[2,96,1024]{2,1,0:T(8,128)(2,1)S(1)}, bf16[2,96,1024]{2,1,0:T(8,128)(2,1)S(1)}, u32[]{:S(2)}, u32[]{:S(2)}) collective-permute-start(bf16[2,96,1024]{2,1,0:T(8,128)(2,1)S(1)} %get-tuple-element.70), channel_id=1, source_target_pairs={{0,8},{8,0},{1,9},{9,1},{2,10},{10,2},{3,11},{11,3},{4,12},{12,4},... | collective-permute-start | bytes 1179656 | tf_op jit(solution)/shard_map/ppermute | solution.py:29
  440.7 14.9 %collective-permute-start.24 = (bf16[2,96,1024]{2,1,0:T(8,128)(2,1)S(1)}, bf16[2,96,1024]{2,1,0:T(8,128)(2,1)S(1)}, u32[]{:S(2)}, u32[]{:S(2)}) collective-permute-start(bf16[2,96,1024]{2,1,0:T(8,128)(2,1)S(1)} %get-tuple-element.71), channel_id=1, source_target_pairs={{0,10},{2,8},{8,2},{10,0},{1,11},{3,9},{9,3},{11,1},{4,14},{6,12},... | collective-permute-start | bytes 1179656 | tf_op jit(solution)/shard_map/ppermute | solution.py:29
  440.7 16.2 %collective-permute-start.23 = (bf16[2,96,1024]{2,1,0:T(8,128)(2,1)S(1)}, bf16[2,96,1024]{2,1,0:T(8,128)(2,1)S(1)}, u32[]{:S(2)}, u32[]{:S(2)}) collective-permute-start(bf16[2,96,1024]{2,1,0:T(8,128)(2,1)S(1)} %get-tuple-element.72), channel_id=1, source_target_pairs={{0,2},{2,0},{1,3},{3,1},{4,6},{6,4},{5,7},{7,5},{8,10},{10,8},{9,1... | collective-permute-start | bytes 1179656 | tf_op jit(solution)/shard_map/ppermute | solution.py:29
  458.2 14.2 %collective-permute-start.35 = (bf16[2,96,1024]{2,1,0:T(8,128)(2,1)S(1)}, bf16[2,96,1024]{2,1,0:T(8,128)(2,1)S(1)}, u32[]{:S(2)}, u32[]{:S(2)}) collective-permute-start(bf16[2,96,1024]{2,1,0:T(8,128)(2,1)S(1)} %get-tuple-element.37), channel_id=1, source_target_pairs={{0,10},{2,8},{8,2},{10,0},{1,11},{3,9},{9,3},{11,1},{4,14},{6,12},... | collective-permute-start | bytes 1179656 | tf_op jit(solution)/shard_map/ppermute | solution.py:29
  460.0 15.6 %collective-permute-start.34 = (bf16[2,96,1024]{2,1,0:T(8,128)(2,1)S(1)}, bf16[2,96,1024]{2,1,0:T(8,128)(2,1)S(1)}, u32[]{:S(2)}, u32[]{:S(2)}) collective-permute-start(bf16[2,96,1024]{2,1,0:T(8,128)(2,1)S(1)} %get-tuple-element.37), channel_id=1, source_target_pairs={{0,2},{2,0},{1,3},{3,1},{4,6},{6,4},{5,7},{7,5},{8,10},{10,8},{9,1... | collective-permute-start | bytes 1179656 | tf_op jit(solution)/shard_map/ppermute | solution.py:29
  460.7 15.1 %collective-permute-start.33 = (bf16[2,96,1024]{2,1,0:T(8,128)(2,1)S(1)}, bf16[2,96,1024]{2,1,0:T(8,128)(2,1)S(1)}, u32[]{:S(2)}, u32[]{:S(2)}) collective-permute-start(bf16[2,96,1024]{2,1,0:T(8,128)(2,1)S(1)} %get-tuple-element.37), channel_id=1, source_target_pairs={{0,8},{8,0},{1,9},{9,1},{2,10},{10,2},{3,11},{11,3},{4,12},{12,4},... | collective-permute-start | bytes 1179656 | tf_op jit(solution)/shard_map/ppermute | solution.py:29
  461.7 22.2 %collective-permute-start.61 = (bf16[32,1024]{1,0:T(8,128)(2,1)S(1)}, bf16[32,1024]{1,0:T(8,128)(2,1)S(1)}, u32[]{:S(2)}, u32[]{:S(2)}) collective-permute-start(bf16[32,1024]{1,0:T(8,128)(2,1)S(1)} %fusion.114), channel_id=1, source_target_pairs={{0,16},{16,0},{1,17},{17,1},{2,18},{18,2},{3,19},{19,3},{4,20},{20... | collective-permute-start | bytes 196616 | tf_op jit(solution)/shard_map/ppermute | solution.py:29
  472.4 6.7 collective-permute-start.53
  477.2 31.9 %collective-permute-start.36 = (bf16[4,2,96,1024]{3,2,1,0:T(8,128)(2,1)}, bf16[4,2,96,1024]{3,2,1,0:T(8,128)(2,1)}, u32[]{:S(2)}, u32[]{:S(2)}) collective-permute-start(bf16[4,2,96,1024]{3,2,1,0:T(8,128)(2,1)} %get-tuple-element.64), channel_id=1, source_target_pairs={{0,1},{1,0},{2,3},{3,2},{4,5},{5,4},{6,7},{7,6},{8,9},{9,8},{10,11... | collective-permute-start | bytes 4718600 | tf_op jit(solution)/shard_map/ppermute | solution.py:29
  479.3 11.9 %collective-permute-start.54 = (bf16[2,2,32,896]{3,2,1,0:T(8,128)(2,1)S(1)}, bf16[2,2,32,896]{3,2,1,0:T(8,128)(2,1)S(1)}, u32[]{:S(2)}, u32[]{:S(2)}) collective-permute-start(bf16[2,2,32,896]{3,2,1,0:T(8,128)(2,1)S(1)} %get-tuple-element.108), channel_id=1, source_target_pairs={{0,8},{8,0},{1,9},{9,1},{2,10},{10,2},{3,11},{11,3},{4,12},{12,4},... | collective-permute-start | bytes 688136 | tf_op jit(solution)/shard_map/ppermute | solution.py:29
  481.8 14.3 %collective-permute-start.65 = (bf16[128,1024]{1,0:T(8,128)(2,1)S(1)}, bf16[128,1024]{1,0:T(8,128)(2,1)S(1)}, u32[]{:S(2)}, u32[]{:S(2)}) collective-permute-start(bf16[128,1024]{1,0:T(8,128)(2,1)S(1)} %fusion.102), channel_id=1, source_target_pairs={{0,16},{16,0},{1,17},{17,1},{2,18},{18,2},{3,19},{19,3},{4,20},{20... | collective-permute-start | bytes 786440 | tf_op jit(solution)/shard_map/ppermute | solution.py:29
  492.1 7.8 %collective-permute-start.55 = (bf16[2,2,32,896]{3,2,1,0:T(8,128)(2,1)}, bf16[2,2,32,896]{3,2,1,0:T(8,128)(2,1)}, u32[]{:S(2)}, u32[]{:S(2)}) collective-permute-start(bf16[2,2,32,896]{3,2,1,0:T(8,128)(2,1)} %get-tuple-element.106), channel_id=1, source_target_pairs={{0,2},{2,0},{1,3},{3,1},{4,6},{6,4},{5,7},{7,5},{8,10},{10,8},{9,1... | collective-permute-start | bytes 688136 | tf_op jit(solution)/shard_map/ppermute | solution.py:29
  537.5 32.6 %collective-permute-start.56 = (bf16[2,32,1024]{2,1,0:T(8,128)(2,1)S(1)}, bf16[2,32,1024]{2,1,0:T(8,128)(2,1)S(1)}, u32[]{:S(2)}, u32[]{:S(2)}) collective-permute-start(bf16[2,32,1024]{2,1,0:T(8,128)(2,1)S(1)} %fusion.107), channel_id=1, source_target_pairs={{0,1},{1,0},{2,3},{3,2},{4,5},{5,4},{6,7},{7,6},{8,9},{9,8},{10,11... | collective-permute-start | bytes 393224 | tf_op jit(solution)/shard_map/ppermute | solution.py:29
  540.3 45.0 %collective-permute-start.62 = (bf16[2,128,1024]{2,1,0:T(8,128)(2,1)}, bf16[2,128,1024]{2,1,0:T(8,128)(2,1)}, u32[]{:S(2)}, u32[]{:S(2)}) collective-permute-start(bf16[2,128,1024]{2,1,0:T(8,128)(2,1)} %fusion.85), channel_id=1, source_target_pairs={{0,4},{4,0},{1,5},{5,1},{2,6},{6,2},{3,7},{7,3},{8,12},{12,8},{9,1... | collective-permute-start | bytes 1572872 | tf_op jit(solution)/shard_map/ppermute | solution.py:29
  559.2 30.5 %collective-permute-start.46 = (bf16[2,2,2,2,32,896]{5,4,3,1,2,0:T(8,128)(2,1)}, bf16[2,2,2,2,32,896]{5,4,3,1,2,0:T(8,128)(2,1)S(1)}, u32[]{:S(2)}, u32[]{:S(2)}) collective-permute-start(bf16[2,2,2,2,32,896]{5,4,3,1,2,0:T(8,128)(2,1)} %fusion.52), channel_id=1, source_target_pairs={{0,4},{4,0},{1,5},{5,1},{2,6},{6,2},{3,7},{7,3},{8,12},{12,8},{9,1... | collective-permute-start | bytes 2752520 | tf_op jit(solution)/shard_map/ppermute | solution.py:29
  570.2 14.6 %collective-permute-start.57 = (bf16[2,32,1024]{2,1,0:T(8,128)(2,1)S(1)}, bf16[2,32,1024]{2,1,0:T(8,128)(2,1)S(1)}, u32[]{:S(2)}, u32[]{:S(2)}) collective-permute-start(bf16[2,32,1024]{2,1,0:T(8,128)(2,1)S(1)} %fusion.108), channel_id=1, source_target_pairs={{0,4},{4,0},{1,5},{5,1},{2,6},{6,2},{3,7},{7,3},{8,12},{12,8},{9,1... | collective-permute-start | bytes 393224 | tf_op jit(solution)/shard_map/ppermute | solution.py:29
  570.4 51.1 %collective-permute-start.37 = (bf16[4,2,96,1024]{3,2,1,0:T(8,128)(2,1)}, bf16[4,2,96,1024]{3,2,1,0:T(8,128)(2,1)}, u32[]{:S(2)}, u32[]{:S(2)}) collective-permute-start(bf16[4,2,96,1024]{3,2,1,0:T(8,128)(2,1)} %fusion.31), channel_id=1, source_target_pairs={{0,1},{1,0},{2,3},{3,2},{4,5},{5,4},{6,7},{7,6},{8,9},{9,8},{10,11... | collective-permute-start | bytes 4718600 | tf_op jit(solution)/shard_map/ppermute | solution.py:29
  584.9 5.8 collective-permute-start.58
  587.1 25.7 %collective-permute-start.63 = (bf16[128,1024]{1,0:T(8,128)(2,1)S(1)}, bf16[128,1024]{1,0:T(8,128)(2,1)S(1)}, u32[]{:S(2)}, u32[]{:S(2)}) collective-permute-start(bf16[128,1024]{1,0:T(8,128)(2,1)S(1)} %fusion.101), channel_id=1, source_target_pairs={{0,16},{16,0},{1,17},{17,1},{2,18},{18,2},{3,19},{19,3},{4,20},{20... | collective-permute-start | bytes 786440 | tf_op jit(solution)/shard_map/ppermute | solution.py:29
  590.0 31.2 %collective-permute-start.47 = (bf16[2,2,2,32,896]{4,3,2,0,1:T(8,128)(2,1)S(1)}, bf16[2,2,2,32,896]{4,3,2,0,1:T(8,128)(2,1)S(1)}, u32[]{:S(2)}, u32[]{:S(2)}) collective-permute-start(bf16[2,2,2,32,896]{4,3,2,0,1:T(8,128)(2,1)S(1)} %fusion.95), channel_id=1, source_target_pairs={{0,16},{16,0},{1,17},{17,1},{2,18},{18,2},{3,19},{19,3},{4,20},{20... | collective-permute-start | bytes 1376264 | tf_op jit(solution)/shard_map/ppermute | solution.py:29
  621.4 7.1 %collective-permute-start.48 = (bf16[2,2,32,896]{3,2,1,0:T(8,128)(2,1)S(1)}, bf16[2,2,32,896]{3,2,1,0:T(8,128)(2,1)S(1)}, u32[]{:S(2)}, u32[]{:S(2)}) collective-permute-start(bf16[2,2,32,896]{3,2,1,0:T(8,128)(2,1)S(1)} %bitcast.616), channel_id=1, source_target_pairs={{0,1},{1,0},{2,3},{3,2},{4,5},{5,4},{6,7},{7,6},{8,9},{9,8},{10,11... | collective-permute-start | bytes 688136 | tf_op jit(solution)/shard_map/ppermute | solution.py:29
  623.9 12.0 %collective-permute-start.38 = (bf16[2,96,1024]{2,1,0:T(8,128)(2,1)S(1)}, bf16[2,96,1024]{2,1,0:T(8,128)(2,1)S(1)}, u32[]{:S(2)}, u32[]{:S(2)}) collective-permute-start(bf16[2,96,1024]{2,1,0:T(8,128)(2,1)S(1)} %get-tuple-element.60), channel_id=1, source_target_pairs={{0,8},{8,0},{1,9},{9,1},{2,10},{10,2},{3,11},{11,3},{4,12},{12,4},... | collective-permute-start | bytes 1179656 | tf_op jit(solution)/shard_map/ppermute | solution.py:29
  624.0 21.4 %collective-permute-start.40 = (bf16[2,96,1024]{2,1,0:T(8,128)(2,1)S(1)}, bf16[2,96,1024]{2,1,0:T(8,128)(2,1)S(1)}, u32[]{:S(2)}, u32[]{:S(2)}) collective-permute-start(bf16[2,96,1024]{2,1,0:T(8,128)(2,1)S(1)} %get-tuple-element.61), channel_id=1, source_target_pairs={{0,10},{2,8},{8,2},{10,0},{1,11},{3,9},{9,3},{11,1},{4,14},{6,12},... | collective-permute-start | bytes 1179656 | tf_op jit(solution)/shard_map/ppermute | solution.py:29
  627.1 19.4 %collective-permute-start.39 = (bf16[2,96,1024]{2,1,0:T(8,128)(2,1)S(1)}, bf16[2,96,1024]{2,1,0:T(8,128)(2,1)S(1)}, u32[]{:S(2)}, u32[]{:S(2)}) collective-permute-start(bf16[2,96,1024]{2,1,0:T(8,128)(2,1)S(1)} %get-tuple-element.62), channel_id=1, source_target_pairs={{0,2},{2,0},{1,3},{3,1},{4,6},{6,4},{5,7},{7,5},{8,10},{10,8},{9,1... | collective-permute-start | bytes 1179656 | tf_op jit(solution)/shard_map/ppermute | solution.py:29
  629.4 20.1 %collective-permute-start.49 = (bf16[2,2,32,896]{3,2,1,0:T(8,128)(2,1)}, bf16[2,2,32,896]{3,2,1,0:T(8,128)(2,1)}, u32[]{:S(2)}, u32[]{:S(2)}) collective-permute-start(bf16[2,2,32,896]{3,2,1,0:T(8,128)(2,1)} %get-tuple-element.102), channel_id=1, source_target_pairs={{0,8},{8,0},{1,9},{9,1},{2,10},{10,2},{3,11},{11,3},{4,12},{12,4},... | collective-permute-start | bytes 688136 | tf_op jit(solution)/shard_map/ppermute | solution.py:29
  648.6 5.4 collective-permute-start.41
  654.0 3.9 collective-permute-start.42
  654.2 15.4 %collective-permute-start.50 = (bf16[2,2,32,896]{3,2,1,0:T(8,128)(2,1)S(1)}, bf16[2,2,32,896]{3,2,1,0:T(8,128)(2,1)S(1)}, u32[]{:S(2)}, u32[]{:S(2)}) collective-permute-start(bf16[2,2,32,896]{3,2,1,0:T(8,128)(2,1)S(1)} %get-tuple-element.100), channel_id=1, source_target_pairs={{0,2},{2,0},{1,3},{3,1},{4,6},{6,4},{5,7},{7,5},{8,10},{10,8},{9,1... | collective-permute-start | bytes 688136 | tf_op jit(solution)/shard_map/ppermute | solution.py:29
  658.0 3.8 collective-permute-start.43
  661.8 3.7 collective-permute-start.44
  (126 other events, 1006.5 us)

commit v3 on v1

v3 whole, which is shorter than its diff:
```python
import math

import jax
import jax.numpy as jnp
import numpy as np
from jax import lax
from jax.experimental import pallas as pl
from jax.experimental.pallas import tpu as pltpu
from jax.sharding import Mesh
from jax.sharding import PartitionSpec as P

HEAD_DIM = 64
ROT = 16
EPS = 1e-05
MASKED = -1e30

AXES = ("e", "zh", "zl", "x", "y", "c")
HEAD_BITS = ("zh", "zl", "x", "y")
T1, T2, D1, D2 = "y", "zl", "zh", "x"
TP = (T1, T2, "c")
RANKS = 8
NEAR = (("c",), (T1,), (T2,), (T1, "c"), (T2, "c"), (T1, T2), (T1, T2, "c"))
FAR = ((D1,), (D2,))
SMALL_AXES = ("c", T1, T2, D1, D2)

F32, BF16 = jnp.float32, jnp.bfloat16
MESH = pl.DeviceIdType.MESH

PAIR = 2 * HEAD_DIM
QKV = 3 * PAIR
SLOTS = 12


def dot(a, b, contract):
    return lax.dot_general(a, b, (contract, ((), ())), preferred_element_type=F32)


class Links:
    def __init__(self, send_sem, recv_sem):
        self.place = {axis: lax.axis_index(axis) for axis in AXES}
        self.send_sem, self.recv_sem, self.used = send_sem, recv_sem, 0

    def reserve(self, count):
        self.used += count
        return self.used - count

    def peer(self, axes):
        return {axis: 1 - self.place[axis] for axis in axes}

    def chip(self, j):
        one, two = self.place[T1], self.place[T2]
        return {T1: one + (j // 2) * (1 - 2 * one), T2: two + (j % 2) * (1 - 2 * two)}

    def meet(self):
        barrier = pltpu.get_barrier_semaphore()
        for axes in NEAR + FAR:
            pl.semaphore_signal(barrier, inc=1, device_id=self.peer(axes), device_id_type=MESH)
        pl.semaphore_wait(barrier, len(NEAR) + len(FAR))

    def copy(self, source, target, device, slot=None):
        if slot is None:
            slot = self.reserve(1)
        if not isinstance(device, dict):
            device = self.peer(device)
        return pltpu.make_async_remote_copy(
            src_ref=source,
            dst_ref=target,
            send_sem=self.send_sem.at[slot],
            recv_sem=self.recv_sem.at[slot],
            device_id=device,
            device_id_type=MESH,
        )


def rank_of(place):
    return place[T1] * 4 + place[T2] * 2 + place["c"]


def block_of(place):
    index = place["zh"]
    for axis in AXES[2:]:
        index = index * 2 + place[axis]
    return index


def flipped(place, axes):
    return {a: (1 - i if a in axes else i) for a, i in place.items()}


class Rows:
    def __init__(self, links, buffer):
        self.links, self.buffer, self.base = links, buffer, links.reserve(8)

    def core(self, j):
        return self.links.copy(
            self.buffer.at[j, 0], self.buffer.at[j, 1], ("c",), self.base + j
        )

    def chip(self, j):
        return self.links.copy(
            self.buffer.at[0, 0], self.buffer.at[j, 0], self.links.chip(j), self.base + 4 + j
        )

    def start(self):
        self.core(0).start()
        for j in (3, 2, 1):
            self.chip(j).start()

    def arrive(self, j):
        @pl.when(j > 0)
        def _():
            self.chip(j).wait_recv()
            self.core(j).start()

        self.core(j).wait_recv()

    def finish(self):
        for j in range(4):
            self.core(j).wait_send()
        for j in range(1, 4):
            self.chip(j).wait_send()


class Sums:
    def __init__(self, links, core_in, chip_in, core_out, chip_out):
        self.links, self.base = links, links.reserve(8)
        self.core_in, self.chip_in, self.core_out, self.chip_out = core_in, chip_in, core_out, chip_out

    def core(self, j):
        return self.links.copy(
            self.core_out.at[j], self.core_in.at[j], ("c",), self.base + j
        )

    def chip(self, j):
        return self.links.copy(
            self.chip_out.at[j - 1], self.chip_in.at[j - 1], self.links.chip(j), self.base + 4 + j
        )

    def run(self, term, scratch, own):
        rows = own.shape[0]

        def pass_on(j, side):
            self.core(j).wait_recv()
            total = scratch[side, :rows] + self.core_in[j].astype(F32)

            @pl.when(j > 0)
            def _():
                self.chip_out[j - 1] = total.astype(BF16)
                self.chip(j).start()

            @pl.when(j == 0)
            def _():
                own[...] = total

        def step(i, carry):
            j = 3 - i
            side = i % 2

            scratch[side] = term(j)
            self.core_out[j] = scratch[side, rows:].astype(BF16)
            self.core(j).start()

            @pl.when(i > 0)
            def _():
                pass_on(j + 1, 1 - side)

            return carry

        lax.fori_loop(0, 4, step, 0)
        pass_on(0, 1)

    def total(self, own):
        for j in (1, 2, 3):
            self.chip(j).wait_recv()
        for j in range(4):
            self.core(j).wait_send()
        for j in (1, 2, 3):
            self.chip(j).wait_send()

        def at(rows):
            value = own[rows]
            for j in (1, 2, 3):
                value = value + self.chip_in[j - 1, rows].astype(F32)
            return value

        return at


def mean_of(value):
    return jnp.sum(value, axis=-1, keepdims=True) * (1.0 / value.shape[-1])


def normalise(stream):
    centred = stream - mean_of(stream)
    inverse = lax.rsqrt(mean_of(centred * centred) + EPS)
    return centred * inverse, inverse


def layers_kernel(
    parts,
    down,
    proj,
    inputs,
    cotangent,
    mask,
    small,
    tables,
    outputs,
    input_grad,
    cat_out,
    down_out,
    proj_out,
    small_out,
    cat_all,
    dp_all,
    hid,
    rnd,
    mask_all,
    qkv_kept,
    probs,
    ca,
    slope,
    mdud,
    scratch,
    core_in,
    chip_in,
    core_out,
    chip_out,
    own,
    stream_two,
    up_one,
    small_sum,
    small_in,
    sums,
    grad_sum,
    grad_in,
    cat_own,
    cat_s1,
    cat_r1,
    cat_s2,
    cat_r2,
    cat_a,
    dp_grad,
    down_s1,
    down_r1,
    down_s2,
    down_r2,
    proj_s1,
    proj_r1,
    proj_s2,
    proj_r2,
    proj_s3,
    proj_r3,
    send_sem,
    recv_sem,
    own_sem,
    free_sem,
):
    links = Links(send_sem, recv_sem)
    me = links.place
    rank, block, slot = rank_of(me), block_of(me), me[D2] * 2 + me[D1]
    mine = me["c"] == me[D2]
    others = jnp.logical_not(mine)
    layers, wide = parts.shape[0], parts.shape[3]
    micros, pack = mask.shape[0], mask.shape[1]
    rows, width = inputs.shape
    lift = wide - QKV
    scale = 1.0 / math.sqrt(HEAD_DIM)
    lane = lax.broadcasted_iota(jnp.int32, (pack, PAIR), 1)
    first_head = lane < HEAD_DIM

    def bias_row(layer, index, columns=None):
        value = small_sum[len(SMALL_AXES), pl.ds(layer * SLOTS + index, 1), :]
        return value

    class Weights:
        def __init__(self, layer):
            self.layer = layer
            self.keep = [
                pltpu.make_async_copy(
                    parts.at[layer, rank], cat_all.at[layer, block], own_sem.at[layer, 0]
                ),
                pltpu.make_async_copy(
                    down.at[layer], self.down_rows(slot), own_sem.at[layer, 1]
                ),
            ]
            self.trades = [
                links.copy(
                    parts.at[layer, rank_of(flipped(me, axes))], cat_all.at[layer, block], axes
                )
                for axes in NEAR
            ]
            self.cat_one = []
            for zl in range(2):
                part = self.cat_rows(me["zh"], zl)
                self.cat_one.append(links.copy(part, part, (D1,)))
            self.cat_two = []
            for zl in range(2):
                for zh in range(2):
                    part = self.cat_rows(zh, zl)
                    self.cat_two.append(links.copy(part, part, (D2,)))
            self.down_one = links.copy(down.at[layer], self.down_rows(slot), (D1,))
            both = self.down_rows(me[D2] * 2, 2)
            self.down_two = links.copy(both, both, (D2,))
            count = proj.shape[1]
            half = dp_all.at[layer, pl.ds(me["zh"] * HEAD_DIM + me["c"] * count, count)]
            self.to_core = links.copy(proj.at[layer], half, ("c",))
            self.stays = pltpu.make_async_copy(proj.at[layer], half, own_sem.at[layer, 2])
            head = dp_all.at[layer, pl.ds(me["zh"] * HEAD_DIM, HEAD_DIM)]
            self.proj_one = links.copy(head, head, (D1,))
            heads = dp_all.at[layer, pl.ds(0, PAIR)]
            self.proj_two = links.copy(heads, heads, (D2,))

        def cat_rows(self, zh, zl):
            return cat_all.at[self.layer, pl.ds(zh * 16 + zl * 8 + me["x"] * 4, 4)]

        def down_rows(self, place, count=1):
            size = down.shape[1]
            return dp_all.at[self.layer, pl.ds(PAIR + place * size, count * size)]

        def start_own(self):
            for copy in self.keep:
                copy.start()

        def start_trades(self):
            for copy in self.trades:
                copy.start()

        def start_rows(self):
            self.keep[1].wait()
            self.down_one.start()

            @pl.when(mine)
            def _():
                self.stays.start()
                self.stays.wait()

            @pl.when(others)
            def _():
                self.to_core.start()
                self.to_core.wait_send()

        def cat_first(self):
            self.keep[0].wait()
            for copy in self.trades:
                copy.wait()
            for copy in self.cat_one:
                copy.start()

        def cat_second(self):
            for zl in range(2):
                self.cat_one[zl].wait()
                for zh in range(2):
                    self.cat_two[2 * zl + zh].start()

        def cat_done(self):
            for copy in self.cat_two:
                copy.wait()

        def proj_first(self):
            @pl.when(mine)
            def _():
                self.to_core.wait_recv()
                self.proj_one.start()

        def rows_second(self):
            self.down_one.wait()
            self.down_two.start()

            @pl.when(mine)
            def _():
                self.proj_one.wait()
                self.proj_two.start()

        def rows_done(self):
            self.down_two.wait()

            @pl.when(mine)
            def _():
                self.proj_two.wait_send()

            @pl.when(others)
            def _():
                self.proj_two.wait_recv()

    def turn(value, sign):
        return (
            value * tables[0]
            + pltpu.roll(value, PAIR - ROT // 2, 1) * (tables[1] * sign)
            + pltpu.roll(value, ROT // 2, 1) * (tables[2] * sign)
        )

    def by_head(value):
        zero = jnp.zeros_like(value)
        return jnp.concatenate(
            [jnp.where(first_head, value, zero), jnp.where(first_head, zero, value)], axis=0
        )

    def of_heads(value):
        return jnp.where(first_head, value[:pack], value[pack:])

    def forward(layer, j):
        hidden = hid[layer, j].reshape(2 * rows, width)
        scratch[0, :, :wide] = dot(hidden, cat_all[layer].reshape(width, wide), ((1,), (0,)))
        bias = bias_row(layer, rank)

        def each(p, carry):
            at = pl.ds(pl.multiple_of(p * pack, pack), pack)
            turned = scratch[0, at, :QKV] + bias[:, :QKV]
            queries = turn(turned[:, :PAIR], 1.0).astype(BF16)
            keys = turn(turned[:, PAIR : 2 * PAIR], 1.0).astype(BF16)
            values = turned[:, 2 * PAIR :].astype(BF16)
            qkv_kept[layer, j, at, :PAIR] = queries
            qkv_kept[layer, j, at, PAIR : 2 * PAIR] = keys
            qkv_kept[layer, j, at, 2 * PAIR :] = values
            hide = mask_all[j, p // micros, p % micros][:, :pack].astype(F32)
            scores = dot(by_head(queries), keys, ((1,), (1,))) * scale
            scores = scores + jnp.concatenate([hide, hide], axis=0)
            shifted = jnp.exp(scores - jnp.max(scores, axis=-1, keepdims=True))
            soft = shifted / jnp.sum(shifted, axis=-1, keepdims=True)
            soft = soft.astype(BF16)
            probs[layer, j, p] = soft
            ca[layer, j, at, :PAIR] = of_heads(dot(soft, values, ((1,), (0,)))).astype(BF16)
            for start in range(QKV, wide, 2 * PAIR):
                cut = slice(start, start + 2 * PAIR)
                raised = scratch[0, at, cut] + bias[:, cut]
                cdf = 0.5 * (1.0 + lax.erf(raised * 0.7071067811865476))
                density = jnp.exp(-0.5 * raised * raised) * 0.3989422804014327
                to = start - QKV
                ca[layer, j, at, PAIR + to : PAIR + to + 2 * PAIR] = (raised * cdf).astype(BF16)
                slope[layer, j, at, to : to + 2 * PAIR] = (cdf + raised * density).astype(BF16)
            return carry

        lax.fori_loop(0, 2 * micros, each, 0)

    def backward(layer, j):
        rounded = rnd[j].reshape(2 * rows, width)
        scratch[0, :, : PAIR + lift] = dot(rounded, dp_all[layer], ((1,), (1,)))

        def each(p, carry):
            at = pl.ds(pl.multiple_of(p * pack, pack), pack)
            for start in range(0, lift, 2 * PAIR):
                cut = slice(start, start + 2 * PAIR)
                grown = scratch[0, at, PAIR + start : 3 * PAIR + start]
                grown = (grown * slope[layer, j, at, cut].astype(F32)).astype(BF16)
                mdud[j, at, QKV + start : QKV + start + 2 * PAIR] = grown
                sums[:, QKV + start : QKV + start + 2 * PAIR] += jnp.sum(
                    grown.astype(F32).reshape(pack // 8, 8, 2 * PAIR), axis=0
                )
            context = by_head(scratch[0, at, :PAIR].astype(BF16))
            queries = by_head(qkv_kept[layer, j, at, :PAIR])
            keys = qkv_kept[layer, j, at, PAIR : 2 * PAIR]
            values = qkv_kept[layer, j, at, 2 * PAIR :]
            kept = probs[layer, j, p]
            soft = kept.astype(F32)
            prob_delta = dot(context, values, ((1,), (1,)))
            row_delta = jnp.sum(soft * prob_delta, axis=-1, keepdims=True)
            score_delta = (soft * (prob_delta - row_delta)).astype(BF16)
            value_delta = dot(kept, context, ((0,), (0,)))
            query_delta = of_heads(dot(score_delta, keys, ((1,), (0,)))) * scale
            key_delta = dot(score_delta, queries, ((0,), (0,))) * scale
            three = (turn(query_delta, -1.0), turn(key_delta, -1.0), value_delta)
            for i, delta in enumerate(three):
                delta = delta.astype(BF16)
                cut = slice(i * PAIR, (i + 1) * PAIR)
                mdud[j, at, cut] = delta
                sums[:, cut] += jnp.sum(delta.astype(F32).reshape(pack // 8, 8, PAIR), axis=0)
            return carry

        lax.fori_loop(0, 2 * micros, each, 0)

    def out_term(layer):
        return lambda j: dot(ca[layer, j], dp_all[layer], ((1,), (0,)))

    def hidden_term(layer):
        return lambda j: dot(mdud[j], cat_all[layer].reshape(width, wide), ((1,), (1,)))

    class Grads:
        def __init__(self, layer):
            self.layer = layer
            self.down_one = links.copy(down_s1, down_r1.at[layer], (D2,))
            self.down_two = links.copy(down_s2, down_r2.at[layer], (D1,))
            self.proj_one = links.copy(proj_s1, proj_r1.at[layer], (D2,))
            self.proj_two = links.copy(proj_s2, proj_r2.at[layer], (D1,))
            self.proj_three = links.copy(proj_s3, proj_r3.at[layer], ("c",))
            self.cat_one = [
                links.copy(cat_s1.at[i], cat_r1.at[layer, i], (D2,)) for i in range(2)
            ]
            self.cat_two = links.copy(cat_s2, cat_r2.at[layer], (D1,))
            self.trades = []
            for axes in NEAR:
                there = flipped(me, axes)
                part = cat_a.at[there["zl"], there["y"] * 2 + there["c"]]
                self.trades.append(links.copy(part, cat_out.at[layer, rank], axes))
            self.keep = pltpu.make_async_copy(
                cat_a.at[me["zl"], me["y"] * 2 + me["c"]], cat_out.at[layer, rank], own_sem.at[layer, 3]
            )

        def rows_one(self):
            layer = self.layer
            kept = ca[layer].reshape(8 * rows, PAIR + lift)
            rounded = rnd[...].reshape(8 * rows, width)
            dp_grad[pl.ds(PAIR, lift)] = dot(kept[:, PAIR:], rounded, ((0,), (0,)))
            dp_grad[pl.ds(0, PAIR)] = dot(kept[:, :PAIR], rounded, ((0,), (0,)))
            half = lift // 2
            down_s1[...] = dp_grad[pl.ds(PAIR + (1 - me[D2]) * half, half)].astype(BF16)
            self.down_one.start()

            @pl.when(others)
            def _():
                proj_s1[...] = dp_grad[pl.ds(0, PAIR)].astype(BF16)
                self.proj_one.start()

        def rows_two(self):
            layer = self.layer
            half, quarter = lift // 2, lift // 4
            base = PAIR + me[D2] * half
            self.down_one.wait()
            at = (1 - me[D1]) * quarter
            down_s2[...] = (
                dp_grad[pl.ds(base + at, quarter)]
                + down_r1[layer, pl.ds(at, quarter)].astype(F32)
            ).astype(BF16)
            self.down_two.start()

            @pl.when(others)
            def _():
                self.proj_one.wait_send()

            @pl.when(mine)
            def _():
                self.proj_one.wait_recv()
                at = (1 - me[D1]) * HEAD_DIM
                proj_s2[...] = (
                    dp_grad[pl.ds(at, HEAD_DIM)]
                    + proj_r1[layer, pl.ds(at, HEAD_DIM)].astype(F32)
                ).astype(BF16)
                self.proj_two.start()

        def rows_three(self):
            layer = self.layer
            half, quarter = lift // 2, lift // 4
            base = PAIR + me[D2] * half
            self.down_two.wait()
            at = me[D1] * quarter
            down_out[layer] = (
                dp_grad[pl.ds(base + at, quarter)]
                + down_r1[layer, pl.ds(at, quarter)].astype(F32)
                + down_r2[layer].astype(F32)
            )
            count = proj.shape[1]

            @pl.when(mine)
            def _():
                self.proj_two.wait()
                at = me[D1] * HEAD_DIM

                def half_of(which):
                    return (
                        dp_grad[pl.ds(at + which * count, count)]
                        + proj_r1[layer, pl.ds(at + which * count, count)].astype(F32)
                        + proj_r2[layer, pl.ds(which * count, count)].astype(F32)
                    )

                proj_out[layer] = half_of(me["c"])
                proj_s3[...] = half_of(1 - me["c"]).astype(BF16)
                self.proj_three.start()
                self.proj_three.wait_send()

            @pl.when(others)
            def _():
                self.proj_three.wait_recv()
                proj_out[layer] = proj_r3[layer].astype(F32)

        def cat_terms(self, i):
            layer = self.layer
            zh = me["zh"] if i else 1 - me["zh"]
            half = width // 2
            columns = pl.ds(pl.multiple_of(zh * half, half), half)
            kept = hid[layer, :, :, :, columns].reshape(8 * rows, half)
            deltas = mdud[...].reshape(8 * rows, wide)
            scratch[:, : width // 8 * 2, :wide] = dot(kept, deltas, ((0,), (0,))).reshape(
                2, width // 4, wide
            )
            size = width // 8
            for zl in range(2):
                cat_s1[i, zl] = scratch[zl, pl.ds((1 - me["x"]) * size, size), :wide].astype(BF16)
                cat_own[i, zl] = scratch[zl, pl.ds(me["x"] * size, size), :wide]
            self.cat_one[i].start()

        def cat_step_two(self):
            layer = self.layer
            self.cat_one[0].wait()
            cat_s2[...] = (cat_own[0] + cat_r1[layer, 0].astype(F32)).astype(BF16)
            self.cat_two.start()

        def cat_step_three(self):
            layer = self.layer
            self.cat_one[1].wait()
            self.cat_two.wait()
            total = cat_own[1] + cat_r1[layer, 1].astype(F32) + cat_r2[layer].astype(F32)
            cat_a[...] = total.astype(BF16).reshape(cat_a.shape)
            for copy in self.trades:
                copy.start()
            self.keep.start()

        def cat_done(self):
            for copy in self.trades:
                copy.wait()
            self.keep.wait()

    def put_sums(layer, index, value):
        grad_sum[0, pl.ds(layer * SLOTS + index, 1), : value.shape[1]] = value

    def own_rows(layer, total, stream_at, up_at, put):
        gain = bias_row(layer, RANKS)
        gain_sum = jnp.zeros((1, width), F32)
        shift_sum = jnp.zeros((1, width), F32)
        for m in range(2 * micros):
            at = pl.ds(m * (rows // (2 * micros)), rows // (2 * micros))
            delta = total(at)
            normed, inverse = normalise(stream_at(at))
            gain_sum = gain_sum + jnp.sum(delta * normed, axis=0, keepdims=True)
            shift_sum = shift_sum + jnp.sum(delta, axis=0, keepdims=True)
            scaled = delta * gain
            put(
                at,
                up_at(at) + inverse * (scaled - mean_of(scaled) - normed * mean_of(scaled * normed)),
            )
        put_sums(layer, RANKS, gain_sum)
        put_sums(layer, RANKS + 1, shift_sum)

    def bias_sums(layer):
        put_sums(layer, rank, jnp.sum(sums[...], axis=0, keepdims=True))
        rounded = jnp.zeros((8, width), F32)
        for m in range(2 * micros):
            size = rows // (2 * micros)
            part = rnd[0, 0, pl.ds(m * size, size)].astype(F32)
            rounded = rounded + jnp.sum(part.reshape(size // 8, 8, width), axis=0)
        put_sums(layer, RANKS + 2, jnp.sum(rounded, axis=0, keepdims=True))

    def give_back(turn_index):
        for axes in (("c",), (T1,), (T2,), (T1, T2)):
            pl.semaphore_signal(
                free_sem.at[turn_index], inc=1, device_id=links.peer(axes), device_id_type=MESH
            )

    def await_places(turn_index):
        pl.semaphore_wait(free_sem.at[turn_index], 4)

    taken = [Weights(layer) for layer in range(layers)]
    grads = [Grads(layer) for layer in range(layers)]
    row_gathers = [Rows(links, hid.at[1]), Rows(links, mask_all), Rows(links, rnd)]
    hidden_two, rounded_one = Rows(links, hid.at[1]), Rows(links, rnd)
    sets = (core_in, chip_in, core_out, chip_out)
    out_one, delta_two, delta_one = Sums(links, *sets), Sums(links, *sets), Sums(links, *sets)
    out_two = Sums(links, *sets)
    small_copies = [
        links.copy(small_sum.at[i], small_in.at[i], (axis,)) for i, axis in enumerate(SMALL_AXES)
    ]
    grad_copies = [
        links.copy(grad_sum.at[i], grad_in.at[i], (axis,)) for i, axis in enumerate(SMALL_AXES)
    ]

    for one in taken:
        one.start_own()
    hid[1, 0, 0] = inputs[...]
    mask_all[0, 0] = mask[...]
    rnd[0, 0] = cotangent[...]
    small_sum[0] = small[...]
    grad_sum[...] = jnp.zeros_like(grad_sum)
    links.meet()

    small_copies[0].start()
    taken[0].start_trades()
    taken[0].start_rows()
    row_gathers[1].start()
    row_gathers[0].start()
    for i in range(len(SMALL_AXES)):
        small_copies[i].wait()
        small_sum[i + 1] = small_sum[i] + small_in[i]
        if i + 1 < len(SMALL_AXES):
            small_copies[i + 1].start()
        if i == 1:
            taken[0].cat_first()
        if i == 2:
            taken[0].proj_first()
    taken[1].start_trades()
    row_gathers[2].start()

    gain, shift = bias_row(0, RANKS), bias_row(0, RANKS + 1)

    def first_norm(j, carry):
        row_gathers[0].arrive(j)
        row_gathers[1].arrive(j)

        def each(p, carry):
            size = rows // 4
            at = pl.ds(pl.multiple_of((p % 4) * size, size), size)
            normed, _ = normalise(hid[1, j, p // 4, at].astype(F32))
            hid[0, j, p // 4, at] = (normed * gain + shift).astype(BF16)
            return carry

        return lax.fori_loop(0, 8, each, carry)

    lax.fori_loop(0, 4, first_norm, 0)
    taken[0].rows_second()
    taken[0].cat_second()
    row_gathers[0].finish()
    row_gathers[1].finish()
    taken[1].cat_first()
    taken[1].start_rows()
    taken[1].proj_first()
    taken[0].cat_done()
    lax.fori_loop(0, 4, lambda j, c: (forward(0, j), c)[1], 0)
    taken[0].rows_done()
    out_one.run(out_term(0), scratch, own)
    taken[1].cat_second()

    def rest_of_rounded(j, carry):
        row_gathers[2].arrive(j)
        return carry

    lax.fori_loop(0, 4, rest_of_rounded, 0)
    row_gathers[2].finish()
    total = out_one.total(own)
    out_bias = bias_row(0, RANKS + 2)
    gain, shift = bias_row(1, RANKS), bias_row(1, RANKS + 1)
    for m in range(4):
        at = pl.ds(m * (rows // 4), rows // 4)
        stream = inputs[at].astype(F32) + total(at) + out_bias
        stream_two[at] = stream
        normed, _ = normalise(stream)
        hid[1, 0, 0, at] = (normed * gain + shift).astype(BF16)
    hidden_two.start()
    taken[1].rows_second()
    taken[1].cat_done()

    def second(j, carry):
        hidden_two.arrive(j)
        forward(1, j)
        return carry

    lax.fori_loop(0, 4, second, 0)
    hidden_two.finish()
    taken[1].rows_done()

    sums[...] = jnp.zeros_like(sums)
    lax.fori_loop(0, 4, lambda j, c: (backward(1, j), c)[1], 0)
    grads[1].rows_one()
    bias_sums(1)
    delta_two.run(hidden_term(1), scratch, own)
    grads[1].cat_terms(0)
    grads[1].cat_terms(1)
    grads[1].rows_two()
    total = delta_two.total(own)

    def put_one(at, value):
        up_one[at] = value
        rnd[0, 0, at] = value.astype(BF16)

    own_rows(1, total, lambda at: stream_two[at], lambda at: cotangent[at].astype(F32), put_one)
    rounded_one.start()
    give_back(0)
    await_places(0)
    out_two.run(out_term(1), scratch, input_grad)
    grads[1].cat_step_two()
    grads[1].rows_three()

    sums[...] = jnp.zeros_like(sums)

    def third(j, carry):
        rounded_one.arrive(j)
        backward(0, j)
        return carry

    lax.fori_loop(0, 4, third, 0)
    rounded_one.finish()
    grads[1].cat_step_three()
    total = out_two.total(input_grad)
    out_bias = bias_row(1, RANKS + 2)
    for m in range(4):
        at = pl.ds(m * (rows // 4), rows // 4)
        outputs[at] = (stream_two[at] + total(at) + out_bias).astype(BF16)
    give_back(1)
    grads[1].cat_done()
    await_places(1)
    delta_one.run(hidden_term(0), scratch, own)
    grads[0].cat_terms(0)
    grads[0].cat_terms(1)
    grads[0].rows_one()
    bias_sums(0)
    grads[0].cat_step_two()
    total = delta_one.total(own)

    def put_last(at, value):
        input_grad[at] = value

    own_rows(0, total, lambda at: inputs[at].astype(F32), lambda at: up_one[at], put_last)
    grad_copies[0].start()
    grads[0].rows_two()
    for i in range(len(SMALL_AXES)):
        grad_copies[i].wait()
        grad_sum[i + 1] = grad_sum[i] + grad_in[i]
        if i + 1 < len(SMALL_AXES):
            grad_copies[i + 1].start()
        if i == 1:
            grads[0].cat_step_three()
        if i == 3:
            grads[0].rows_three()
    small_out[...] = grad_sum[len(SMALL_AXES)]
    grads[0].cat_done()


def run_layers(parts, down, proj, inputs, cotangent, mask, small, tables):
    layers, _, count, wide = parts.shape
    rows, width = inputs.shape
    micros, pack, lanes = mask.shape
    lift = wide - QKV
    vmem = pl.BlockSpec(memory_space=pltpu.VMEM)
    anywhere = pl.BlockSpec(memory_space=pltpu.HBM)
    shape = jax.ShapeDtypeStruct
    stages = len(SMALL_AXES)
    small_rows = small.shape[0]
    copies = 256
    cat_size = width // 8
    buffers = [
        ((layers, 32, count, wide), BF16),
        ((layers, PAIR + lift, width), BF16),
        ((layers, 4, 2, rows, width), BF16),
        ((4, 2, rows, width), BF16),
        ((4, 2, micros, pack, lanes), BF16),
        ((layers, 4, 2 * rows, QKV), BF16),
        ((layers, 4, 2 * micros, 2 * pack, pack), BF16),
        ((layers, 4, 2 * rows, PAIR + lift), BF16),
        ((layers, 4, 2 * rows, lift), BF16),
        ((4, 2 * rows, wide), BF16),
        ((2, 2 * rows, width), F32),
        ((4, rows, width), BF16),
        ((3, rows, width), BF16),
        ((4, rows, width), BF16),
        ((3, rows, width), BF16),
        ((rows, width), F32),
        ((rows, width), F32),
        ((rows, width), F32),
        ((stages + 1, small_rows, width), F32),
        ((stages, small_rows, width), F32),
        ((8, wide), F32),
        ((stages + 1, small_rows, width), F32),
        ((stages, small_rows, width), F32),
        ((2, 2, cat_size, wide), F32),
        ((2, 2, cat_size, wide), BF16),
        ((layers, 2, 2, cat_size, wide), BF16),
        ((2, cat_size, wide), BF16),
        ((layers, 2, cat_size, wide), BF16),
        ((2, 4, count, wide), BF16),
        ((PAIR + lift, width), F32),
        ((lift // 2, width), BF16),
        ((layers, lift // 2, width), BF16),
        ((lift // 4, width), BF16),
        ((layers, lift // 4, width), BF16),
        ((PAIR, width), BF16),
        ((layers, PAIR, width), BF16),
        ((HEAD_DIM, width), BF16),
        ((layers, HEAD_DIM, width), BF16),
        ((HEAD_DIM // 2, width), BF16),
        ((layers, HEAD_DIM // 2, width), BF16),
    ]
    return pl.pallas_call(
        layers_kernel,
        out_shape=(
            shape((rows, width), BF16),
            shape((rows, width), F32),
            shape((layers, RANKS, count, wide), BF16),
            shape((layers,) + down.shape[1:], F32),
            shape((layers,) + proj.shape[1:], F32),
            shape(small.shape, F32),
        ),
        in_specs=[anywhere] * 3 + [vmem] * 5,
        out_specs=(vmem, vmem, anywhere, vmem, vmem, vmem),
        scratch_shapes=[pltpu.VMEM(dims, kind) for dims, kind in buffers]
        + [
            pltpu.SemaphoreType.DMA((copies,)),
            pltpu.SemaphoreType.DMA((copies,)),
            pltpu.SemaphoreType.DMA((layers, 4)),
            pltpu.SemaphoreType.REGULAR((2,)),
        ],
        compiler_params=pltpu.CompilerParams(
            collective_id=0, has_side_effects=True, vmem_limit_bytes=63 << 20
        ),
    )(parts, down, proj, inputs, cotangent, mask, small, tables)


def split_heads(value, parts):
    lead = value.ndim - 1
    value = value.reshape(value.shape[:-1] + (parts, 2, 2, 2, 2, HEAD_DIM))
    place = {axis: lead + 1 + i for i, axis in enumerate(HEAD_BITS)}
    order = [place[T1], place[T2], place[D2]] + list(range(lead + 1)) + [place[D1], lead + 5]
    return value.transpose(order)


def join_heads(value):
    lead = value.ndim - 6
    names = {T1: 0, T2: 1, D2: 2, D1: lead + 4}
    order = [3 + i for i in range(lead)] + [3 + lead] + [names[a] for a in HEAD_BITS] + [lead + 5]
    value = value.transpose(order)
    return value.reshape(value.shape[:lead] + (-1,))


def split_columns(value):
    lead = value.ndim - 1
    value = value.reshape(value.shape[:-1] + (2, 2, 2, 2, 2, -1))
    place = {axis: lead + i for i, axis in enumerate(AXES[1:])}
    order = [place[a] for a in TP] + list(range(lead)) + [place[D2], place[D1], lead + 5]
    return value.transpose(order)


def join_columns(value):
    lead = value.ndim - 6
    names = {a: i for i, a in enumerate(TP)} | {D2: 3 + lead, D1: 4 + lead}
    order = [3 + i for i in range(lead)] + [names[a] for a in AXES[1:]] + [lead + 5]
    value = value.transpose(order)
    return value.reshape(value.shape[:lead] + (-1,))


def refold(block, extra):
    if extra == 1:
        return block
    whole = lax.all_gather(block, AXES, axis=1, tiled=True)
    rows = whole.shape[1] // 32
    return lax.dynamic_slice_in_dim(whole, lax.axis_index(AXES[1:]) * rows, rows, 1)


def unfold(block, extra):
    if extra == 1:
        return block
    rows = block.shape[1]
    whole = jnp.zeros((block.shape[0], 32 * rows) + block.shape[2:], F32)
    whole = lax.dynamic_update_slice_in_dim(whole, block, lax.axis_index(AXES[1:]) * rows, 1)
    return lax.psum_scatter(whole, AXES, scatter_dimension=1, tiled=True)


def at_place(block):
    size = block.shape[1]
    whole = jnp.zeros((block.shape[0], 32 * size), F32)
    return lax.dynamic_update_slice_in_dim(
        whole, block.astype(F32), lax.axis_index(AXES[1:]) * size, 1
    )


def rope_tables(pack):
    half = ROT // 2
    angle = np.arange(pack, dtype=np.float32)[:, None] * (
        np.float32(10000.0) ** (-np.arange(0, ROT, 2, dtype=np.float32) / np.float32(ROT))
    )
    angle = angle.astype(np.float32)
    tables = np.zeros((3, pack, 2, HEAD_DIM), np.float32)
    tables[0] = 1.0
    tables[0, :, :, :half] = tables[0, :, :, half:ROT] = np.cos(angle)[:, None]
    tables[1, :, :, :half] = -np.sin(angle)[:, None]
    tables[2, :, :, half:ROT] = np.sin(angle)[:, None]
    return tables.reshape(3, pack, PAIR)


def shards(
    inputs,
    cotangent,
    segments,
    pack_length,
    norm_gain,
    norm_shift,
    qkv_weight,
    qv_bias,
    proj_weight,
    proj_bias,
    up_weight,
    up_bias,
    down_weight,
    down_bias,
):
    micros, pack, width = inputs.shape
    layers = qkv_weight.shape[0]
    extra = lax.axis_size("e")
    position = jnp.arange(pack)
    is_live = position[None, :] < pack_length
    causal = position[:, None] >= position[None, :]
    diagonal = position[:, None] == position[None, :]
    allowed = (
        (segments[:, :, None] == segments[:, None, :])
        & causal
        & (is_live[:, None, :] | diagonal)
    )
    mask = jnp.where(allowed, 0.0, MASKED).astype(BF16)
    mask = jnp.pad(mask, ((0, 0), (0, 0), (0, -pack % 128)))

    qkv_mine, up_mine = refold(qkv_weight, extra), refold(up_weight, extra)
    proj_mine, down_mine = refold(proj_weight, extra), refold(down_weight, extra)
    count = qkv_mine.shape[1]
    qkv_parts = jnp.moveaxis(split_heads(qkv_mine, 3), 3, 0).reshape(layers, RANKS, count, -1)
    up_parts = jnp.moveaxis(split_columns(up_mine), 3, 0).reshape(layers, RANKS, count, -1)
    parts = jnp.concatenate([qkv_parts, up_parts], axis=-1)

    def ranks(value):
        return jnp.moveaxis(value, 3, 0).reshape(layers, RANKS, -1)

    qv = at_place(refold(qv_bias, extra))
    upb = at_place(refold(up_bias, extra))
    q_rows, v_rows = ranks(split_heads(qv[:, :width], 1)), ranks(split_heads(qv[:, width:], 1))
    by_rank = [q_rows, jnp.zeros_like(q_rows), v_rows, ranks(split_columns(upb))]
    by_rank = jnp.concatenate(by_rank, axis=-1)
    by_rank = jnp.pad(by_rank, ((0, 0), (0, 0), (0, width - by_rank.shape[-1])))
    whole = [
        at_place(refold(norm_gain, extra)),
        at_place(refold(norm_shift, extra)),
        at_place(refold(proj_bias, extra).astype(F32) + refold(down_bias, extra).astype(F32)),
        jnp.zeros((layers, width), F32),
    ]
    small = jnp.concatenate([by_rank, jnp.stack(whole, axis=1)], axis=1)
    small = small.reshape(layers * SLOTS, width)

    live = is_live[:, :, None].astype(BF16)
    out, input_grad, cat_grad, down_grad, proj_grad, small_grad = run_layers(
        parts,
        down_mine,
        proj_mine,
        inputs.reshape(micros * pack, width),
        (cotangent * live).reshape(micros * pack, width),
        mask,
        small,
        jnp.asarray(rope_tables(pack)),
    )
    cat_grad = cat_grad.reshape(layers, 2, 2, 2, count, -1)
    qkv_grad = jnp.moveaxis(cat_grad[..., :QKV], 0, 3).reshape(
        2, 2, 2, layers, count, 3, 2, HEAD_DIM
    )
    up_grad = jnp.moveaxis(cat_grad[..., QKV:], 0, 3).reshape(2, 2, 2, layers, count, 2, 2, -1)
    small_grad = small_grad.reshape(layers, SLOTS, width)
    if extra > 1:
        small_grad = lax.psum(small_grad, "e")
    by_rank = jnp.moveaxis(small_grad[:, :RANKS].reshape(layers, 2, 2, 2, width), 0, 3)

    def heads_of(start):
        part = by_rank[..., start : start + PAIR]
        return join_heads(part.reshape(2, 2, 2, layers, 1, 2, HEAD_DIM))

    upb_grad = by_rank[..., QKV : QKV + up_parts.shape[-1]]
    upb_grad = join_columns(upb_grad.reshape(2, 2, 2, layers, 2, 2, -1))
    qvb_grad = jnp.concatenate([heads_of(0), heads_of(2 * PAIR)], axis=1)

    def own_share(value):
        size = value.shape[1] // (32 * extra)
        return lax.dynamic_slice_in_dim(value, lax.axis_index(AXES) * size, size, 1)

    bias_grad = own_share(small_grad[:, RANKS + 2])
    return (
        out.reshape(micros, pack, width),
        input_grad.reshape(micros, pack, width),
        own_share(small_grad[:, RANKS]),
        own_share(small_grad[:, RANKS + 1]),
        unfold(join_heads(qkv_grad).astype(F32), extra),
        own_share(qvb_grad),
        unfold(proj_grad, extra),
        bias_grad,
        unfold(join_columns(up_grad).astype(F32), extra),
        own_share(upb_grad),
        unfold(down_grad, extra),
        bias_grad,
    )


def solution(mesh):
    devices = mesh.devices.size
    fine = Mesh(mesh.devices.reshape(devices // 32, 2, 2, 2, 2, 2), AXES)
    cube, flat = P(None, AXES, None), P(None, AXES)
    placed = (cube, cube, flat, flat, flat, flat, cube, flat, cube, flat, cube, flat, cube, flat)
    given = (cube, cube, flat, flat, cube, flat, cube, flat, cube, flat, cube, flat)
    return jax.shard_map(shards, mesh=fine, in_specs=placed, out_specs=given, check_vma=False)
```

time: 706 us -> 378 us (0.54)
  Pallas kernels: 0 us -> 347 us
  waiting for transfers between devices: 277 us -> 0 us
  local copies, waits for them, and re-layouts: 158 us -> 20.6 us
  starting transfers between devices: 107 us -> 0 us
  matrix products: 74.1 us -> 0 us
  other arithmetic: 80.2 us -> 8.69 us
    pallas_call x0 -> x1, Pallas kernels: none -> 347 us  [run_layers(): pl.pallas_call(layers_kernel, out_shape=(shape((rows, width), BF16), shap...]
    ppermute x106 -> x0, waiting for transfers between devices: 277 us -> none  [swap(): return lax.ppermute(value, tuple(sorted(axes, key=AXES.index)), pairs)]
    ppermute x106 -> x0, starting transfers between devices: 107 us -> none  [swap(): return lax.ppermute(value, tuple(sorted(axes, key=AXES.index)), pairs)]
    dot_general x34 -> x0, matrix products: 69.6 us -> none  [the longest x24 58.7 us: dot(): lax.dot_general(a, b, (contract, ((), ())), preferred_element_type=F32)]
    unnamed x258 -> x23, local copies, waits for them, and re-layouts: 39.2 us -> 3.9 us
    another operation x42 -> x2, other arithmetic: 31.9 us -> 1.39 us  [shards(): small = jnp.concatenate([by_rank, jnp.stack(whole, axis=1)], axis=1)]
    slice x20 -> x5, local copies, waits for them, and re-layouts: 20.2 us -> 0.04 us  [the longest x1 0.02 us: shards(): bias_grad = own_share(small_grad[:, RANKS + 2])]
    convert_element_type x37 -> x6, local copies, waits for them, and re-layouts: 26 us -> 7.84 us  [the longest x3 4.55 us: shards(): join_heads(qkv_grad).astype(F32)]
  transfers between devices with their start and end apart: 106 -> 0, of which waited for: 51 -> 0; matrix products, arithmetic and copies ran while one was open for 29% -> 0% of each run, Pallas kernels for 0% -> 0%
where the time goes in v3:
time: 378 us; the launch traced here: 377 us
  Pallas kernels  347 us (92%)
  local copies, waits for them, and re-layouts  20.6 us (5%)
  other arithmetic  8.69 us (2%)
    pallas_call x1, Pallas kernels, run_layers(): pl.pallas_call(layers_kernel, out_shape=(shape((rows, width), BF16), shap...  347 us

profile of v3, /device:TPU:0, one launch (start us, length us, event | category | flops | bytes accessed | tf_op | source)
XLA Modules:
  0.0 377.2 jit_solution(7210660735579374930)
XLA Ops:
  0.6 0.0 copy-start.3
  0.7 0.0 copy-start.5
  0.7 0.7 bitcast_convert_fusion.1
  1.4 0.7 bitcast_convert_fusion
  2.1 0.7 convert_element_type.61
  2.7 0.7 convert_add_fusion
  3.4 0.7 iota_compare_fusion.2
  4.2 0.2 dynamic_update_slice.22
  4.3 0.2 dynamic_update_slice.21
  4.5 0.2 dynamic_update_slice.20
  4.7 0.2 dynamic_update_slice.18
  4.9 0.1 reshape.193
  5.0 0.1 reshape.194
  5.1 0.1 reshape.195
  5.2 0.1 reshape.196
  5.3 0.9 select_convert_fusion
  6.2 0.6 pad.8.mask
  6.8 0.7 constant_dynamic-update-slice_fusion
  7.6 0.1 concatenate.14
  7.7 0.7 reshape.199.small
  8.4 0.0 copy-done.5
  8.4 0.8 broadcast_multiply_fusion
  9.2 0.0 copy-done.3
  9.2 0.4 reshape.189
  9.6 0.5 copy.67
  10.1 0.2 reshape.190
  10.3 0.0 copy-done.6
  10.3 0.5 reshape.187
  10.8 0.8 copy.66
  11.6 0.5 reshape.188
  12.1 1.0 pad_maximum_fusion.parts
  13.1 346.9 %shard_map.241 = (bf16[192,1024]{1,0:T(8,128)(2,1)}, f32[192,1024]{1,0:T(8,128)}, bf16[2,8,32,896]{3,2,1,0:T(8,128)(2,1)}, f32[2,128,1024]{2,1,0:T(8,128)}, f32[2,32,1024]{2,1,0:T(8,128)}, /*index=5*/f32[24,1024]{1,0:T(8,128)}) custom-call(bf16[2,8,32,896]{3,2,1,0:T(8,128)(2,1)} %pad_maximum_fusion.parts, bf16[2,128,1024]{2,1,0:T(8,128)(2,1)} %down.1, ...), custom_call_target="tpu_custom_call" | custom-call | tf_op jit(solution)/shard_map/pallas_call | solution.py:869
  360.0 0.0 copy-start.1
  360.0 1.0 reshape.202
  361.1 0.1 copy.59
  361.1 0.1 constant_dynamic-slice_fusion.1
  361.2 0.6 constant_dynamic-slice_fusion.2
  361.9 0.6 constant_dynamic-slice_fusion.3
  362.6 0.6 constant_dynamic-slice_fusion
  363.2 0.1 reshape.207
  363.3 0.1 reshape.208
  363.4 0.1 reshape.205
  363.5 0.1 reshape.206
  363.6 0.6 fusion
  364.2 1.1 convert_bitcast_fusion.1
  365.3 0.0 copy-done.1
  365.3 0.1 convert_bitcast_fusion
  365.4 0.7 reshape.216
  366.1 0.8 copy.65
  366.9 1.8 reshape.214
  368.7 1.0 reshape.215
  369.7 1.2 copy.64
  371.0 0.0 copy-start.4
  371.0 0.0 copy-start.2
  371.0 2.3 reshape.213
  373.3 0.0 copy-done.8
  373.3 0.6 copy.79
  373.9 0.0 copy-done.4
  373.9 0.7 copy.80
  374.6 0.0 copy-done.2
  374.6 0.9 copy.81
  375.5 0.0 copy-done.7
  375.5 0.7 copy.82
  376.2 1.0 copy.83
  (31 shorter events, 0.4 us)
Async XLA Ops:
  0.6 8.6 %copy-start.3 = (bf16[2,32,4096]{2,1,0:T(8,128)(2,1)S(1)}, bf16[2,32,4096]{2,1,0:T(8,128)(2,1)}, u32[]{:S(2)}) copy-start(bf16[2,32,4096]{2,1,0:T(8,128)(2,1)} %param.25) | copy-start | bytes 1572868
  0.7 7.7 %copy-start.5 = (bf16[2,96,1024]{2,1,0:T(8,128)(2,1)S(1)}, bf16[2,96,1024]{2,1,0:T(8,128)(2,1)}, u32[]{:S(2)}) copy-start(bf16[2,96,1024]{2,1,0:T(8,128)(2,1)} %param.16) | copy-start | bytes 1179652
  9.2 1.1 copy-start.6
  360.0 5.3 %copy-start.1 = (bf16[2,8,32,896]{3,2,1,0:T(8,128)(2,1)S(1)}, bf16[2,8,32,896]{3,2,1,0:T(8,128)(2,1)}, u32[]{:S(2)}) copy-start(bf16[2,8,32,896]{3,2,1,0:T(8,128)(2,1)} %get-tuple-element.21) | copy-start | bytes 2752516
  361.2 12.1 %copy-start.8 = (f32[2,1,32]{2,1,0:T(1,128)}, f32[2,1,32]{2,1,0:T(1,128)S(1)}, u32[]{:S(2)}) copy-start(f32[2,1,32]{2,1,0:T(1,128)S(1)} %constant_dynamic-slice_fusion.1) | copy-start | bytes 772
  371.0 2.9 copy-start.4
  371.0 3.7 copy-start.2
  373.3 2.2 copy-start.7
  373.3 2.9 copy-start

commit v4 on v3

v4 whole, which is shorter than its diff:
```python
import math

import jax
import jax.numpy as jnp
import numpy as np
from jax import lax
from jax.experimental import pallas as pl
from jax.experimental.pallas import tpu as pltpu
from jax.sharding import Mesh
from jax.sharding import PartitionSpec as P

HEAD_DIM = 64
ROT = 16
EPS = 1e-05
MASKED = -1e30

AXES = ("e", "zh", "zl", "x", "y", "c")
T1, T2, D1, D2 = "y", "zl", "zh", "x"
TP = (T1, T2, "c")
RANKS = 8
NEAR = (("c",), (T1,), (T2,), (T1, "c"), (T2, "c"), (T1, T2), (T1, T2, "c"))
FAR = ((D1,), (D2,))
SMALL_AXES = ("c", T1, T2, D1, D2)

F32, BF16 = jnp.float32, jnp.bfloat16
MESH = pl.DeviceIdType.MESH

PAIR = 2 * HEAD_DIM
QKV = 3 * PAIR


def dot(a, b, contract):
    return lax.dot_general(a, b, (contract, ((), ())), preferred_element_type=F32)


class Links:
    def __init__(self, send_sem, recv_sem):
        self.place = {axis: lax.axis_index(axis) for axis in AXES}
        self.send_sem, self.recv_sem, self.used = send_sem, recv_sem, 0

    def reserve(self, count):
        self.used += count
        return self.used - count

    def peer(self, axes):
        return {axis: 1 - self.place[axis] for axis in axes}

    def meet(self):
        barrier = pltpu.get_barrier_semaphore()
        for axes in NEAR + FAR:
            pl.semaphore_signal(barrier, inc=1, device_id=self.peer(axes), device_id_type=MESH)
        pl.semaphore_wait(barrier, len(NEAR) + len(FAR))

    def copy(self, source, target, device, slot=None):
        if slot is None:
            slot = self.reserve(1)
        if not isinstance(device, dict):
            device = self.peer(device)
        return pltpu.make_async_remote_copy(
            src_ref=source,
            dst_ref=target,
            send_sem=self.send_sem.at[slot],
            recv_sem=self.recv_sem.at[slot],
            device_id=device,
            device_id_type=MESH,
        )


def rank_of(place):
    return place[T1] * 4 + place[T2] * 2 + place["c"]


def block_of(place):
    index = place["zh"]
    for axis in AXES[2:]:
        index = index * 2 + place[axis]
    return index


def flipped(place, axes):
    return {a: (1 - i if a in axes else i) for a, i in place.items()}


class Rows:
    def __init__(self, links, buffer):
        self.links, self.buffer, self.base = links, buffer, links.reserve(8)

    def core(self, j):
        return self.links.copy(
            self.buffer.at[j, 0], self.buffer.at[j, 1], ("c",), self.base + j
        )

    def chip(self, j):
        source, axes = (0, (T1,)) if isinstance(j, jax.Array) else ((0, 0, 0, 1)[j], (T2,) if j == 1 else (T1,))
        return self.links.copy(
            self.buffer.at[source, 0], self.buffer.at[j, 0], axes, self.base + 4 + j
        )

    def start(self):
        self.core(0).start()
        self.chip(1).start()
        self.chip(2).start()

    def forward(self):
        self.chip(1).wait_recv()
        self.chip(3).start()
        self.core(1).start()

    def arrive(self, j):
        @pl.when(j > 1)
        def _():
            self.chip(j).wait_recv()
            self.core(j).start()

        self.core(j).wait_recv()

    def finish(self):
        for j in range(4):
            self.core(j).wait_send()
        for j in range(1, 4):
            self.chip(j).wait_send()


def far_first(i):
    return 3 - i


def near_first(i):
    return i + 1 - 3 * (i // 3) - (3 - i) // 3


class Sums:
    def __init__(self, links, core_in, chip_in, core_out, chip_out):
        self.links, self.base = links, links.reserve(8)
        self.core_in, self.chip_in, self.core_out, self.chip_out = core_in, chip_in, core_out, chip_out

    def core(self, j):
        return self.links.copy(
            self.core_out.at[j], self.core_in.at[j], ("c",), self.base + j
        )

    def chip(self, j):
        return self.links.copy(
            self.chip_out.at[j - 1],
            self.chip_in.at[j - 1],
            (T2,) if j == 1 else (T1,),
            self.base + 4 + j,
        )

    def run(self, before, term, scratch, own, order):
        rows = own.shape[0]

        def pass_on(j):
            self.core(j).wait_recv()
            for m in range(2):
                at = pl.ds(m * (rows // 2), rows // 2)
                total = scratch[1, at] + self.core_in[j, at].astype(F32)
                for k in (1, 2, 3):

                    @pl.when(j == k)
                    def _():
                        value = total
                        if k == 1:
                            if m == 0:
                                self.chip(3).wait_recv()
                            value = value + self.chip_in[2, at].astype(F32)
                        self.chip_out[k - 1, at] = value.astype(BF16)
                        if m == 1:
                            self.chip(k).start()

                @pl.when(j == 0)
                def _():
                    own[at] = total

        def step(i, carry):
            j = order(i)
            before(i, j)

            @pl.when(i > 0)
            def _():
                pass_on(order(i - 1))

            term(j, scratch.at[1])
            self.core_out[j] = scratch[1, rows:].astype(BF16)
            self.core(j).start()
            return carry

        lax.fori_loop(0, 4, step, 0)
        pass_on(order(3))

    def total(self, own):
        for j in (1, 2):
            self.chip(j).wait_recv()
        for j in range(4):
            self.core(j).wait_send()
        for j in (1, 2, 3):
            self.chip(j).wait_send()

        def at(rows):
            value = own[rows]
            for j in (1, 2):
                value = value + self.chip_in[j - 1, rows].astype(F32)
            return value

        return at


def mean_of(value):
    return jnp.sum(value, axis=-1, keepdims=True) * (1.0 / value.shape[-1])


def normalise(stream):
    centred = stream - mean_of(stream)
    inverse = lax.rsqrt(mean_of(centred * centred) + EPS)
    return centred * inverse, inverse


def layers_kernel(
    qkv,
    up,
    down,
    proj,
    inputs,
    cotangent,
    marks,
    small,
    tables,
    outputs,
    input_grad,
    gain_out,
    shift_out,
    qkv_out,
    qvb_out,
    proj_out,
    bias_out,
    up_out,
    upb_out,
    down_out,
    parts,
    cat_all,
    dp_all,
    hid,
    rnd,
    mask_all,
    qkv_kept,
    probs,
    ca,
    slope,
    mdud,
    scratch,
    core_in,
    chip_in,
    core_out,
    chip_out,
    own,
    stream_two,
    up_one,
    small_sum,
    small_in,
    sums,
    grad_sum,
    cat_own,
    cat_s1,
    cat_r1,
    cat_s2,
    cat_r2,
    cat_a,
    dp_grad,
    down_s1,
    down_r1,
    down_s2,
    down_r2,
    proj_s1,
    proj_r1,
    proj_s2,
    proj_r2,
    proj_s3,
    proj_r3,
    send_sem,
    recv_sem,
    own_sem,
    free_sem,
    fetch_sem,
):
    links = Links(send_sem, recv_sem)
    me = links.place
    rank, block, slot = rank_of(me), block_of(me), me[D2] * 2 + me[D1]
    mine = me["c"] == me[D2]
    others = jnp.logical_not(mine)
    layers, wide = parts.shape[0], parts.shape[3]
    micros, lanes = marks.shape
    rows, width = inputs.shape
    pack = rows // micros
    count = qkv.shape[1]
    lift = wide - QKV
    scale = 1.0 / math.sqrt(HEAD_DIM)
    lane = lax.broadcasted_iota(jnp.int32, (pack, PAIR), 1)
    first_head = lane < HEAD_DIM

    def ranks_row(layer):
        return layer * RANKS + rank

    def named_row(layer, index):
        return layers * RANKS + 3 * layer + index

    def bias_row(index):
        return small_sum[len(SMALL_AXES), pl.ds(index, 1), :]

    pieces = 3 + up.shape[2] // width
    raw = [core_out.at[i // 6, pl.ds(i % 6 * count, count)] for i in range(layers * pieces)]
    final = [scratch.at[i // 8, pl.ds(i % 8 * count, count)] for i in range(layers * pieces)]

    def fetch_columns():
        copies = []
        for i in range(layers * pieces):
            layer, k = i // pieces, i % pieces
            source = qkv.at[layer, :, pl.ds(k * width, width)] if k < 3 else up.at[
                layer, :, pl.ds((k - 3) * width, width)
            ]
            copies.append(pltpu.make_async_copy(source, raw[i], fetch_sem.at[i]))
        return copies

    def return_columns(layer):
        copies = []
        for k in range(pieces):
            i = layer * pieces + k
            target = qkv_out.at[layer, :, pl.ds(k * width, width)] if k < 3 else up_out.at[
                layer, :, pl.ds((k - 3) * width, width)
            ]
            copies.append(pltpu.make_async_copy(final[i], target, fetch_sem.at[i]))
        return copies

    lane_row = lax.broadcasted_iota(jnp.int32, (count, PAIR), 1) < HEAD_DIM

    def shared(one, other):
        one, other = one.astype(F32), other.astype(F32)
        return (
            jnp.where(lane_row, one, pltpu.roll(other, HEAD_DIM, 1)),
            jnp.where(lane_row, pltpu.roll(one, HEAD_DIM, 1), other),
        )

    def columns_by_rank(layer):
        base = layer * pieces
        for p in range(3):
            for zl in range(2):
                for x in range(2):
                    tiles = [
                        raw[base + p][:, (zh * 4 + zl * 2 + x) * PAIR : (zh * 4 + zl * 2 + x + 1) * PAIR]
                        for zh in range(2)
                    ]
                    for y, tile in enumerate(shared(*tiles)):
                        parts[layer, y * 4 + zl * 2 + x, :, p * PAIR : (p + 1) * PAIR] = tile.astype(BF16)
        size = up.shape[2] // 32
        for b in range(32):
            zh, zl, x, y, c = b // 16, b // 8 % 2, b // 4 % 2, b // 2 % 2, b % 2
            k, at = b * size // width, b * size % width
            to = QKV + (x * 2 + zh) * size
            parts[layer, y * 4 + zl * 2 + c, :, to : to + size] = raw[base + 3 + k][:, at : at + size]

    def columns_by_name(layer):
        base = layer * pieces
        for p in range(3):
            for zl in range(2):
                for x in range(2):
                    tiles = [
                        parts[layer, y * 4 + zl * 2 + x, :, p * PAIR : (p + 1) * PAIR] for y in range(2)
                    ]
                    for zh, tile in enumerate(shared(*tiles)):
                        at = (zh * 4 + zl * 2 + x) * PAIR
                        final[base + p][:, at : at + PAIR] = tile
        size = up.shape[2] // 32
        for b in range(32):
            zh, zl, x, y, c = b // 16, b // 8 % 2, b // 4 % 2, b // 2 % 2, b % 2
            k, at = b * size // width, b * size % width
            to = QKV + (x * 2 + zh) * size
            tile = parts[layer, y * 4 + zl * 2 + c, :, to : to + size]
            final[base + 3 + k][:, at : at + size] = tile.astype(F32)

    head_rank = me["c"] * 4 + me["x"] * 2 + me["y"]
    head_cut = pl.ds(pl.multiple_of(me["zh"] * 2 * PAIR, PAIR), PAIR)
    up_size = up.shape[2] // 32
    up_cut = pl.ds(pl.multiple_of(QKV + slot * up_size, PAIR), up_size)

    ranked = layers * RANKS
    named = small_sum.shape[1] - ranked
    rank_row = lax.broadcasted_iota(jnp.int32, (RANKS, PAIR), 0)

    def spread_small():
        small_sum[0, :ranked] = jnp.zeros((ranked, width), F32)
        small_sum[0, ranked:] = pltpu.roll(small[:named], block * (width // 32), 1)
        for layer in range(layers):
            at = slice(layer * RANKS, (layer + 1) * RANKS)
            pair = jnp.broadcast_to(small[named + layer : named + layer + 1, :PAIR], (RANKS, PAIR))
            pair = pltpu.roll(pair, me["zl"] * HEAD_DIM, 1)
            small_sum[0, at, head_cut] = jnp.where(rank_row == head_rank, pair, 0.0)
            more = named + layers + layer
            more = jnp.broadcast_to(small[more : more + 1, :up_size], (RANKS, up_size))
            small_sum[0, at, up_cut] = jnp.where(rank_row == rank, more, 0.0)

    def own_small(total):
        share = width // 32
        moved = pltpu.roll(total[ranked:], (32 - block) % 32 * share, 1)
        for layer in range(layers):
            start = layer * 3
            gain_out[layer : layer + 1] = moved[start : start + 1, :share]
            shift_out[layer : layer + 1] = moved[start + 1 : start + 2, :share]
            bias_out[layer : layer + 1] = moved[start + 2 : start + 3, :share]
            at = slice(layer * RANKS, (layer + 1) * RANKS)
            pair = pltpu.roll(total[at, head_cut], me["zl"] * HEAD_DIM, 1)
            pair = jnp.where(rank_row == head_rank, pair, 0.0)
            qvb_out[layer : layer + 1] = jnp.sum(pair, axis=0, keepdims=True)[:, :HEAD_DIM]
            more = jnp.where(rank_row == rank, total[at, up_cut], 0.0)
            upb_out[layer : layer + 1] = jnp.sum(more, axis=0, keepdims=True)

    def build_mask(m):
        row = lax.broadcasted_iota(jnp.int32, (lanes, lanes), 0)
        column = lax.broadcasted_iota(jnp.int32, (lanes, lanes), 1)
        across = jnp.broadcast_to(marks[pl.ds(m, 1), :], (lanes, lanes))
        length = marks[pl.ds(m, 1), pack : pack + 1]
        live = column.astype(F32) < length
        allowed = (across.T == across) & (column <= row) & (live | (column == row))
        hidden = jnp.where(allowed, 0.0, MASKED).astype(BF16)
        mask_all[0, 0, m] = hidden[:pack]
        live = lax.broadcasted_iota(jnp.int32, (pack, 1), 0).astype(F32) < length
        at = pl.ds(m * pack, pack)
        rnd[0, 0, at] = jnp.where(live, cotangent[at].astype(F32), 0.0).astype(BF16)

    class Piece:
        def __init__(self, own, at):
            here, there = at(me["zh"]), at(1 - me["zh"])
            self.one = links.copy(here if own is None else own, here, (D1,))
            self.near = links.copy(here if own is None else own, here, (D2,))
            self.far = links.copy(there, there, (D2,))

        def start(self):
            self.one.start()

        def start_near(self):
            self.near.start()

        def step(self):
            self.one.wait()

        def start_far(self):
            self.far.start()

        def done(self):
            self.near.wait()
            self.far.wait()

    class Heads:
        def __init__(self, layer):
            self.layer = layer
            count = proj.shape[1]
            half = dp_all.at[layer, pl.ds(me["zh"] * HEAD_DIM + me["c"] * count, count)]
            self.to_core = links.copy(proj.at[layer], half, ("c",))
            self.stays = pltpu.make_async_copy(proj.at[layer], half, own_sem.at[layer, 2])
            head = dp_all.at[layer, pl.ds(me["zh"] * HEAD_DIM, HEAD_DIM)]
            self.one = links.copy(head, head, (D1,))
            heads = dp_all.at[layer, pl.ds(0, PAIR)]
            self.two = links.copy(heads, heads, (D2,))

        def prepare(self):
            @pl.when(mine)
            def _():
                self.stays.start()
                self.stays.wait()

            @pl.when(others)
            def _():
                self.to_core.start()
                self.to_core.wait_send()

        def start(self):
            @pl.when(mine)
            def _():
                self.to_core.wait_recv()
                self.one.start()

        def step(self):
            @pl.when(mine)
            def _():
                self.one.wait()

        def start_far(self):
            @pl.when(mine)
            def _():
                self.two.start()

        def done(self):
            @pl.when(mine)
            def _():
                self.two.wait_send()

            @pl.when(others)
            def _():
                self.two.wait_recv()

    class Weights:
        def __init__(self, layer):
            self.layer = layer
            size = down.shape[1]
            self.keep = [
                pltpu.make_async_copy(
                    parts.at[layer, rank], cat_all.at[layer, block], own_sem.at[layer, 0]
                ),
                pltpu.make_async_copy(
                    down.at[layer], self.down_rows(me["zh"], 0, size), own_sem.at[layer, 1]
                ),
            ]
            self.trades = [
                links.copy(
                    parts.at[layer, rank_of(flipped(me, axes))], cat_all.at[layer, block], axes
                )
                for axes in NEAR
            ]
            self.cat = [
                Piece(None, lambda zh, zl=zl, h=h: self.cat_rows(zh, zl, h))
                for zl in range(2)
                for h in range(2)
            ]
            half = size // 2
            self.down = [
                Piece(
                    down.at[layer, pl.ds(h * half, half)],
                    lambda zh, h=h: self.down_rows(zh, h * half, half),
                )
                for h in range(2)
            ]
            self.heads = Heads(layer)

        def cat_rows(self, zh, zl, h):
            return cat_all.at[self.layer, pl.ds(zh * 16 + zl * 8 + me["x"] * 4 + 2 * h, 2)]

        def down_rows(self, zh, start, count):
            size = down.shape[1]
            return dp_all.at[
                self.layer, pl.ds(PAIR + (me[D2] * 2 + zh) * size + start, count)
            ]

        def start_trades(self):
            self.keep[0].start()
            for copy in self.trades:
                copy.start()

        def traded(self):
            self.keep[0].wait()
            for copy in self.trades:
                copy.wait()

        def cat_done(self):
            for piece in self.cat:
                piece.done()

        def rows_done(self):
            self.keep[1].wait()
            for piece in self.down:
                piece.done()
            self.heads.done()

    def turn(value, sign):
        return (
            value * tables[0]
            + pltpu.roll(value, PAIR - ROT // 2, 1) * (tables[1] * sign)
            + pltpu.roll(value, ROT // 2, 1) * (tables[2] * sign)
        )

    def by_head(value):
        zero = jnp.zeros_like(value)
        return jnp.concatenate(
            [jnp.where(first_head, value, zero), jnp.where(first_head, zero, value)], axis=0
        )

    def of_heads(value):
        return jnp.where(first_head, value[:pack], value[pack:])

    def forward(layer, j):
        hidden = hid[layer, j].reshape(2 * rows, width)
        for cut in (slice(0, QKV), slice(QKV, wide)):
            columns = cat_all[layer, :, :, cut].reshape(width, -1)
            scratch[0, :, cut] = dot(hidden, columns, ((1,), (0,)))
        bias = bias_row(ranks_row(layer))

        def each(p, carry):
            at = pl.ds(pl.multiple_of(p * pack, pack), pack)
            turned = scratch[0, at, :QKV] + bias[:, :QKV]
            queries = turn(turned[:, :PAIR], 1.0).astype(BF16)
            keys = turn(turned[:, PAIR : 2 * PAIR], 1.0).astype(BF16)
            values = turned[:, 2 * PAIR :].astype(BF16)
            qkv_kept[layer, j, at, :PAIR] = queries
            qkv_kept[layer, j, at, PAIR : 2 * PAIR] = keys
            qkv_kept[layer, j, at, 2 * PAIR :] = values
            hide = mask_all[j, p // micros, p % micros][:, :pack].astype(F32)
            scores = dot(by_head(queries), keys, ((1,), (1,))) * scale
            scores = scores + jnp.concatenate([hide, hide], axis=0)
            shifted = jnp.exp(scores - jnp.max(scores, axis=-1, keepdims=True))
            soft = shifted / jnp.sum(shifted, axis=-1, keepdims=True)
            soft = soft.astype(BF16)
            probs[layer, j, p] = soft
            ca[layer, j, at, :PAIR] = of_heads(dot(soft, values, ((1,), (0,)))).astype(BF16)
            for start in range(QKV, wide, 2 * PAIR):
                cut = slice(start, start + 2 * PAIR)
                raised = scratch[0, at, cut] + bias[:, cut]
                cdf = 0.5 * (1.0 + lax.erf(raised * 0.7071067811865476))
                density = jnp.exp(-0.5 * raised * raised) * 0.3989422804014327
                to = start - QKV
                ca[layer, j, at, PAIR + to : PAIR + to + 2 * PAIR] = (raised * cdf).astype(BF16)
                slope[layer, j, at, to : to + 2 * PAIR] = (cdf + raised * density).astype(BF16)
            return carry

        lax.fori_loop(0, 2 * micros, each, 0)

    def backward(layer, j):
        rounded = rnd[j].reshape(2 * rows, width)
        for cut in (slice(0, PAIR), slice(PAIR, PAIR + lift)):
            scratch[0, :, cut] = dot(rounded, dp_all[layer, cut], ((1,), (1,)))

        def each(p, carry):
            at = pl.ds(pl.multiple_of(p * pack, pack), pack)
            for start in range(0, lift, 2 * PAIR):
                cut = slice(start, start + 2 * PAIR)
                grown = scratch[0, at, PAIR + start : 3 * PAIR + start]
                grown = (grown * slope[layer, j, at, cut].astype(F32)).astype(BF16)
                mdud[j, at, QKV + start : QKV + start + 2 * PAIR] = grown
                sums[:, QKV + start : QKV + start + 2 * PAIR] += jnp.sum(
                    grown.astype(F32).reshape(pack // 8, 8, 2 * PAIR), axis=0
                )
            context = by_head(scratch[0, at, :PAIR].astype(BF16))
            queries = by_head(qkv_kept[layer, j, at, :PAIR])
            keys = qkv_kept[layer, j, at, PAIR : 2 * PAIR]
            values = qkv_kept[layer, j, at, 2 * PAIR :]
            kept = probs[layer, j, p]
            soft = kept.astype(F32)
            prob_delta = dot(context, values, ((1,), (1,)))
            row_delta = jnp.sum(soft * prob_delta, axis=-1, keepdims=True)
            score_delta = (soft * (prob_delta - row_delta)).astype(BF16)
            value_delta = dot(kept, context, ((0,), (0,)))
            query_delta = of_heads(dot(score_delta, keys, ((1,), (0,)))) * scale
            key_delta = dot(score_delta, queries, ((0,), (0,))) * scale
            three = (turn(query_delta, -1.0), turn(key_delta, -1.0), value_delta)
            for i, delta in enumerate(three):
                delta = delta.astype(BF16)
                cut = slice(i * PAIR, (i + 1) * PAIR)
                mdud[j, at, cut] = delta
                sums[:, cut] += jnp.sum(delta.astype(F32).reshape(pack // 8, 8, PAIR), axis=0)
            return carry

        lax.fori_loop(0, 2 * micros, each, 0)

    halves = (slice(0, width // 2), slice(width // 2, width))

    def out_term(layer):
        def put(j, target):
            for cut in halves:
                target[:, cut] = dot(ca[layer, j], dp_all[layer, :, cut], ((1,), (0,)))

        return put

    def hidden_term(layer):
        def put(j, target):
            for half, cut in enumerate(halves):
                columns = cat_all[layer, pl.ds(16 * half, 16)].reshape(width // 2, wide)
                target[:, cut] = dot(mdud[j], columns, ((1,), (1,)))

        return put

    class Grads:
        def __init__(self, layer):
            self.layer = layer
            self.down_one = links.copy(down_s1, down_r1.at[layer], (D2,))
            self.down_two = links.copy(down_s2, down_r2.at[layer], (D1,))
            self.proj_one = links.copy(proj_s1, proj_r1.at[layer], (D2,))
            self.proj_two = links.copy(proj_s2, proj_r2.at[layer], (D1,))
            self.proj_three = links.copy(proj_s3, proj_r3.at[layer], ("c",))
            self.cat_one = [
                [links.copy(cat_s1.at[i, zl], cat_r1.at[layer, i, zl], (D2,)) for zl in range(2)]
                for i in range(2)
            ]
            self.cat_two = [
                links.copy(cat_s2.at[zl], cat_r2.at[layer, zl], (D1,)) for zl in range(2)
            ]
            self.trades = []
            for axes in NEAR:
                there = flipped(me, axes)
                part = cat_a.at[there["zl"], there["y"] * 2 + there["c"]]
                self.trades.append(links.copy(part, parts.at[layer, rank], axes))
            self.keep = pltpu.make_async_copy(
                cat_a.at[me["zl"], me["y"] * 2 + me["c"]], parts.at[layer, rank], own_sem.at[layer, 3]
            )

        def rows_terms(self, start, stop):
            layer = self.layer
            size = (stop - start) * 2 * rows
            kept = ca[layer, start:stop].reshape(size, PAIR + lift)
            for cut in halves:
                rounded = rnd[start:stop, :, :, cut].reshape(size, width // 2)
                for part in (pl.ds(PAIR, lift), pl.ds(0, PAIR)):
                    side = kept[:, PAIR:] if part.start else kept[:, :PAIR]
                    value = dot(side, rounded, ((0,), (0,)))
                    if start:
                        value = value + dp_grad[part, cut]
                    dp_grad[part, cut] = value

        def rows_one(self):
            half = lift // 2
            down_s1[...] = dp_grad[pl.ds(PAIR + (1 - me[D2]) * half, half)].astype(BF16)
            self.down_one.start()

            @pl.when(others)
            def _():
                proj_s1[...] = dp_grad[pl.ds(0, PAIR)].astype(BF16)
                self.proj_one.start()

        def rows_two(self):
            layer = self.layer
            half, quarter = lift // 2, lift // 4
            base = PAIR + me[D2] * half
            self.down_one.wait()
            at = (1 - me[D1]) * quarter
            down_s2[...] = (
                dp_grad[pl.ds(base + at, quarter)]
                + down_r1[layer, pl.ds(at, quarter)].astype(F32)
            ).astype(BF16)
            self.down_two.start()

            @pl.when(others)
            def _():
                self.proj_one.wait_send()

            @pl.when(mine)
            def _():
                self.proj_one.wait_recv()
                at = (1 - me[D1]) * HEAD_DIM
                proj_s2[...] = (
                    dp_grad[pl.ds(at, HEAD_DIM)]
                    + proj_r1[layer, pl.ds(at, HEAD_DIM)].astype(F32)
                ).astype(BF16)
                self.proj_two.start()

        def rows_three(self):
            layer = self.layer
            half, quarter = lift // 2, lift // 4
            base = PAIR + me[D2] * half
            self.down_two.wait()
            at = me[D1] * quarter
            down_out[layer] = (
                dp_grad[pl.ds(base + at, quarter)]
                + down_r1[layer, pl.ds(at, quarter)].astype(F32)
                + down_r2[layer].astype(F32)
            )
            count = proj.shape[1]

            @pl.when(mine)
            def _():
                self.proj_two.wait()
                at = me[D1] * HEAD_DIM

                def half_of(which):
                    return (
                        dp_grad[pl.ds(at + which * count, count)]
                        + proj_r1[layer, pl.ds(at + which * count, count)].astype(F32)
                        + proj_r2[layer, pl.ds(which * count, count)].astype(F32)
                    )

                proj_out[layer] = half_of(me["c"])
                proj_s3[...] = half_of(1 - me["c"]).astype(BF16)
                self.proj_three.start()
                self.proj_three.wait_send()

            @pl.when(others)
            def _():
                self.proj_three.wait_recv()
                proj_out[layer] = proj_r3[layer].astype(F32)

        def cat_terms(self, i):
            layer = self.layer
            zh = me["zh"] if i else 1 - me["zh"]
            deltas = mdud[...].reshape(8 * rows, wide)
            for zl in range(2):
                start = pl.multiple_of((zh * 2 + zl) * (width // 4), width // 4)
                kept = hid[layer, :, :, :, pl.ds(start, width // 4)].reshape(8 * rows, width // 4)
                scratch[zl, : width // 4, :wide] = dot(kept, deltas, ((0,), (0,)))
            size = width // 8
            for zl in range(2):
                cat_s1[i, zl] = scratch[zl, pl.ds((1 - me["x"]) * size, size), :wide].astype(BF16)
                self.cat_one[i][zl].start()
                cat_own[i, zl] = scratch[zl, pl.ds(me["x"] * size, size), :wide]

        def cat_step_two(self, zl):
            layer = self.layer
            self.cat_one[0][zl].wait()
            cat_s2[zl] = (cat_own[0, zl] + cat_r1[layer, 0, zl].astype(F32)).astype(BF16)
            self.cat_two[zl].start()

        def cat_step_three(self, zl):
            layer = self.layer
            self.cat_one[1][zl].wait()
            self.cat_two[zl].wait()
            total = (
                cat_own[1, zl]
                + cat_r1[layer, 1, zl].astype(F32)
                + cat_r2[layer, zl].astype(F32)
            )
            cat_a[zl] = total.astype(BF16).reshape(cat_a.shape[1:])

        def cat_trade(self):
            for copy in self.trades:
                copy.start()
            self.keep.start()

        def cat_done(self):
            for copy in self.trades:
                copy.wait()
            self.keep.wait()

    def put_sums(index, value):
        grad_sum[pl.ds(index, 1), : value.shape[1]] = value

    def own_rows(layer, total, stream_at, up_at, put):
        gain = bias_row(named_row(layer, 0))
        gain_sum = jnp.zeros((1, width), F32)
        shift_sum = jnp.zeros((1, width), F32)
        for m in range(2 * micros):
            at = pl.ds(m * (rows // (2 * micros)), rows // (2 * micros))
            delta = total(at)
            normed, inverse = normalise(stream_at(at))
            gain_sum = gain_sum + jnp.sum(delta * normed, axis=0, keepdims=True)
            shift_sum = shift_sum + jnp.sum(delta, axis=0, keepdims=True)
            scaled = delta * gain
            put(
                at,
                up_at(at) + inverse * (scaled - mean_of(scaled) - normed * mean_of(scaled * normed)),
            )
        put_sums(named_row(layer, 0), gain_sum)
        put_sums(named_row(layer, 1), shift_sum)

    def bias_sums(layer):
        put_sums(ranks_row(layer), jnp.sum(sums[...], axis=0, keepdims=True))
        rounded = jnp.zeros((8, width), F32)
        for m in range(2 * micros):
            size = rows // (2 * micros)
            part = rnd[0, 0, pl.ds(m * size, size)].astype(F32)
            rounded = rounded + jnp.sum(part.reshape(size // 8, 8, width), axis=0)
        put_sums(named_row(layer, 2), jnp.sum(rounded, axis=0, keepdims=True))

    def give_back(turn_index):
        for axes in (("c",), (T1,), (T2,)):
            pl.semaphore_signal(
                free_sem.at[turn_index], inc=1, device_id=links.peer(axes), device_id_type=MESH
            )

    def await_places(turn_index):
        pl.semaphore_wait(free_sem.at[turn_index], 3)

    taken = [Weights(layer) for layer in range(layers)]
    grads = [Grads(layer) for layer in range(layers)]
    row_gathers = [Rows(links, hid.at[1]), Rows(links, mask_all), Rows(links, rnd)]
    hidden_two, rounded_one = Rows(links, hid.at[1]), Rows(links, rnd)
    sets = (core_in, chip_in, core_out, chip_out)
    out_one, delta_two, delta_one = Sums(links, *sets), Sums(links, *sets), Sums(links, *sets)
    out_two = Sums(links, *sets)

    def grad_stage(i):
        return grad_sum if i == 0 else small_sum.at[i - 1]

    small_copies = [
        links.copy(small_sum.at[i], small_in.at[i], (axis,)) for i, axis in enumerate(SMALL_AXES)
    ]
    grad_copies = [
        links.copy(grad_stage(i), small_in.at[i], (axis,)) for i, axis in enumerate(SMALL_AXES)
    ]

    chain = [taken[0].down[0]] + taken[0].cat + [taken[0].down[1], taken[0].heads]
    chain = chain + taken[1].cat + taken[1].down + [taken[1].heads]

    def pump(k):
        chain[k].step()
        if k + 2 < len(chain):
            chain[k + 2].start()
        chain[k].start_far()

    def small_step(i):
        small_copies[i].wait()
        small_sum[i + 1] = small_sum[i] + small_in[i]
        if i + 1 < len(SMALL_AXES):
            small_copies[i + 1].start()

    fetched = fetch_columns()
    for copy in fetched:
        copy.start()
    for one in taken:
        one.keep[1].start()
    spread_small()
    hid[1, 0, 0] = inputs[...]
    for copy in fetched[:pieces]:
        copy.wait()
    columns_by_rank(0)
    links.meet()
    taken[0].start_trades()
    small_copies[0].start()
    chain[0].start()
    for piece in taken[0].down:
        piece.start_near()
    for m in range(micros):
        build_mask(m)
    taken[0].heads.prepare()
    taken[1].heads.prepare()
    grad_sum[...] = jnp.zeros_like(grad_sum)
    small_step(0)
    taken[0].traded()
    chain[1].start()
    row_gathers[1].start()
    row_gathers[0].start()
    for piece in taken[0].cat:
        piece.start_near()
    small_step(1)
    pump(0)
    small_step(2)
    row_gathers[1].forward()
    for copy in fetched[pieces:]:
        copy.wait()
    columns_by_rank(1)
    small_step(3)
    pump(1)
    small_step(4)
    row_gathers[0].forward()
    taken[1].start_trades()

    gain, shift = bias_row(named_row(0, 0)), bias_row(named_row(0, 1))

    def first_norm(j, carry):
        row_gathers[0].arrive(j)
        row_gathers[1].arrive(j)

        def each(p, carry):
            size = rows // 4
            at = pl.ds(pl.multiple_of((p % 4) * size, size), size)
            normed, _ = normalise(hid[1, j, p // 4, at].astype(F32))
            hid[0, j, p // 4, at] = (normed * gain + shift).astype(BF16)
            return carry

        lax.fori_loop(0, 8, each, 0)
        for k in range(3):

            @pl.when(j == k)
            def _():
                pump(2 + k)

        return carry

    lax.fori_loop(0, 4, first_norm, 0)
    row_gathers[0].finish()
    row_gathers[1].finish()
    row_gathers[2].start()
    taken[1].traded()
    pump(5)
    for piece in taken[1].cat + taken[1].down:
        piece.start_near()
    taken[0].cat_done()

    def first(i, j):
        forward(0, j)

        @pl.when(i == 0)
        def _():
            pump(6)
            taken[0].rows_done()
            row_gathers[2].forward()

        for k in range(1, 4):

            @pl.when(i == k)
            def _():
                pump(6 + k)

    out_one.run(first, out_term(0), scratch, own, far_first)
    pump(10)

    def rest_of_rounded(j, carry):
        row_gathers[2].arrive(j)
        return carry

    lax.fori_loop(0, 4, rest_of_rounded, 0)
    row_gathers[2].finish()
    total = out_one.total(own)
    out_bias = bias_row(named_row(0, 2))
    gain, shift = bias_row(named_row(1, 0)), bias_row(named_row(1, 1))
    for m in range(4):
        at = pl.ds(m * (rows // 4), rows // 4)
        stream = inputs[at].astype(F32) + total(at) + out_bias
        stream_two[at] = stream
        normed, _ = normalise(stream)
        hid[1, 0, 0, at] = (normed * gain + shift).astype(BF16)
    hidden_two.start()
    pump(11)
    taken[1].cat_done()

    def second(j, carry):
        hidden_two.arrive(j)
        forward(1, j)

        @pl.when(j == 0)
        def _():
            hidden_two.forward()
            pump(12)
            pump(13)

        @pl.when(j == 2)
        def _():
            taken[1].rows_done()
            grads[1].rows_terms(0, 3)

        return carry

    lax.fori_loop(0, 4, second, 0)
    hidden_two.finish()
    grads[1].rows_terms(3, 4)
    grads[1].rows_one()

    sums[...] = jnp.zeros_like(sums)

    def fourth(i, j):
        backward(1, j)

        @pl.when(i == 2)
        def _():
            grads[1].rows_two()

    delta_two.run(fourth, hidden_term(1), scratch, own, far_first)
    bias_sums(1)
    give_back(2)
    grads[1].cat_terms(0)
    grads[1].cat_terms(1)
    total = delta_two.total(own)
    await_places(2)

    def put_one(at, value):
        up_one[at] = value
        rnd[0, 0, at] = value.astype(BF16)

    own_rows(1, total, lambda at: stream_two[at], lambda at: rnd[0, 0, at].astype(F32), put_one)
    rounded_one.start()
    give_back(0)
    sums[...] = jnp.zeros_like(sums)
    for zl in range(2):
        grads[1].cat_step_two(zl)
    grads[1].rows_three()
    await_places(0)
    rounded_one.forward()

    def third(i, j):
        @pl.when(i == 2)
        def _():
            for zl in range(2):
                grads[1].cat_step_three(zl)
            grads[1].cat_trade()
            rounded_one.arrive(1)

        @pl.when(i < 3)
        def _():
            rounded_one.arrive(j)

        @pl.when(i == 2)
        def _():
            rounded_one.finish()
            grads[0].rows_terms(0, 4)
            grads[0].rows_one()

        backward(0, j)

    delta_one.run(third, hidden_term(0), scratch, own, near_first)
    grads[0].cat_terms(0)
    grads[0].cat_terms(1)
    bias_sums(0)
    grads[0].rows_two()
    for zl in range(2):
        grads[0].cat_step_two(zl)
    total = delta_one.total(own)

    def put_last(at, value):
        input_grad[at] = value

    own_rows(0, total, lambda at: inputs[at].astype(F32), lambda at: up_one[at], put_last)
    grad_copies[0].start()
    give_back(1)
    grads[1].cat_done()
    await_places(1)
    out_two.run(lambda i, j: None, out_term(1), scratch, own, far_first)
    for i in range(len(SMALL_AXES)):
        grad_copies[i].wait()
        grad_stage(i + 1)[...] = grad_stage(i)[...] + small_in[i]
        if i + 1 < len(SMALL_AXES):
            grad_copies[i + 1].start()
        if i == 2:
            for zl in range(2):
                grads[0].cat_step_three(zl)
            grads[0].cat_trade()
        if i == 3:
            grads[0].rows_three()
    own_small(grad_stage(len(SMALL_AXES)))
    total = out_two.total(own)
    out_bias = bias_row(named_row(1, 2))
    for m in range(4):
        at = pl.ds(m * (rows // 4), rows // 4)
        outputs[at] = (stream_two[at] + total(at) + out_bias).astype(BF16)
    returned = return_columns(1) + return_columns(0)
    columns_by_name(1)
    for copy in returned[:pieces]:
        copy.start()
    grads[0].cat_done()
    columns_by_name(0)
    for copy in returned[pieces:]:
        copy.start()
    for copy in returned:
        copy.wait()


def named_rows(layers):
    return -(-3 * layers // 8) * 8


def run_layers(qkv, up, down, proj, inputs, cotangent, marks, small, tables):
    layers, count = qkv.shape[:2]
    rows, width = inputs.shape
    micros, lanes = marks.shape
    pack = rows // micros
    lift = up.shape[2] // RANKS
    wide = QKV + lift
    vmem = pl.BlockSpec(memory_space=pltpu.VMEM)
    anywhere = pl.BlockSpec(memory_space=pltpu.HBM)
    shape = jax.ShapeDtypeStruct
    stages = len(SMALL_AXES)
    small_rows = layers * RANKS + named_rows(layers)
    copies = 256
    cat_size = width // 8
    buffers = [
        ((layers, RANKS, count, wide), BF16),
        ((layers, 32, count, wide), BF16),
        ((layers, PAIR + lift, width), BF16),
        ((layers, 4, 2, rows, width), BF16),
        ((4, 2, rows, width), BF16),
        ((4, 2, micros, pack, lanes), BF16),
        ((layers, 4, 2 * rows, QKV), BF16),
        ((layers, 4, 2 * micros, 2 * pack, pack), BF16),
        ((layers, 4, 2 * rows, PAIR + lift), BF16),
        ((layers, 4, 2 * rows, lift), BF16),
        ((4, 2 * rows, wide), BF16),
        ((2, 2 * rows, width), F32),
        ((4, rows, width), BF16),
        ((3, rows, width), BF16),
        ((4, rows, width), BF16),
        ((3, rows, width), BF16),
        ((rows, width), F32),
        ((rows, width), F32),
        ((rows, width), F32),
        ((stages + 1, small_rows, width), F32),
        ((stages, small_rows, width), F32),
        ((8, wide), F32),
        ((small_rows, width), F32),
        ((2, 2, cat_size, wide), F32),
        ((2, 2, cat_size, wide), BF16),
        ((layers, 2, 2, cat_size, wide), BF16),
        ((2, cat_size, wide), BF16),
        ((layers, 2, cat_size, wide), BF16),
        ((2, 4, count, wide), BF16),
        ((PAIR + lift, width), F32),
        ((lift // 2, width), BF16),
        ((layers, lift // 2, width), BF16),
        ((lift // 4, width), BF16),
        ((layers, lift // 4, width), BF16),
        ((PAIR, width), BF16),
        ((layers, PAIR, width), BF16),
        ((HEAD_DIM, width), BF16),
        ((layers, HEAD_DIM, width), BF16),
        ((HEAD_DIM // 2, width), BF16),
        ((layers, HEAD_DIM // 2, width), BF16),
    ]
    return pl.pallas_call(
        layers_kernel,
        out_shape=(
            shape((rows, width), BF16),
            shape((rows, width), F32),
            shape((layers, width // 32), F32),
            shape((layers, width // 32), F32),
            shape(qkv.shape, F32),
            shape((layers, 2 * width // 32), F32),
            shape(proj.shape, F32),
            shape((layers, width // 32), F32),
            shape(up.shape, F32),
            shape((layers, up.shape[2] // 32), F32),
            shape(down.shape, F32),
        ),
        in_specs=[anywhere] * 4 + [vmem] * 5,
        out_specs=(vmem,) * 4 + (anywhere,) + (vmem,) * 3 + (anywhere,) + (vmem,) * 2,
        scratch_shapes=[pltpu.VMEM(dims, kind) for dims, kind in buffers]
        + [
            pltpu.SemaphoreType.DMA((copies,)),
            pltpu.SemaphoreType.DMA((copies,)),
            pltpu.SemaphoreType.DMA((layers, 4)),
            pltpu.SemaphoreType.REGULAR((3,)),
            pltpu.SemaphoreType.DMA((layers * 7,)),
        ],
        compiler_params=pltpu.CompilerParams(
            collective_id=0, has_side_effects=True, vmem_limit_bytes=63 << 20
        ),
    )(qkv, up, down, proj, inputs, cotangent, marks, small, tables)


def refold(block, extra):
    if extra == 1:
        return block
    whole = lax.all_gather(block, AXES, axis=1, tiled=True)
    rows = whole.shape[1] // 32
    return lax.dynamic_slice_in_dim(whole, lax.axis_index(AXES[1:]) * rows, rows, 1)


def unfold(block, extra):
    if extra == 1:
        return block
    rows = block.shape[1]
    whole = jnp.zeros((block.shape[0], 32 * rows) + block.shape[2:], F32)
    whole = lax.dynamic_update_slice_in_dim(whole, block, lax.axis_index(AXES[1:]) * rows, 1)
    return lax.psum_scatter(whole, AXES, scatter_dimension=1, tiled=True)


def rope_tables(pack):
    half = ROT // 2
    angle = np.arange(pack, dtype=np.float32)[:, None] * (
        np.float32(10000.0) ** (-np.arange(0, ROT, 2, dtype=np.float32) / np.float32(ROT))
    )
    angle = angle.astype(np.float32)
    tables = np.zeros((3, pack, 2, HEAD_DIM), np.float32)
    tables[0] = 1.0
    tables[0, :, :, :half] = tables[0, :, :, half:ROT] = np.cos(angle)[:, None]
    tables[1, :, :, :half] = -np.sin(angle)[:, None]
    tables[2, :, :, half:ROT] = np.sin(angle)[:, None]
    return tables.reshape(3, pack, PAIR)


def shards(
    inputs,
    cotangent,
    segments,
    pack_length,
    norm_gain,
    norm_shift,
    qkv_weight,
    qv_bias,
    proj_weight,
    proj_bias,
    up_weight,
    up_bias,
    down_weight,
    down_bias,
):
    micros, pack, width = inputs.shape
    layers = qkv_weight.shape[0]
    extra = lax.axis_size("e")
    marks = jnp.concatenate([segments, pack_length], axis=1).astype(F32)
    marks = jnp.pad(marks, ((0, 0), (0, -(pack + 1) % 128)))

    def row(value):
        return jnp.pad(value.astype(F32), ((0, 0), (0, width - value.shape[1])))

    biases = refold(proj_bias, extra).astype(F32) + refold(down_bias, extra).astype(F32)
    vectors = [row(refold(norm_gain, extra)), row(refold(norm_shift, extra)), row(biases)]
    vectors = jnp.stack(vectors, axis=1).reshape(3 * layers, width)
    named = named_rows(layers)
    small = jnp.concatenate(
        [
            jnp.pad(vectors, ((0, named - 3 * layers), (0, 0))),
            row(refold(qv_bias, extra)),
            row(refold(up_bias, extra)),
            jnp.zeros((-2 * layers % 8, width), F32),
        ]
    )
    given = run_layers(
        refold(qkv_weight, extra),
        refold(up_weight, extra),
        refold(down_weight, extra),
        refold(proj_weight, extra),
        inputs.reshape(micros * pack, width),
        cotangent.reshape(micros * pack, width),
        marks,
        small,
        jnp.asarray(rope_tables(pack)),
    )
    out, input_grad = given[:2]
    gain, shift, qkv, qvb, proj, bias, up, upb, down = [unfold(g, extra) for g in given[2:]]
    return (
        out.reshape(micros, pack, width),
        input_grad.reshape(micros, pack, width),
        gain,
        shift,
        qkv,
        qvb,
        proj,
        bias,
        up,
        upb,
        down,
        bias,
    )


def solution(mesh):
    devices = mesh.devices.size
    fine = Mesh(mesh.devices.reshape(devices // 32, 2, 2, 2, 2, 2), AXES)
    cube, flat = P(None, AXES, None), P(None, AXES)
    placed = (cube, cube, flat, flat, flat, flat, cube, flat, cube, flat, cube, flat, cube, flat)
    given = (cube, cube, flat, flat, cube, flat, cube, flat, cube, flat, cube, flat)
    return jax.shard_map(shards, mesh=fine, in_specs=placed, out_specs=given, check_vma=False)
```

time: 378 us -> 315 us (0.83)
  Pallas kernels: 347 us -> 300 us
  other arithmetic: 8.69 us -> 0.81 us
  local copies, waits for them, and re-layouts: 20.6 us -> 13.8 us
    pallas_call x1, Pallas kernels: 347 us -> 300 us  [run_layers(): pl.pallas_call(layers_kernel, out_shape=(shape((rows, width), BF16), shap...]
    unnamed x23 -> x49, local copies, waits for them, and re-layouts: 3.9 us -> 13.1 us
    convert_element_type x6 -> x0, local copies, waits for them, and re-layouts: 7.84 us -> none  [the longest x3 4.55 us: shards(): join_heads(qkv_grad).astype(F32)]
    reshape x21 -> x1, local copies, waits for them, and re-layouts: 5.35 us -> 0.02 us  [shards(): vectors = jnp.stack(vectors, axis=1).reshape(3 * layers, width)]
where the time goes in v4:
time: 315 us
  Pallas kernels  300 us (95%)
  local copies, waits for them, and re-layouts  13.8 us (4%)
    pallas_call x1, Pallas kernels, run_layers(): pl.pallas_call(layers_kernel, out_shape=(shape((rows, width), BF16), shap...  300 us
    unnamed x49, local copies, waits for them, and re-layouts  13.1 us

profile of v4, /device:TPU:0, one launch (start us, length us, event | category | flops | bytes accessed | tf_op | source)
XLA Modules:
  0.0 314.9 jit_solution(4235000586984620917)
XLA Ops:
  0.7 0.0 copy-start.17
  0.7 0.1 pad.46.clone
  0.7 0.6 copy-done.17
  1.3 0.0 copy-start.6
  1.3 0.1 copy.29
  1.4 0.6 copy-done.6
  2.0 0.1 add_convert_fusion
  2.1 0.0 copy-start.15
  2.1 0.0 copy-start.16
  2.1 0.6 pad.34.marks
  2.6 0.1 copy-done.15
  2.7 0.0 copy-done.16
  2.7 0.0 copy-start.11
  2.7 0.0 copy-start.12
  2.8 0.6 copy-done.11
  3.4 0.0 copy-done.12
  3.5 0.0 copy-start.13
  3.5 0.0 copy-start.14
  3.5 0.6 copy-done.13
  4.1 0.0 copy-done.14
  4.1 0.7 fusion.1.small
  4.8 299.6 %shard_map.238 = (bf16[192,1024]{1,0:T(8,128)(2,1)}, f32[192,1024]{1,0:T(8,128)}, f32[2,32]{1,0:T(2,128)}, f32[2,32]{1,0:T(2,128)}, f32[2,32,3072]{2,1,0:T(8,128...) custom-call(bf16[2,32,3072]{2,1,0:T(8,128)(2,1)} %qkv.1, ...), custom_call_target="tpu_custom_call" | custom-call | tf_op jit(solution)/shard_map/pallas_call | solution.py:1178
  304.4 0.0 copy-start.3
  304.5 1.3 copy.43
  305.7 1.8 copy.44
  307.5 0.0 copy-done.3
  307.5 0.0 copy-start.10
  307.5 0.0 copy-start.2
  307.5 0.9 copy.45
  308.4 0.0 copy-done.10
  308.4 0.0 copy-start.9
  308.4 0.6 copy.46
  309.0 0.1 copy-done.9
  309.1 0.6 copy.47
  309.6 0.0 copy-done.2
  309.6 0.0 copy-start.8
  309.6 0.0 copy-start.4
  309.6 0.0 copy-start.1
  309.6 0.9 copy.48
  310.5 0.0 copy-done.8
  310.5 0.6 copy.49
  311.1 0.0 copy-done.4
  311.1 0.0 copy-start.5
  311.1 0.7 copy.50
  311.8 0.0 copy-done.5
  311.8 0.6 copy.51
  312.4 0.0 copy-done.1
  312.4 0.0 copy-start.7
  312.4 0.0 copy-start
  312.4 1.0 copy.52
  313.3 0.0 copy-done.7
  313.3 0.6 copy.53
  313.9 0.1 copy-done
  314.0 1.0 copy.54
  (8 shorter events, 0.1 us)
Async XLA Ops:
  0.7 0.7 copy-start.17
  1.3 0.7 copy-start.6
  2.1 0.7 copy-start.15
  2.1 0.7 copy-start.16
  2.7 0.7 copy-start.11
  2.7 0.7 copy-start.12
  3.5 0.7 copy-start.13
  3.5 0.7 copy-start.14
  304.4 3.1 copy-start.3
  307.5 0.9 copy-start.10
  307.5 2.1 copy-start.2
  308.4 0.7 copy-start.9
  309.6 0.9 copy-start.8
  309.6 1.5 copy-start.4
  309.6 2.7 copy-start.1
  311.1 0.7 copy-start.5
  312.4 1.0 copy-start.7
  312.4 1.6 copy-start

commit v5 on v4

--- a/solution.py
+++ b/solution.py
@@ -20,7 +20,8 @@
 RANKS = 8
 NEAR = (("c",), (T1,), (T2,), (T1, "c"), (T2, "c"), (T1, T2), (T1, T2, "c"))
 FAR = ((D1,), (D2,))
-SMALL_AXES = ("c", T1, T2, D1, D2)
+SMALL_AXES = ("zh", "x", "zl", "y", "c")
+GRAD_AXES = ("c", T1, T2, D1, D2)
 
 F32, BF16 = jnp.float32, jnp.bfloat16
 MESH = pl.DeviceIdType.MESH
@@ -83,42 +84,46 @@
 
 class Rows:
     def __init__(self, links, buffer):
-        self.links, self.buffer, self.base = links, buffer, links.reserve(8)
+        self.links, self.buffer, self.base = links, buffer, links.reserve(9)
+        self.near = [
+            None,
+            links.copy(buffer.at[0, 0], buffer.at[1, 0], (T2,), self.base + 5),
+            links.copy(buffer.at[0, 0], buffer.at[2, 0], (T1,), self.base + 6),
+        ]
+        self.far = [
+            links.copy(buffer.at[1, 0], buffer.at[3, 0], (T1,), self.base + 7),
+        ]
 
     def core(self, j):
         return self.links.copy(
             self.buffer.at[j, 0], self.buffer.at[j, 1], ("c",), self.base + j
         )
 
-    def chip(self, j):
-        source, axes = (0, (T1,)) if isinstance(j, jax.Array) else ((0, 0, 0, 1)[j], (T2,) if j == 1 else (T1,))
-        return self.links.copy(
-            self.buffer.at[source, 0], self.buffer.at[j, 0], axes, self.base + 4 + j
-        )
-
     def start(self):
         self.core(0).start()
-        self.chip(1).start()
-        self.chip(2).start()
+        self.near[1].start()
+        self.near[2].start()
 
     def forward(self):
-        self.chip(1).wait_recv()
-        self.chip(3).start()
+        self.near[1].wait_recv()
+        self.far[0].start()
         self.core(1).start()
+        self.near[2].wait_recv()
+        self.core(2).start()
 
     def arrive(self, j):
-        @pl.when(j > 1)
+        @pl.when(j == 3)
         def _():
-            self.chip(j).wait_recv()
-            self.core(j).start()
+            self.far[0].wait_recv()
+            self.core(3).start()
 
         self.core(j).wait_recv()
 
     def finish(self):
         for j in range(4):
             self.core(j).wait_send()
-        for j in range(1, 4):
-            self.chip(j).wait_send()
+        for copy in self.near[1:] + self.far:
+            copy.wait_send()
 
 
 def far_first(i):
@@ -130,8 +135,9 @@
 
 
 class Sums:
-    def __init__(self, links, core_in, chip_in, core_out, chip_out):
+    def __init__(self, links, core_in, chip_in, core_out, chip_out, turned=False):
         self.links, self.base = links, links.reserve(8)
+        self.relayed, self.far_axis = (2, T2) if turned else (1, T1)
         self.core_in, self.chip_in, self.core_out, self.chip_out = core_in, chip_in, core_out, chip_out
 
     def core(self, j):
@@ -143,11 +149,11 @@
         return self.links.copy(
             self.chip_out.at[j - 1],
             self.chip_in.at[j - 1],
-            (T2,) if j == 1 else (T1,),
+            ((T2,), (T1,), (self.far_axis,))[j - 1],
             self.base + 4 + j,
         )
 
-    def run(self, before, term, scratch, own, order):
+    def run(self, before, term, scratch, own, order, hold=False):
         rows = own.shape[0]
 
         def pass_on(j):
@@ -160,12 +166,12 @@
                     @pl.when(j == k)
                     def _():
                         value = total
-                        if k == 1:
+                        if k == self.relayed and not hold:
                             if m == 0:
                                 self.chip(3).wait_recv()
                             value = value + self.chip_in[2, at].astype(F32)
                         self.chip_out[k - 1, at] = value.astype(BF16)
-                        if m == 1:
+                        if m == 1 and not hold:
                             self.chip(k).start()
 
                 @pl.when(j == 0)
@@ -186,13 +192,27 @@
             return carry
 
         lax.fori_loop(0, 4, step, 0)
-        pass_on(order(3))
-
-    def total(self, own):
+        return lambda: pass_on(order(3))
+
+    def release(self):
+        self.chip(3).start()
+        self.chip(3 - self.relayed).start()
+
+    def relay(self):
+        self.chip(3).wait_recv()
+        rows, place = self.chip_out.shape[1], self.relayed - 1
+        for m in range(4):
+            at = pl.ds(m * (rows // 4), rows // 4)
+            value = self.chip_out[place, at].astype(F32) + self.chip_in[2, at].astype(F32)
+            self.chip_out[place, at] = value.astype(BF16)
+        self.chip(self.relayed).start()
+
+    def total(self, own, held=False):
         for j in (1, 2):
             self.chip(j).wait_recv()
-        for j in range(4):
-            self.core(j).wait_send()
+        if not held:
+            for j in range(4):
+                self.core(j).wait_send()
         for j in (1, 2, 3):
             self.chip(j).wait_send()
 
@@ -255,10 +275,12 @@
     own,
     stream_two,
     up_one,
-    small_sum,
-    small_in,
+    small_all,
+    named,
+    rank_bias,
     sums,
     grad_sum,
+    grad_in,
     cat_own,
     cat_s1,
     cat_r1,
@@ -297,14 +319,8 @@
     lane = lax.broadcasted_iota(jnp.int32, (pack, PAIR), 1)
     first_head = lane < HEAD_DIM
 
-    def ranks_row(layer):
-        return layer * RANKS + rank
-
-    def named_row(layer, index):
-        return layers * RANKS + 3 * layer + index
-
-    def bias_row(index):
-        return small_sum[len(SMALL_AXES), pl.ds(index, 1), :]
+    def bias_row(layer, kind):
+        return named[kind, layer : layer + 1, :]
 
     pieces = 3 + up.shape[2] // width
     raw = [core_out.at[i // 6, pl.ds(i % 6 * count, count)] for i in range(layers * pieces)]
@@ -381,36 +397,56 @@
     up_size = up.shape[2] // 32
     up_cut = pl.ds(pl.multiple_of(QKV + slot * up_size, PAIR), up_size)
 
-    ranked = layers * RANKS
-    named = small_sum.shape[1] - ranked
     rank_row = lax.broadcasted_iota(jnp.int32, (RANKS, PAIR), 0)
-
-    def spread_small():
-        small_sum[0, :ranked] = jnp.zeros((ranked, width), F32)
-        small_sum[0, ranked:] = pltpu.roll(small[:named], block * (width // 32), 1)
+    own_tile = me["c"] * 16 + me["y"] * 8 + me["zl"] * 4 + me["x"] * 2 + me["zh"]
+
+    def expand_small():
+        share = width // 32
+        lanes_of = lax.broadcasted_iota(jnp.int32, (8, PAIR), 1) // share
+        for group in range(8):
+            zh, zl, x = group // 4, group // 2 % 2, group % 2
+            tiles = [small_all[c * 16 + y * 8 + zl * 4 + x * 2 + zh] for y in range(2) for c in range(2)]
+            for kind in range(3):
+                value = jnp.zeros((8, PAIR), F32)
+                for r, tile in enumerate(tiles):
+                    moved = (r - kind) % 4 * share
+                    tile = pltpu.roll(tile, moved, 1) if moved else tile
+                    value = jnp.where(lanes_of == r, tile, value)
+                named[kind, :, group * PAIR : (group + 1) * PAIR] = value
+        rank_bias[...] = jnp.zeros_like(rank_bias)
+        here = lax.broadcasted_iota(jnp.int32, (8, PAIR), 1) < HEAD_DIM
         for layer in range(layers):
-            at = slice(layer * RANKS, (layer + 1) * RANKS)
-            pair = jnp.broadcast_to(small[named + layer : named + layer + 1, :PAIR], (RANKS, PAIR))
-            pair = pltpu.roll(pair, me["zl"] * HEAD_DIM, 1)
-            small_sum[0, at, head_cut] = jnp.where(rank_row == head_rank, pair, 0.0)
-            more = named + layers + layer
-            more = jnp.broadcast_to(small[more : more + 1, :up_size], (RANKS, up_size))
-            small_sum[0, at, up_cut] = jnp.where(rank_row == rank, more, 0.0)
-
-    def own_small(total):
+            at = slice(layer, layer + 1)
+            for part in range(2):
+                heads = []
+                for zh in range(2):
+                    tile = small_all[
+                        me["y"] * 16 + me["c"] * 8 + zh * 4 + me["zl"] * 2 + part, layers : layers + 1, :
+                    ]
+                    tile = jnp.broadcast_to(tile, (8, PAIR))
+                    heads.append(tile if zh == layer else pltpu.roll(tile, HEAD_DIM, 1))
+                cut = slice(2 * part * PAIR, (2 * part + 1) * PAIR)
+                rank_bias[at, cut] = jnp.where(here, heads[0], heads[1])[:1]
+            for x in range(2):
+                for zh in range(2):
+                    tile = me["c"] * 16 + me["y"] * 8 + me["zl"] * 4 + x * 2 + zh
+                    to = QKV + (x * 2 + zh) * up_size
+                    line = layers + 1 + layer
+                    rank_bias[at, to : to + up_size] = small_all[tile, line : line + 1, :]
+
+    def own_small(layer):
         share = width // 32
-        moved = pltpu.roll(total[ranked:], (32 - block) % 32 * share, 1)
-        for layer in range(layers):
-            start = layer * 3
-            gain_out[layer : layer + 1] = moved[start : start + 1, :share]
-            shift_out[layer : layer + 1] = moved[start + 1 : start + 2, :share]
-            bias_out[layer : layer + 1] = moved[start + 2 : start + 3, :share]
-            at = slice(layer * RANKS, (layer + 1) * RANKS)
-            pair = pltpu.roll(total[at, head_cut], me["zl"] * HEAD_DIM, 1)
-            pair = jnp.where(rank_row == head_rank, pair, 0.0)
-            qvb_out[layer : layer + 1] = jnp.sum(pair, axis=0, keepdims=True)[:, :HEAD_DIM]
-            more = jnp.where(rank_row == rank, total[at, up_cut], 0.0)
-            upb_out[layer : layer + 1] = jnp.sum(more, axis=0, keepdims=True)
+        total = grad_sum.at[layer, len(SMALL_AXES)]
+        moved = pltpu.roll(total[RANKS:], (32 - block) % 32 * share, 1)
+        at = slice(layer, layer + 1)
+        gain_out[at] = moved[0:1, :share]
+        shift_out[at] = moved[1:2, :share]
+        bias_out[at] = moved[2:3, :share]
+        pair = pltpu.roll(total[:RANKS, head_cut], me["zl"] * HEAD_DIM, 1)
+        pair = jnp.where(rank_row == head_rank, pair, 0.0)
+        qvb_out[at] = jnp.sum(pair, axis=0, keepdims=True)[:, :HEAD_DIM]
+        more = jnp.where(rank_row == rank, total[:RANKS, up_cut], 0.0)
+        upb_out[at] = jnp.sum(more, axis=0, keepdims=True)
 
     def build_mask(m):
         row = lax.broadcasted_iota(jnp.int32, (lanes, lanes), 0)
@@ -579,7 +615,7 @@
         for cut in (slice(0, QKV), slice(QKV, wide)):
             columns = cat_all[layer, :, :, cut].reshape(width, -1)
             scratch[0, :, cut] = dot(hidden, columns, ((1,), (0,)))
-        bias = bias_row(ranks_row(layer))
+        bias = rank_bias[layer : layer + 1, :]
 
         def each(p, carry):
             at = pl.ds(pl.multiple_of(p * pack, pack), pack)
@@ -779,12 +815,11 @@
             for zl in range(2):
                 start = pl.multiple_of((zh * 2 + zl) * (width // 4), width // 4)
                 kept = hid[layer, :, :, :, pl.ds(start, width // 4)].reshape(8 * rows, width // 4)
-                scratch[zl, : width // 4, :wide] = dot(kept, deltas, ((0,), (0,)))
-            size = width // 8
-            for zl in range(2):
-                cat_s1[i, zl] = scratch[zl, pl.ds((1 - me["x"]) * size, size), :wide].astype(BF16)
+                scratch[0, : width // 4, :wide] = dot(kept, deltas, ((0,), (0,)))
+                size = width // 8
+                cat_s1[i, zl] = scratch[0, pl.ds((1 - me["x"]) * size, size), :wide].astype(BF16)
                 self.cat_one[i][zl].start()
-                cat_own[i, zl] = scratch[zl, pl.ds(me["x"] * size, size), :wide]
+                cat_own[i, zl] = scratch[0, pl.ds(me["x"] * size, size), :wide]
 
         def cat_step_two(self, zl):
             layer = self.layer
@@ -813,11 +848,11 @@
                 copy.wait()
             self.keep.wait()
 
-    def put_sums(index, value):
-        grad_sum[pl.ds(index, 1), : value.shape[1]] = value
+    def put_sums(layer, index, value):
+        grad_sum[layer, 0, pl.ds(index, 1), : value.shape[1]] = value
 
     def own_rows(layer, total, stream_at, up_at, put):
-        gain = bias_row(named_row(layer, 0))
+        gain = bias_row(layer, 0)
         gain_sum = jnp.zeros((1, width), F32)
         shift_sum = jnp.zeros((1, width), F32)
         for m in range(2 * micros):
@@ -831,17 +866,17 @@
                 at,
                 up_at(at) + inverse * (scaled - mean_of(scaled) - normed * mean_of(scaled * normed)),
             )
-        put_sums(named_row(layer, 0), gain_sum)
-        put_sums(named_row(layer, 1), shift_sum)
+        put_sums(layer, RANKS + 0, gain_sum)
+        put_sums(layer, RANKS + 1, shift_sum)
 
     def bias_sums(layer):
-        put_sums(ranks_row(layer), jnp.sum(sums[...], axis=0, keepdims=True))
+        put_sums(layer, rank, jnp.sum(sums[...], axis=0, keepdims=True))
         rounded = jnp.zeros((8, width), F32)
         for m in range(2 * micros):
             size = rows // (2 * micros)
             part = rnd[0, 0, pl.ds(m * size, size)].astype(F32)
             rounded = rounded + jnp.sum(part.reshape(size // 8, 8, width), axis=0)
-        put_sums(named_row(layer, 2), jnp.sum(rounded, axis=0, keepdims=True))
+        put_sums(layer, RANKS + 2, jnp.sum(rounded, axis=0, keepdims=True))
 
     def give_back(turn_index):
         for axes in (("c",), (T1,), (T2,)):
@@ -858,54 +893,69 @@
     hidden_two, rounded_one = Rows(links, hid.at[1]), Rows(links, rnd)
     sets = (core_in, chip_in, core_out, chip_out)
     out_one, delta_two, delta_one = Sums(links, *sets), Sums(links, *sets), Sums(links, *sets)
-    out_two = Sums(links, *sets)
-
-    def grad_stage(i):
-        return grad_sum if i == 0 else small_sum.at[i - 1]
-
-    small_copies = [
-        links.copy(small_sum.at[i], small_in.at[i], (axis,)) for i, axis in enumerate(SMALL_AXES)
+    spare = hid.at[1]
+    out_two = Sums(links, core_in, spare.at[0:3, 0], core_out, spare.at[0:3, 1], True)
+    small_copies = []
+    for i, axis in enumerate(SMALL_AXES):
+        tiles = small_all.at[pl.ds(own_tile // 2**i * 2**i, 2**i)]
+        small_copies.append(links.copy(tiles, tiles, (axis,)))
+    grad_copies = [
+        [
+            links.copy(grad_sum.at[layer, i], grad_in.at[layer, i], (axis,))
+            for i, axis in enumerate(GRAD_AXES)
+        ]
+        for layer in range(layers)
     ]
-    grad_copies = [
-        links.copy(grad_stage(i), small_in.at[i], (axis,)) for i, axis in enumerate(SMALL_AXES)
-    ]
+
+    def grad_step(layer, i):
+        grad_copies[layer][i].wait()
+        grad_sum[layer, i + 1] = grad_sum[layer, i] + grad_in[layer, i]
+        if i + 1 < len(SMALL_AXES):
+            grad_copies[layer][i + 1].start()
+        else:
+            own_small(layer)
 
     chain = [taken[0].down[0]] + taken[0].cat + [taken[0].down[1], taken[0].heads]
     chain = chain + taken[1].cat + taken[1].down + [taken[1].heads]
 
     def pump(k):
         chain[k].step()
-        if k + 2 < len(chain):
-            chain[k + 2].start()
+        for piece in chain[max(ahead(k - 1), 2) : ahead(k)]:
+            piece.start()
         chain[k].start_far()
+
+    def ahead(k):
+        return min(k + 3 if k < 5 else k + 5, len(chain))
 
     def small_step(i):
         small_copies[i].wait()
-        small_sum[i + 1] = small_sum[i] + small_in[i]
         if i + 1 < len(SMALL_AXES):
             small_copies[i + 1].start()
+        else:
+            expand_small()
 
     fetched = fetch_columns()
     for copy in fetched:
         copy.start()
     for one in taken:
         one.keep[1].start()
-    spread_small()
-    hid[1, 0, 0] = inputs[...]
+    small_all[own_tile] = small[...]
+    links.meet()
+    small_copies[0].start()
+    chain[0].start()
     for copy in fetched[:pieces]:
         copy.wait()
     columns_by_rank(0)
-    links.meet()
     taken[0].start_trades()
-    small_copies[0].start()
-    chain[0].start()
     for piece in taken[0].down:
         piece.start_near()
+    hid[1, 0, 0] = inputs[...]
     for m in range(micros):
         build_mask(m)
     taken[0].heads.prepare()
     taken[1].heads.prepare()
-    grad_sum[...] = jnp.zeros_like(grad_sum)
+    for layer in range(layers):
+        grad_sum[layer, 0] = jnp.zeros_like(grad_sum[layer, 0])
     small_step(0)
     taken[0].traded()
     chain[1].start()
@@ -926,7 +976,7 @@
     row_gathers[0].forward()
     taken[1].start_trades()
 
-    gain, shift = bias_row(named_row(0, 0)), bias_row(named_row(0, 1))
+    gain, shift = bias_row(0, 0), bias_row(0, 1)
 
     def first_norm(j, carry):
         row_gathers[0].arrive(j)
@@ -973,7 +1023,7 @@
             def _():
                 pump(6 + k)
 
-    out_one.run(first, out_term(0), scratch, own, far_first)
+    out_one.run(first, out_term(0), scratch, own, far_first)()
     pump(10)
 
     def rest_of_rounded(j, carry):
@@ -983,8 +1033,8 @@
     lax.fori_loop(0, 4, rest_of_rounded, 0)
     row_gathers[2].finish()
     total = out_one.total(own)
-    out_bias = bias_row(named_row(0, 2))
-    gain, shift = bias_row(named_row(1, 0)), bias_row(named_row(1, 1))
+    out_bias = bias_row(0, 2)
+    gain, shift = bias_row(1, 0), bias_row(1, 1)
     for m in range(4):
         at = pl.ds(m * (rows // 4), rows // 4)
         stream = inputs[at].astype(F32) + total(at) + out_bias
@@ -1005,32 +1055,21 @@
             pump(12)
             pump(13)
 
-        @pl.when(j == 2)
-        def _():
-            taken[1].rows_done()
-            grads[1].rows_terms(0, 3)
-
         return carry
 
     lax.fori_loop(0, 4, second, 0)
     hidden_two.finish()
-    grads[1].rows_terms(3, 4)
-    grads[1].rows_one()
+    taken[1].rows_done()
 
     sums[...] = jnp.zeros_like(sums)
 
-    def fourth(i, j):
-        backward(1, j)
-
-        @pl.when(i == 2)
-        def _():
-            grads[1].rows_two()
-
-    delta_two.run(fourth, hidden_term(1), scratch, own, far_first)
+    delta_two.run(lambda i, j: backward(1, j), hidden_term(1), scratch, own, far_first)()
+    grads[1].cat_terms(0)
+    grads[1].cat_terms(1)
+    grads[1].rows_terms(0, 4)
     bias_sums(1)
     give_back(2)
-    grads[1].cat_terms(0)
-    grads[1].cat_terms(1)
+    grads[1].rows_one()
     total = delta_two.total(own)
     await_places(2)
 
@@ -1040,20 +1079,33 @@
 
     own_rows(1, total, lambda at: stream_two[at], lambda at: rnd[0, 0, at].astype(F32), put_one)
     rounded_one.start()
+    grad_copies[1][0].start()
+    sums[...] = jnp.zeros_like(sums)
+    out_two.run(lambda i, j: None, out_term(1), scratch, own, far_first, True)()
+    for m in range(4):
+        at = pl.ds(m * (rows // 4), rows // 4)
+        stream_two[at] = stream_two[at] + own[at] + bias_row(1, 2)
     give_back(0)
-    sums[...] = jnp.zeros_like(sums)
-    for zl in range(2):
-        grads[1].cat_step_two(zl)
-    grads[1].rows_three()
+    rounded_one.forward()
+    out_two.release()
+    for j in range(4):
+        out_two.core(j).wait_send()
     await_places(0)
-    rounded_one.forward()
 
     def third(i, j):
+        for k in range(4):
+
+            @pl.when(i == k)
+            def _():
+                grad_step(1, k)
+
+        @pl.when(i == 1)
+        def _():
+            for zl in range(2):
+                grads[1].cat_step_two(zl)
+
         @pl.when(i == 2)
         def _():
-            for zl in range(2):
-                grads[1].cat_step_three(zl)
-            grads[1].cat_trade()
             rounded_one.arrive(1)
 
         @pl.when(i < 3)
@@ -1063,60 +1115,60 @@
         @pl.when(i == 2)
         def _():
             rounded_one.finish()
-            grads[0].rows_terms(0, 4)
-            grads[0].rows_one()
+
+        @pl.when(i == 3)
+        def _():
+            grads[1].rows_two()
 
         backward(0, j)
 
-    delta_one.run(third, hidden_term(0), scratch, own, near_first)
+    last = delta_one.run(third, hidden_term(0), scratch, own, near_first)
+    for zl in range(2):
+        grads[1].cat_step_three(zl)
     grads[0].cat_terms(0)
+    grads[1].cat_trade()
     grads[0].cat_terms(1)
+    grads[1].rows_three()
+    grads[0].rows_terms(0, 4)
+    grads[0].rows_one()
+    out_two.relay()
     bias_sums(0)
-    grads[0].rows_two()
+    grad_step(1, 4)
+    last()
     for zl in range(2):
         grads[0].cat_step_two(zl)
-    total = delta_one.total(own)
-
-    def put_last(at, value):
-        input_grad[at] = value
-
-    own_rows(0, total, lambda at: inputs[at].astype(F32), lambda at: up_one[at], put_last)
-    grad_copies[0].start()
-    give_back(1)
     grads[1].cat_done()
-    await_places(1)
-    out_two.run(lambda i, j: None, out_term(1), scratch, own, far_first)
-    for i in range(len(SMALL_AXES)):
-        grad_copies[i].wait()
-        grad_stage(i + 1)[...] = grad_stage(i)[...] + small_in[i]
-        if i + 1 < len(SMALL_AXES):
-            grad_copies[i + 1].start()
-        if i == 2:
-            for zl in range(2):
-                grads[0].cat_step_three(zl)
-            grads[0].cat_trade()
-        if i == 3:
-            grads[0].rows_three()
-    own_small(grad_stage(len(SMALL_AXES)))
-    total = out_two.total(own)
-    out_bias = bias_row(named_row(1, 2))
-    for m in range(4):
-        at = pl.ds(m * (rows // 4), rows // 4)
-        outputs[at] = (stream_two[at] + total(at) + out_bias).astype(BF16)
     returned = return_columns(1) + return_columns(0)
     columns_by_name(1)
     for copy in returned[:pieces]:
         copy.start()
+    total = delta_one.total(own)
+
+    def put_last(at, value):
+        input_grad[at] = value
+
+    own_rows(0, total, lambda at: inputs[at].astype(F32), lambda at: up_one[at], put_last)
+    grad_copies[0][0].start()
+    total = out_two.total(stream_two, True)
+    for m in range(4):
+        at = pl.ds(m * (rows // 4), rows // 4)
+        outputs[at] = total(at).astype(BF16)
+    grad_step(0, 0)
+    for zl in range(2):
+        grads[0].cat_step_three(zl)
+    grads[0].cat_trade()
+    grad_step(0, 1)
+    grad_step(0, 2)
+    grads[0].rows_two()
+    grad_step(0, 3)
     grads[0].cat_done()
     columns_by_name(0)
     for copy in returned[pieces:]:
         copy.start()
+    grad_step(0, 4)
+    grads[0].rows_three()
     for copy in returned:
         copy.wait()
-
-
-def named_rows(layers):
-    return -(-3 * layers // 8) * 8
 
 
 def run_layers(qkv, up, down, proj, inputs, cotangent, marks, small, tables):
@@ -1130,7 +1182,6 @@
     anywhere = pl.BlockSpec(memory_space=pltpu.HBM)
     shape = jax.ShapeDtypeStruct
     stages = len(SMALL_AXES)
-    small_rows = layers * RANKS + named_rows(layers)
     copies = 256
     cat_size = width // 8
     buffers = [
@@ -1153,10 +1204,12 @@
         ((rows, width), F32),
         ((rows, width), F32),
         ((rows, width), F32),
-        ((stages + 1, small_rows, width), F32),
-        ((stages, small_rows, width), F32),
+        ((32,) + small.shape, F32),
+        ((3, 8, width), F32),
         ((8, wide), F32),
-        ((small_rows, width), F32),
+        ((8, wide), F32),
+        ((layers, stages + 1, 2 * RANKS, width), F32),
+        ((layers, stages, 2 * RANKS, width), F32),
         ((2, 2, cat_size, wide), F32),
         ((2, 2, cat_size, wide), BF16),
         ((layers, 2, 2, cat_size, wide), BF16),
@@ -1259,21 +1312,18 @@
     marks = jnp.concatenate([segments, pack_length], axis=1).astype(F32)
     marks = jnp.pad(marks, ((0, 0), (0, -(pack + 1) % 128)))
 
-    def row(value):
-        return jnp.pad(value.astype(F32), ((0, 0), (0, width - value.shape[1])))
+    def wide(value):
+        return jnp.pad(value.astype(F32), ((0, 0), (0, PAIR - value.shape[1])))
 
     biases = refold(proj_bias, extra).astype(F32) + refold(down_bias, extra).astype(F32)
-    vectors = [row(refold(norm_gain, extra)), row(refold(norm_shift, extra)), row(biases)]
-    vectors = jnp.stack(vectors, axis=1).reshape(3 * layers, width)
-    named = named_rows(layers)
-    small = jnp.concatenate(
-        [
-            jnp.pad(vectors, ((0, named - 3 * layers), (0, 0))),
-            row(refold(qv_bias, extra)),
-            row(refold(up_bias, extra)),
-            jnp.zeros((-2 * layers % 8, width), F32),
-        ]
-    )
+    three = [refold(norm_gain, extra).astype(F32), refold(norm_shift, extra).astype(F32), biases]
+    small = [
+        wide(jnp.concatenate(three, axis=1)),
+        wide(refold(qv_bias, extra).reshape(1, -1)),
+        wide(refold(up_bias, extra)),
+    ]
+    small = jnp.concatenate(small)
+    small = jnp.pad(small, ((0, -small.shape[0] % 8), (0, 0)))
     given = run_layers(
         refold(qkv_weight, extra),
         refold(up_weight, extra),

time: 315 us -> 295 us (0.937)
  Pallas kernels: 300 us -> 278 us
    pallas_call x1, Pallas kernels: 300 us -> 278 us  [run_layers(): pl.pallas_call(layers_kernel, out_shape=(shape((rows, width), BF16), shap...]
where the time goes in v5:
time: 295 us
  Pallas kernels  278 us (94%)
  local copies, waits for them, and re-layouts  15 us (5%)
    pallas_call x1, Pallas kernels, run_layers(): pl.pallas_call(layers_kernel, out_shape=(shape((rows, width), BF16), shap...  278 us
    unnamed x49, local copies, waits for them, and re-layouts  14.4 us

profile of v5, /device:TPU:0, one launch (start us, length us, event | category | flops | bytes accessed | tf_op | source)
XLA Modules:
  0.0 294.8 jit_solution(771612444408321236)
XLA Ops:
  0.6 0.0 copy-start.13
  0.7 0.6 copy-done.13
  1.3 0.0 copy-start.14
  1.3 0.1 reshape.55
  1.4 0.6 copy-done.14
  2.0 0.0 copy-start.6
  2.0 0.1 copy.27
  2.1 0.6 copy-done.6
  2.6 0.1 add_convert_fusion
  2.7 0.0 copy-start.15
  2.7 0.6 pad.12.marks
  3.3 0.1 copy-done.15
  3.4 0.0 copy-start.16
  3.4 0.7 copy-done.16
  4.0 0.0 copy-start.11
  4.0 0.0 copy-start.12
  4.0 0.6 copy-done.11
  4.7 0.0 copy-done.12
  4.7 0.0 copy-start.17
  4.7 0.1 select_maximum_fusion.2
  4.8 0.6 copy-done.17
  5.4 0.6 select_maximum_fusion.small
  6.0 278.4 %shard_map.238 = (bf16[192,1024]{1,0:T(8,128)(2,1)}, f32[192,1024]{1,0:T(8,128)}, f32[2,32]{1,0:T(2,128)}, f32[2,32]{1,0:T(2,128)}, f32[2,32,3072]{2,1,0:T(8,128...) custom-call(bf16[2,32,3072]{2,1,0:T(8,128)(2,1)} %qkv.1, ...), custom_call_target="tpu_custom_call" | custom-call | tf_op jit(solution)/shard_map/pallas_call | solution.py:1231
  284.3 0.0 copy-start.3
  284.3 1.3 copy.40
  285.6 1.8 copy.41
  287.4 0.0 copy-done.3
  287.4 0.0 copy-start.10
  287.4 0.0 copy-start.2
  287.4 0.9 copy.42
  288.3 0.0 copy-done.10
  288.3 0.0 copy-start.9
  288.3 0.6 copy.43
  288.9 0.1 copy-done.9
  289.0 0.6 copy.44
  289.5 0.0 copy-done.2
  289.5 0.0 copy-start.8
  289.5 0.0 copy-start.4
  289.5 0.0 copy-start.1
  289.5 0.9 copy.45
  290.4 0.0 copy-done.8
  290.4 0.6 copy.46
  291.0 0.0 copy-done.4
  291.0 0.0 copy-start.5
  291.0 0.7 copy.47
  291.7 0.0 copy-done.5
  291.7 0.6 copy.48
  292.3 0.0 copy-done.1
  292.3 0.0 copy-start.7
  292.3 0.0 copy-start
  292.3 1.0 copy.49
  293.2 0.0 copy-done.7
  293.2 0.6 copy.50
  293.8 0.1 copy-done
  293.9 1.0 copy.51
  (4 shorter events, 0.0 us)
Async XLA Ops:
  0.6 0.7 copy-start.13
  1.3 0.7 copy-start.14
  2.0 0.7 copy-start.6
  2.7 0.7 copy-start.15
  3.4 0.7 copy-start.16
  4.0 0.7 copy-start.11
  4.0 0.7 copy-start.12
  4.7 0.7 copy-start.17
  284.3 3.1 %copy-start.3 = (f32[192,1024]{1,0:T(8,128)S(1)}, f32[192,1024]{1,0:T(8,128)}, u32[]{:S(2)}) copy-start(f32[192,1024]{1,0:T(8,128)} %get-tuple-element.24) | copy-start | bytes 2359300
  287.4 0.9 copy-start.10
  287.4 2.1 copy-start.2
  288.3 0.7 copy-start.9
  289.5 0.9 copy-start.8
  289.5 1.5 copy-start.4
  289.5 2.7 copy-start.1
  291.0 0.7 copy-start.5
  292.3 1.0 copy-start.7
  292.3 1.6 copy-start

commit v6 on v5

--- a/solution.py
+++ b/solution.py
@@ -644,7 +644,7 @@
                 slope[layer, j, at, to : to + 2 * PAIR] = (cdf + raised * density).astype(BF16)
             return carry
 
-        lax.fori_loop(0, 2 * micros, each, 0)
+        lax.fori_loop(0, 2 * micros, each, 0, unroll=4)
 
     def backward(layer, j):
         rounded = rnd[j].reshape(2 * rows, width)
@@ -681,7 +681,7 @@
                 sums[:, cut] += jnp.sum(delta.astype(F32).reshape(pack // 8, 8, PAIR), axis=0)
             return carry
 
-        lax.fori_loop(0, 2 * micros, each, 0)
+        lax.fori_loop(0, 2 * micros, each, 0, unroll=4)
 
     halves = (slice(0, width // 2), slice(width // 2, width))
 
@@ -1149,23 +1149,20 @@
 
     own_rows(0, total, lambda at: inputs[at].astype(F32), lambda at: up_one[at], put_last)
     grad_copies[0][0].start()
+    for i in range(len(GRAD_AXES)):
+        grad_step(0, i)
     total = out_two.total(stream_two, True)
     for m in range(4):
         at = pl.ds(m * (rows // 4), rows // 4)
         outputs[at] = total(at).astype(BF16)
-    grad_step(0, 0)
     for zl in range(2):
         grads[0].cat_step_three(zl)
     grads[0].cat_trade()
-    grad_step(0, 1)
-    grad_step(0, 2)
     grads[0].rows_two()
-    grad_step(0, 3)
     grads[0].cat_done()
     columns_by_name(0)
     for copy in returned[pieces:]:
         copy.start()
-    grad_step(0, 4)
     grads[0].rows_three()
     for copy in returned:
         copy.wait()

time: 295 us -> 287 us (0.973)
  Pallas kernels: 278 us -> 270 us
    pallas_call x1, Pallas kernels: 278 us -> 270 us  [run_layers(): pl.pallas_call(layers_kernel, out_shape=(shape((rows, width), BF16), shap...]
where the time goes in v6:
time: 287 us
  Pallas kernels  270 us (94%)
  local copies, waits for them, and re-layouts  15 us (5%)
    pallas_call x1, Pallas kernels, run_layers(): pl.pallas_call(layers_kernel, out_shape=(shape((rows, width), BF16), shap...  270 us
    unnamed x49, local copies, waits for them, and re-layouts  14.4 us

profile of v6, /device:TPU:0, one launch (start us, length us, event | category | flops | bytes accessed | tf_op | source)
XLA Modules:
  0.0 286.5 jit_solution(17551622547762367671)
XLA Ops:
  0.6 0.0 copy-start.13
  0.7 0.6 copy-done.13
  1.3 0.0 copy-start.14
  1.3 0.1 reshape.55
  1.4 0.6 copy-done.14
  2.0 0.0 copy-start.6
  2.0 0.1 copy.27
  2.1 0.6 copy-done.6
  2.6 0.1 add_convert_fusion
  2.7 0.0 copy-start.15
  2.7 0.6 pad.12.marks
  3.3 0.1 copy-done.15
  3.4 0.0 copy-start.16
  3.4 0.7 copy-done.16
  4.0 0.0 copy-start.11
  4.0 0.0 copy-start.12
  4.0 0.6 copy-done.11
  4.7 0.0 copy-done.12
  4.7 0.0 copy-start.17
  4.7 0.1 select_maximum_fusion.2
  4.8 0.6 copy-done.17
  5.4 0.6 select_maximum_fusion.small
  6.0 270.1 %shard_map.238 = (bf16[192,1024]{1,0:T(8,128)(2,1)}, f32[192,1024]{1,0:T(8,128)}, f32[2,32]{1,0:T(2,128)}, f32[2,32]{1,0:T(2,128)}, f32[2,32,3072]{2,1,0:T(8,128...) custom-call(bf16[2,32,3072]{2,1,0:T(8,128)(2,1)} %qkv.1, ...), custom_call_target="tpu_custom_call" | custom-call | tf_op jit(solution)/shard_map/pallas_call | solution.py:1228
  276.0 0.0 copy-start.3
  276.0 1.3 copy.40
  277.3 1.8 copy.41
  279.1 0.0 copy-done.3
  279.1 0.0 copy-start.10
  279.1 0.0 copy-start.2
  279.1 0.9 copy.42
  280.0 0.0 copy-done.10
  280.0 0.0 copy-start.9
  280.0 0.6 copy.43
  280.6 0.1 copy-done.9
  280.7 0.6 copy.44
  281.2 0.0 copy-done.2
  281.2 0.0 copy-start.8
  281.2 0.0 copy-start.4
  281.2 0.0 copy-start.1
  281.2 0.9 copy.45
  282.1 0.0 copy-done.8
  282.1 0.6 copy.46
  282.7 0.0 copy-done.4
  282.7 0.0 copy-start.5
  282.7 0.7 copy.47
  283.4 0.0 copy-done.5
  283.4 0.6 copy.48
  283.9 0.0 copy-done.1
  284.0 0.0 copy-start.7
  284.0 0.0 copy-start
  284.0 1.0 copy.49
  284.9 0.0 copy-done.7
  284.9 0.6 copy.50
  285.5 0.1 copy-done
  285.6 1.0 copy.51
  (4 shorter events, 0.0 us)
Async XLA Ops:
  0.6 0.7 copy-start.13
  1.3 0.7 copy-start.14
  2.0 0.7 copy-start.6
  2.7 0.7 copy-start.15
  3.4 0.7 copy-start.16
  4.0 0.7 copy-start.11
  4.0 0.7 copy-start.12
  4.7 0.7 copy-start.17
  276.0 3.1 %copy-start.3 = (f32[192,1024]{1,0:T(8,128)S(1)}, f32[192,1024]{1,0:T(8,128)}, u32[]{:S(2)}) copy-start(f32[192,1024]{1,0:T(8,128)} %get-tuple-element.24) | copy-start | bytes 2359300
  279.1 0.9 copy-start.10
  279.1 2.1 copy-start.2
  280.0 0.7 copy-start.9
  281.2 0.9 copy-start.8
  281.2 1.5 copy-start.4
  281.2 2.7 copy-start.1
  282.7 0.7 copy-start.5
  284.0 1.0 copy-start.7
  284.0 1.6 copy-start

commit v7 on v6

--- a/solution.py
+++ b/solution.py
@@ -1004,8 +1004,6 @@
     row_gathers[2].start()
     taken[1].traded()
     pump(5)
-    for piece in taken[1].cat + taken[1].down:
-        piece.start_near()
     taken[0].cat_done()
 
     def first(i, j):
@@ -1015,6 +1013,8 @@
         def _():
             pump(6)
             taken[0].rows_done()
+            for piece in taken[1].cat + taken[1].down:
+                piece.start_near()
             row_gathers[2].forward()
 
         for k in range(1, 4):

time: 287 us -> 285 us (level)
  no operation moved by 1% of the time
where the time goes in v7:
time: 285 us
  Pallas kernels  268 us (94%)
  local copies, waits for them, and re-layouts  15 us (5%)
    pallas_call x1, Pallas kernels, run_layers(): pl.pallas_call(layers_kernel, out_shape=(shape((rows, width), BF16), shap...  268 us
    unnamed x49, local copies, waits for them, and re-layouts  14.4 us

profile of v7, /device:TPU:0, one launch (start us, length us, event | category | flops | bytes accessed | tf_op | source)
XLA Modules:
  0.0 284.7 jit_solution(15581204036486440544)
XLA Ops:
  0.6 0.0 copy-start.13
  0.7 0.6 copy-done.13
  1.3 0.0 copy-start.14
  1.3 0.1 reshape.55
  1.4 0.6 copy-done.14
  2.0 0.0 copy-start.6
  2.0 0.1 copy.27
  2.1 0.6 copy-done.6
  2.6 0.1 add_convert_fusion
  2.7 0.0 copy-start.15
  2.7 0.6 pad.12.marks
  3.3 0.1 copy-done.15
  3.4 0.0 copy-start.16
  3.4 0.7 copy-done.16
  4.0 0.0 copy-start.11
  4.0 0.0 copy-start.12
  4.0 0.6 copy-done.11
  4.7 0.0 copy-done.12
  4.7 0.0 copy-start.17
  4.7 0.1 select_maximum_fusion.2
  4.8 0.6 copy-done.17
  5.4 0.6 select_maximum_fusion.small
  6.0 268.2 %shard_map.238 = (bf16[192,1024]{1,0:T(8,128)(2,1)}, f32[192,1024]{1,0:T(8,128)}, f32[2,32]{1,0:T(2,128)}, f32[2,32]{1,0:T(2,128)}, f32[2,32,3072]{2,1,0:T(8,128...) custom-call(bf16[2,32,3072]{2,1,0:T(8,128)(2,1)} %qkv.1, ...), custom_call_target="tpu_custom_call" | custom-call | tf_op jit(solution)/shard_map/pallas_call | solution.py:1228
  274.1 0.0 copy-start.3
  274.2 1.3 copy.40
  275.5 1.8 copy.41
  277.2 0.0 copy-done.3
  277.2 0.0 copy-start.10
  277.2 0.0 copy-start.2
  277.2 0.9 copy.42
  278.1 0.0 copy-done.10
  278.1 0.0 copy-start.9
  278.1 0.6 copy.43
  278.7 0.1 copy-done.9
  278.8 0.6 copy.44
  279.3 0.0 copy-done.2
  279.3 0.0 copy-start.8
  279.3 0.0 copy-start.4
  279.4 0.0 copy-start.1
  279.4 0.9 copy.45
  280.2 0.0 copy-done.8
  280.2 0.6 copy.46
  280.8 0.0 copy-done.4
  280.8 0.0 copy-start.5
  280.8 0.7 copy.47
  281.5 0.0 copy-done.5
  281.5 0.6 copy.48
  282.1 0.0 copy-done.1
  282.1 0.0 copy-start.7
  282.1 0.0 copy-start
  282.1 1.0 copy.49
  283.1 0.0 copy-done.7
  283.1 0.6 copy.50
  283.6 0.1 copy-done
  283.7 1.0 copy.51
  (4 shorter events, 0.0 us)
Async XLA Ops:
  0.6 0.7 copy-start.13
  1.3 0.7 copy-start.14
  2.0 0.7 copy-start.6
  2.7 0.7 copy-start.15
  3.4 0.7 copy-start.16
  4.0 0.7 copy-start.11
  4.0 0.7 copy-start.12
  4.7 0.7 copy-start.17
  274.1 3.1 %copy-start.3 = (f32[192,1024]{1,0:T(8,128)S(1)}, f32[192,1024]{1,0:T(8,128)}, u32[]{:S(2)}) copy-start(f32[192,1024]{1,0:T(8,128)} %get-tuple-element.24) | copy-start | bytes 2359300
  277.2 0.9 copy-start.10
  277.2 2.1 copy-start.2
  278.1 0.7 copy-start.9
  279.3 0.9 copy-start.8
  279.3 1.5 copy-start.4
  279.4 2.7 copy-start.1
  280.8 0.7 copy-start.5
  282.1 1.0 copy-start.7
  282.1 1.6 copy-start
